TPU v7x, 32 devices: a whole 2x2x4 slice. The times are simulated.
32 devices in a mesh: fsdp: 2 (over x), context: 4 (over y, core), tensor: 4 (over z).
Axes of the slice: x: 2, y: 2, z: 4, core: 2. Of those that a mesh axis runs over, the one named last changes fastest.
Arguments:
- hidden_in: bfloat16 [4096, 2048], P(('fsdp', 'context')), may hold values from -6 to 6
- segments: int32 [2, 2048], P('fsdp'), may hold values from 0 to 4, as said below
- cotangent: bfloat16 [4096, 2048], P(('fsdp', 'context')), may hold values from -6 to 6
- attn_gain: bfloat16 [2048], P(('fsdp', 'context')), may hold values from 0.25 to 1.75
- query_weight: bfloat16 [2048, 2048], P(('fsdp', 'context'), 'tensor'), may hold values from -0.125 to 0.125
- key_weight: bfloat16 [2048, 1024], P(('fsdp', 'context'), 'tensor'), may hold values from -0.125 to 0.125
- value_weight: bfloat16 [2048, 1024], P(('fsdp', 'context'), 'tensor'), may hold values from -0.125 to 0.125
- output_weight: bfloat16 [2048, 2048], P(('fsdp', 'context'), 'tensor'), may hold values from -3 to 3
- qnorm_gain: bfloat16 [128], replicated, may hold values from 0.25 to 1.75
- knorm_gain: bfloat16 [128], replicated, may hold values from 0.25 to 1.75
- ffn_gain: bfloat16 [2048], P(('fsdp', 'context')), may hold values from 0.25 to 1.75
- gate_weight: bfloat16 [2048, 6144], P(('fsdp', 'context'), 'tensor'), may hold values from -0.125 to 0.125
- up_weight: bfloat16 [2048, 6144], P(('fsdp', 'context'), 'tensor'), may hold values from -0.125 to 0.125
- down_weight: bfloat16 [2048, 6144], P(('fsdp', 'context'), 'tensor'), may hold values from -0.109375 to 0.109375
Outputs:
- output: bfloat16 [4096, 2048], P(('fsdp', 'context'))
- input_grad: float32 [4096, 2048], P(('fsdp', 'context'))
- attn_gain_grad: float32 [2048], P(('fsdp', 'context'))
- query_grad: float32 [2048, 2048], P(('fsdp', 'context'), 'tensor')
- key_grad: float32 [2048, 1024], P(('fsdp', 'context'), 'tensor')
- value_grad: float32 [2048, 1024], P(('fsdp', 'context'), 'tensor')
- output_grad: float32 [2048, 2048], P(('fsdp', 'context'), 'tensor')
- qnorm_grad: float32 [128], replicated
- knorm_grad: float32 [128], replicated
- ffn_gain_grad: float32 [2048], P(('fsdp', 'context'))
- gate_grad: float32 [2048, 6144], P(('fsdp', 'context'), 'tensor')
- up_grad: float32 [2048, 6144], P(('fsdp', 'context'), 'tensor')
- down_grad: float32 [2048, 6144], P(('fsdp', 'context'), 'tensor')
Inputs may be any that keep to these rules, and one draw needn't show every extreme that they name: `segments`: document numbers never fall along the positions of a sequence; in every sequence one document covers positions 255 to 1792; the first position has number 0 and the last number 4; some numbers may be skipped.
All inputs are finite; a program needn't handle non-finite values.
Results may differ from a plain program's by a relative error of at most 0.014.
Values may be sent and summed in bfloat16 or wider, within the bound.
No kernel may reach another device: no remote copies, remote signals or barrier semaphores. Data moves between devices by JAX's collectives and lax.ppermute only.
A program may use at most 256 MiB of HBM per device.

v0:
```python
import jax
import jax.numpy as jnp
from jax import lax
from jax.sharding import PartitionSpec as P

EPS = 1e-06
THETA = 1000000.0


def dot_plain(matrix_a, matrix_b):
    return jnp.dot(matrix_a, matrix_b, preferred_element_type=jnp.float32)


def dot_right_t(matrix_a, matrix_b):
    return lax.dot_general(
        matrix_a, matrix_b, (((1,), (1,)), ((), ())), preferred_element_type=jnp.float32
    )


def dot_left_t(matrix_a, matrix_b):
    return lax.dot_general(
        matrix_a, matrix_b, (((0,), (0,)), ((), ())), preferred_element_type=jnp.float32
    )


def rounded(values):
    return lax.optimization_barrier(values.astype(jnp.bfloat16)).astype(jnp.float32)


def rms_scale(values):
    return lax.rsqrt(jnp.mean(values * values, axis=-1, keepdims=True) + EPS)


def stored_positions(length, pieces):
    half_rows = length // (2 * pieces)
    rows = jnp.arange(length, dtype=jnp.int32)
    block = rows // half_rows
    owner = block // 2
    place = jnp.where(block % 2 == 0, owner, 2 * pieces - 1 - owner)
    return place * half_rows + rows % half_rows


def rope_tables(values, positions):
    half_dim = values.shape[-1] // 2
    inverse = THETA ** (-(jnp.arange(half_dim).astype(jnp.float32) * 2.0 / values.shape[-1]))
    angles = positions.astype(jnp.float32)[:, None] * inverse[None, :]
    return (half_dim, jnp.cos(angles)[:, None, :], jnp.sin(angles)[:, None, :])


def rotary(values, positions):
    half_dim, cosine, sine_table = rope_tables(values, positions)
    first_half = values[..., :half_dim]
    second_half = values[..., half_dim:]
    return jnp.concatenate(
        [
            first_half * cosine - second_half * sine_table,
            second_half * cosine + first_half * sine_table,
        ],
        axis=-1,
    )


def unrotary(grads_in, positions):
    half_dim, cosine, sine_table = rope_tables(grads_in, positions)
    first_half = grads_in[..., :half_dim]
    second_half = grads_in[..., half_dim:]
    return jnp.concatenate(
        [
            first_half * cosine + second_half * sine_table,
            second_half * cosine - first_half * sine_table,
        ],
        axis=-1,
    )


def norm_back(grad_unit, unit_values, scale_values):
    return scale_values * (
        grad_unit - unit_values * jnp.mean(grad_unit * unit_values, axis=-1, keepdims=True)
    )


def shards(
    hidden_in,
    segments,
    cotangent,
    attn_gain,
    query_weight,
    key_weight,
    value_weight,
    output_weight,
    qnorm_gain,
    knorm_gain,
    ffn_gain,
    gate_weight,
    up_weight,
    down_weight,
):
    (
        gain_one,
        query_full,
        key_full,
        value_full,
        out_full,
        gain_two,
        gate_full,
        up_full,
        down_full,
    ) = (
        lax.all_gather(attn_gain, ("fsdp", "context"), axis=0, tiled=True),
        lax.all_gather(query_weight, ("fsdp", "context"), axis=0, tiled=True),
        lax.all_gather(key_weight, ("fsdp", "context"), axis=0, tiled=True),
        lax.all_gather(value_weight, ("fsdp", "context"), axis=0, tiled=True),
        lax.all_gather(output_weight, ("fsdp", "context"), axis=0, tiled=True),
        lax.all_gather(ffn_gain, ("fsdp", "context"), axis=0, tiled=True),
        lax.all_gather(gate_weight, ("fsdp", "context"), axis=0, tiled=True),
        lax.all_gather(up_weight, ("fsdp", "context"), axis=0, tiled=True),
        lax.all_gather(down_weight, ("fsdp", "context"), axis=0, tiled=True),
    )
    head_dim = qnorm_gain.shape[0]
    local_rows = hidden_in.shape[0]
    pieces = lax.axis_size("context")
    total_rows = local_rows * pieces
    query_heads = query_weight.shape[1] // head_dim
    value_heads = key_weight.shape[1] // head_dim
    group_size = query_heads // value_heads
    offset = lax.axis_index("context") * local_rows
    key_positions = stored_positions(total_rows, pieces)
    positions = lax.dynamic_slice_in_dim(key_positions, offset, local_rows)
    seg_keys = jnp.take(segments[0], key_positions)
    seg_local = lax.dynamic_slice_in_dim(seg_keys, offset, local_rows)
    qgain = qnorm_gain.astype(jnp.float32)
    kgain = knorm_gain.astype(jnp.float32)
    hidden = hidden_in.astype(jnp.float32)
    scale_one = rms_scale(hidden)
    normed_one = hidden * scale_one
    inputs_one = (normed_one * gain_one.astype(jnp.float32)).astype(jnp.bfloat16)
    query_proj = dot_plain(inputs_one, query_full).reshape(local_rows, query_heads, head_dim)
    key_proj = dot_plain(inputs_one, key_full).reshape(local_rows, value_heads, head_dim)
    value_low = dot_plain(inputs_one, value_full).astype(jnp.bfloat16)
    query_scale = rms_scale(query_proj)
    query_unit = query_proj * query_scale
    key_scale = rms_scale(key_proj)
    key_unit = key_proj * key_scale
    queries = rotary(query_unit * qgain, positions).astype(jnp.bfloat16)
    keys_low = rotary(key_unit * kgain, positions).astype(jnp.bfloat16)
    key_all, value_all = (
        lax.all_gather(
            keys_low.reshape(local_rows, value_heads * head_dim), "context", axis=0, tiled=True
        ),
        lax.all_gather(value_low, "context", axis=0, tiled=True),
    )
    key_all = key_all.reshape(total_rows, value_heads, head_dim)
    value_all = value_all.reshape(total_rows, value_heads, head_dim)
    block_rows = min(512, local_rows)
    block_count = local_rows // block_rows
    factor = head_dim ** (-0.5)
    query_blocks = queries.reshape(block_count, block_rows, value_heads, group_size, head_dim)
    pos_blocks = positions.reshape(block_count, block_rows)
    seg_blocks = seg_local.reshape(block_count, block_rows)

    def masked_scores(query_block, pos_block, seg_block):
        scores = (
            jnp.einsum("bkgd,skd->bkgs", query_block, key_all, preferred_element_type=jnp.float32)
            * factor
        )
        allowed = (key_positions[None, :] <= pos_block[:, None]) & (
            seg_keys[None, :] == seg_block[:, None]
        )
        return jnp.where(allowed[:, None, None, :], scores, -1e30)

    def attend(operands):
        query_block, pos_block, seg_block = operands
        scores = masked_scores(query_block, pos_block, seg_block)
        row_top = jnp.max(scores, axis=-1, keepdims=True)
        exponent = jnp.exp(scores - row_top)
        totals = jnp.sum(exponent, axis=-1, keepdims=True)
        probability = (exponent / totals).astype(jnp.bfloat16)
        attended = jnp.einsum(
            "bkgs,skd->bkgd", probability, value_all, preferred_element_type=jnp.float32
        )
        return (attended, row_top + jnp.log(totals))

    attended, log_total = lax.map(attend, (query_blocks, pos_blocks, seg_blocks))
    attended_low = attended.reshape(local_rows, query_heads * head_dim).astype(jnp.bfloat16)
    attn_out = lax.psum(dot_right_t(attended_low, out_full), "tensor")
    middle = hidden + attn_out
    scale_two = rms_scale(middle)
    normed_two = middle * scale_two
    inputs_two = (normed_two * gain_two.astype(jnp.float32)).astype(jnp.bfloat16)
    gate_in = dot_plain(inputs_two, gate_full)
    up_in = dot_plain(inputs_two, up_full)
    gate_sigmoid = jax.nn.sigmoid(gate_in)
    active = gate_in * gate_sigmoid
    product = (active * up_in).astype(jnp.bfloat16)
    ffn_out = lax.psum(dot_right_t(product, down_full).astype(jnp.bfloat16), "tensor").astype(
        jnp.float32
    )
    output = (middle + ffn_out).astype(jnp.bfloat16)
    (
        gain_one,
        query_full,
        key_full,
        value_full,
        out_full,
        gain_two,
        gate_full,
        up_full,
        down_full,
    ) = (
        lax.all_gather(attn_gain, ("fsdp", "context"), axis=0, tiled=True),
        lax.all_gather(query_weight, ("fsdp", "context"), axis=0, tiled=True),
        lax.all_gather(key_weight, ("fsdp", "context"), axis=0, tiled=True),
        lax.all_gather(value_weight, ("fsdp", "context"), axis=0, tiled=True),
        lax.all_gather(output_weight, ("fsdp", "context"), axis=0, tiled=True),
        lax.all_gather(ffn_gain, ("fsdp", "context"), axis=0, tiled=True),
        lax.all_gather(gate_weight, ("fsdp", "context"), axis=0, tiled=True),
        lax.all_gather(up_weight, ("fsdp", "context"), axis=0, tiled=True),
        lax.all_gather(down_weight, ("fsdp", "context"), axis=0, tiled=True),
    )
    grad_down = dot_left_t(cotangent, product)
    dproduct = dot_plain(cotangent, down_full)
    dgate = (dproduct * up_in * gate_sigmoid * (1.0 + gate_in * (1.0 - gate_sigmoid))).astype(
        jnp.bfloat16
    )
    dup_low = (dproduct * active).astype(jnp.bfloat16)
    grad_gate = dot_left_t(inputs_two, dgate)
    grad_up = dot_left_t(inputs_two, dup_low)
    dnormed_two = lax.psum(dot_right_t(dgate, gate_full) + dot_right_t(dup_low, up_full), "tensor")
    gain_two_grad = jnp.sum(dnormed_two * normed_two, axis=0)
    dmiddle = cotangent.astype(jnp.float32) + norm_back(
        dnormed_two * gain_two.astype(jnp.float32), normed_two, scale_two
    )
    dattn = dmiddle.astype(jnp.bfloat16)
    grad_output = dot_left_t(dattn, attended_low)
    dattended = dot_plain(dattn, out_full).astype(jnp.bfloat16)
    grad_blocks = dattended.reshape(block_count, block_rows, value_heads, group_size, head_dim)

    def back_block(accumulated, operands):
        key_accum, value_accum = accumulated
        query_block, pos_block, seg_block, lse_block, grad_block = operands
        scores = masked_scores(query_block, pos_block, seg_block)
        probability = jnp.exp(scores - lse_block)
        dprobs = jnp.einsum(
            "bkgd,skd->bkgs", grad_block, value_all, preferred_element_type=jnp.float32
        )
        row_delta = jnp.sum(probability * dprobs, axis=-1, keepdims=True)
        dscores = (probability * (dprobs - row_delta)).astype(jnp.bfloat16)
        dquery = (
            jnp.einsum("bkgs,skd->bkgd", dscores, key_all, preferred_element_type=jnp.float32)
            * factor
        )
        key_accum = (
            key_accum
            + jnp.einsum("bkgs,bkgd->skd", dscores, query_block, preferred_element_type=jnp.float32)
            * factor
        )
        value_accum = value_accum + jnp.einsum(
            "bkgs,bkgd->skd",
            probability.astype(jnp.bfloat16),
            grad_block,
            preferred_element_type=jnp.float32,
        )
        return ((key_accum, value_accum), dquery)

    empty_keys = jnp.zeros((total_rows, value_heads, head_dim), jnp.float32)
    (key_accum, value_accum), dquery = lax.scan(
        back_block,
        (empty_keys, empty_keys),
        (query_blocks, pos_blocks, seg_blocks, log_total, grad_blocks),
    )
    key_grad_own, value_grad_own = (
        lax.psum_scatter(
            key_accum.reshape(total_rows, value_heads * head_dim),
            "context",
            scatter_dimension=0,
            tiled=True,
        ),
        lax.psum_scatter(
            value_accum.reshape(total_rows, value_heads * head_dim),
            "context",
            scatter_dimension=0,
            tiled=True,
        ),
    )
    dqueries = rounded(dquery.reshape(local_rows, query_heads, head_dim))
    dkeys = rounded(key_grad_own.reshape(local_rows, value_heads, head_dim))
    dvalues = value_grad_own.astype(jnp.bfloat16)
    dquery_rot = unrotary(dqueries, positions)
    dkey_rot = unrotary(dkeys, positions)
    qnorm_local = jnp.sum(dquery_rot * query_unit, axis=(0, 1))
    knorm_local = jnp.sum(dkey_rot * key_unit, axis=(0, 1))
    dquery_proj = (
        norm_back(dquery_rot * qgain, query_unit, query_scale)
        .reshape(local_rows, query_heads * head_dim)
        .astype(jnp.bfloat16)
    )
    dkey_proj = (
        norm_back(dkey_rot * kgain, key_unit, key_scale)
        .reshape(local_rows, value_heads * head_dim)
        .astype(jnp.bfloat16)
    )
    grad_query = dot_left_t(inputs_one, dquery_proj)
    grad_key = dot_left_t(inputs_one, dkey_proj)
    grad_value = dot_left_t(inputs_one, dvalues)
    dnormed_one = lax.psum(
        dot_right_t(dquery_proj, query_full)
        + dot_right_t(dkey_proj, key_full)
        + dot_right_t(dvalues, value_full),
        "tensor",
    )
    gain_one_grad = jnp.sum(dnormed_one * normed_one, axis=0)
    dhidden = dmiddle + norm_back(dnormed_one * gain_one.astype(jnp.float32), normed_one, scale_one)
    summed = (
        lax.psum_scatter(gain_one_grad, ("fsdp", "context"), scatter_dimension=0, tiled=True),
        lax.psum_scatter(grad_query, ("fsdp", "context"), scatter_dimension=0, tiled=True),
        lax.psum_scatter(grad_key, ("fsdp", "context"), scatter_dimension=0, tiled=True),
        lax.psum_scatter(grad_value, ("fsdp", "context"), scatter_dimension=0, tiled=True),
        lax.psum_scatter(grad_output, ("fsdp", "context"), scatter_dimension=0, tiled=True),
        lax.psum_scatter(gain_two_grad, ("fsdp", "context"), scatter_dimension=0, tiled=True),
        lax.psum_scatter(grad_gate, ("fsdp", "context"), scatter_dimension=0, tiled=True),
        lax.psum_scatter(grad_up, ("fsdp", "context"), scatter_dimension=0, tiled=True),
        lax.psum_scatter(grad_down, ("fsdp", "context"), scatter_dimension=0, tiled=True),
    )
    qnorm_total, knorm_total = lax.psum((qnorm_local, knorm_local), ("fsdp", "context", "tensor"))
    return (
        output,
        dhidden,
        summed[0],
        summed[1],
        summed[2],
        summed[3],
        summed[4],
        qnorm_total,
        knorm_total,
        summed[5],
        summed[6],
        summed[7],
        summed[8],
    )


def solution(mesh):
    in_specs = (
        P(("fsdp", "context"), None),
        P("fsdp", None),
        P(("fsdp", "context"), None),
        P(("fsdp", "context")),
        P(("fsdp", "context"), "tensor"),
        P(("fsdp", "context"), "tensor"),
        P(("fsdp", "context"), "tensor"),
        P(("fsdp", "context"), "tensor"),
        P(),
        P(),
        P(("fsdp", "context")),
        P(("fsdp", "context"), "tensor"),
        P(("fsdp", "context"), "tensor"),
        P(("fsdp", "context"), "tensor"),
    )
    out_specs = (
        P(("fsdp", "context"), None),
        P(("fsdp", "context"), None),
        P(("fsdp", "context")),
        P(("fsdp", "context"), "tensor"),
        P(("fsdp", "context"), "tensor"),
        P(("fsdp", "context"), "tensor"),
        P(("fsdp", "context"), "tensor"),
        P(),
        P(),
        P(("fsdp", "context")),
        P(("fsdp", "context"), "tensor"),
        P(("fsdp", "context"), "tensor"),
        P(("fsdp", "context"), "tensor"),
    )
    return jax.shard_map(shards, mesh=mesh, in_specs=in_specs, out_specs=out_specs, check_vma=False)
```

profile of v0, /device:TPU:0, one launch (start us, length us, event | category | flops | bytes accessed | tf_op | source)
XLA Modules:
  0.0 1495.9 jit_solution(6455886784930189797)
XLA Ops:
  22.0 14.1 all-gather.12.cloned.1.call-done
  40.8 20.7 %all-gather.16.cloned.1.call-done = bf16[2048,256]{1,0:T(8,128)(2,1)} async-done(((bf16[256,256]{1,0:T(8,128)(2,1)}), bf16[2048,256]{1,0:T(8,128)(2,1)}) %all-gather.16.cloned.1.call-update) | async-done | bytes 1048592 | tf_op jit(solution)/shard_map/all_gather | solution.py:111
  65.6 11.8 gather_fusion
  82.6 27.5 %all-gather.20.cloned.1.call-done = bf16[2048,512]{1,0:T(8,128)(2,1)} async-done(((bf16[256,512]{1,0:T(8,128)(2,1)}), bf16[2048,512]{1,0:T(8,128)(2,1)}) %all-gather.20.cloned.1.call-update) | async-done | bytes 2097168 | tf_op jit(solution)/shard_map/all_gather | solution.py:110
  117.4 11.4 all-gather.18.cloned.1.call-done
  174.5 144.1 %all-reduce.9.cloned.1.call-done = f32[512,2048]{1,0:T(8,128)} async-done(((f32[512,2048]{1,0:T(8,128)}), f32[512,2048]{1,0:T(8,128)}) %all-reduce.9.cloned.1.call-update) | async-done | bytes 4194320 | tf_op jit(solution)/shard_map/psum | solution.py:185
  325.1 40.1 %all-gather.24.cloned.1.call-done = bf16[2048,1536]{1,0:T(8,128)(2,1)} async-done(((bf16[256,1536]{1,0:T(8,128)(2,1)}), bf16[2048,1536]{1,0:T(8,128)(2,1)}) %all-gather.24.cloned.1.call-update) | async-done | bytes 6291472 | tf_op jit(solution)/shard_map/all_gather | solution.py:115
  373.7 39.1 %all-gather.26.cloned.1.call-done = bf16[2048,1536]{1,0:T(8,128)(2,1)} async-done(((bf16[256,1536]{1,0:T(8,128)(2,1)}), bf16[2048,1536]{1,0:T(8,128)(2,1)}) %all-gather.26.cloned.1.call-update) | async-done | bytes 6291472 | tf_op jit(solution)/shard_map/all_gather | solution.py:116
  421.3 39.0 %all-gather.28.cloned.1.call-done = bf16[2048,1536]{1,0:T(8,128)(2,1)} async-done(((bf16[256,1536]{1,0:T(8,128)(2,1)}), bf16[2048,1536]{1,0:T(8,128)(2,1)}) %all-gather.28.cloned.1.call-update) | async-done | bytes 6291472 | tf_op jit(solution)/shard_map/all_gather | solution.py:117
  491.2 147.0 %all-reduce.13.cloned.1.call-done = f32[512,2048]{1,0:T(8,128)} async-done(((f32[512,2048]{1,0:T(8,128)}), f32[512,2048]{1,0:T(8,128)}) %all-reduce.13.cloned.1.call-update) | async-done | bytes 4194320 | tf_op jit(solution)/shard_map/psum | solution.py:228
  643.2 83.3 %all-reduce.11.cloned.1.call-done = bf16[512,2048]{1,0:T(8,128)(2,1)} async-done(((bf16[512,2048]{1,0:T(8,128)(2,1)}), bf16[512,2048]{1,0:T(8,128)(2,1)}) %all-reduce.11.cloned.1.call-update) | async-done | bytes 2097168 | tf_op jit(solution)/shard_map/psum | solution.py:195
  737.5 16.4 %fusion = (f32[512,2,2]{0,2,1:T(2,128)}, f32[2,2048,512,2]{2,1,3,0:T(8,128)}) fusion(f32[512,2,2,2048]{0,3,2,1:T(8,128)} %get-tuple-element.174, f32[512,2,2]{0,2,1:T(2,128)S(1)} %log_add_fusion, bf16[512,2,2,128]{0,3,2,1:T(8,128)(2,1)} %bitcast.160, bf16[2048,2,128,1]{2,1,0,3:T(2,128)(2,1)} %bitcast.156), kind=kOutput, calls=%fused_computation.3 | convolution fusion | flops 1086322688 | bytes 35143680 | tf_op jit(solution)/shard_map/while/body/eval_jaxpr/bkgd,skd->bkgs/dot_general | solution.py:243
  789.8 12.7 reduce-scatter.10.cloned.1.call-done
  806.9 29.3 %reduce-scatter.12.cloned.1.call-done = f32[512,256]{0,1:T(8,128)} async-done(((f32[2048,256]{0,1:T(8,128)}), f32[512,256]{0,1:T(8,128)}) %reduce-scatter.12.cloned.1.call-update) | async-done | bytes 524304 | tf_op jit(solution)/shard_map/reduce_scatter | solution.py:278
  892.3 43.2 %all-reduce.2 = (f32[128]{0:T(128)}, f32[128]{0:T(128)}) all-reduce(f32[128]{0:T(128)S(1)} %bitcast_reduce_fusion, f32[128]{0:T(128)S(1)} %bitcast_reduce_fusion.1), channel_id=1, replica_groups=mesh['fsdp'=2,'context'=4,'tensor'=4] {'fsdp','context','tensor'}, use_global_device_ids=true, to_apply=%region_25.26 | all-reduce | flops 256 | bytes 2048 | tf_op jit(solution)/shard_map/psum | solution.py:324
  935.6 64.2 %all-reduce.15.cloned.1.call-done = f32[512,2048]{1,0:T(8,128)} async-done(((f32[512,2048]{1,0:T(8,128)}), f32[512,2048]{1,0:T(8,128)}) %all-reduce.15.cloned.1.call-update) | async-done | bytes 4194320 | tf_op jit(solution)/shard_map/psum | solution.py:305
  1003.1 24.0 %all-reduce.3 = (f32[2048]{0:T(1024)S(1)}, f32[2048]{0:T(1024)S(1)}) all-reduce(f32[2048]{0:T(1024)S(1)} %get-tuple-element.136, f32[2048]{0:T(1024)S(1)} %copy-done.26), channel_id=4, replica_groups=mesh['fsdp'=2,'context'=4,'tensor'=4] {'fsdp','context'}, use_global_device_ids=true, to_apply=%region_18.19.clone | all-reduce | flops 4096 | bytes 32768
  1035.8 58.7 %reduce-scatter.26.cloned.1.call-done = f32[256,1536]{0,1:T(8,128)} async-done(((f32[2048,1536]{0,1:T(8,128)}), f32[256,1536]{0,1:T(8,128)}) %reduce-scatter.26.cloned.1.call-update) | async-done | bytes 1572880 | tf_op jit(solution)/shard_map/reduce_scatter | solution.py:322
  1097.6 52.1 %reduce-scatter.14.cloned.1.call-done = f32[256,512]{1,0:T(8,128)} async-done(((f32[2048,512]{1,0:T(8,128)}), f32[256,512]{1,0:T(8,128)}) %reduce-scatter.14.cloned.1.call-update) | async-done | bytes 524304 | tf_op jit(solution)/shard_map/reduce_scatter | solution.py:315
  1149.7 55.5 %reduce-scatter.20.cloned.1.call-done = f32[256,512]{1,0:T(8,128)} async-done(((f32[2048,512]{1,0:T(8,128)}), f32[256,512]{1,0:T(8,128)}) %reduce-scatter.20.cloned.1.call-update) | async-done | bytes 524304 | tf_op jit(solution)/shard_map/reduce_scatter | solution.py:318
  1205.2 45.1 %reduce-scatter.16.cloned.1.call-done = f32[256,256]{1,0:T(8,128)} async-done(((f32[2048,256]{1,0:T(8,128)}), f32[256,256]{1,0:T(8,128)}) %reduce-scatter.16.cloned.1.call-update) | async-done | bytes 262160 | tf_op jit(solution)/shard_map/reduce_scatter | solution.py:316
  1250.3 45.3 %reduce-scatter.18.cloned.1.call-done = f32[256,256]{1,0:T(8,128)} async-done(((f32[2048,256]{1,0:T(8,128)}), f32[256,256]{1,0:T(8,128)}) %reduce-scatter.18.cloned.1.call-update) | async-done | bytes 262160 | tf_op jit(solution)/shard_map/reduce_scatter | solution.py:317
  1295.6 96.5 %reduce-scatter.22.cloned.1.call-done = f32[256,1536]{1,0:T(8,128)} async-done(((f32[2048,1536]{1,0:T(8,128)}), f32[256,1536]{1,0:T(8,128)}) %reduce-scatter.22.cloned.1.call-update) | async-done | bytes 1572880 | tf_op jit(solution)/shard_map/reduce_scatter | solution.py:320
  1392.2 96.5 %reduce-scatter.24.cloned.1.call-done = f32[256,1536]{1,0:T(8,128)} async-done(((f32[2048,1536]{1,0:T(8,128)}), f32[256,1536]{1,0:T(8,128)}) %reduce-scatter.24.cloned.1.call-update) | async-done | bytes 1572880 | tf_op jit(solution)/shard_map/reduce_scatter | solution.py:321
  (216 shorter events, 262.1 us)
Async XLA Ops:
  7.2 28.9 %all-gather.12.cloned.1.call-start = ((), (), s32[]{:S(2)}) async-start(), calls=%async_computation.9 | async-start | bytes 1179648 | tf_op jit(solution)/shard_map/all_gather | solution.py:112
  7.9 53.6 %all-gather.16.cloned.1.call-start = ((), (), s32[]{:S(2)}) async-start(), calls=%async_computation.11 | async-start | bytes 1179648 | tf_op jit(solution)/shard_map/all_gather | solution.py:111
  8.7 71.8 %all-gather.14.cloned.1.call-start = ((), (), s32[]{:S(2)}) async-start(), calls=%async_computation.10 | async-start | bytes 1310720 | tf_op jit(solution)/shard_map/all_gather | solution.py:150
  39.5 70.6 %all-gather.20.cloned.1.call-start = ((), (), s32[]{:S(2)}) async-start(), calls=%async_computation.13 | async-start | bytes 2359296 | tf_op jit(solution)/shard_map/all_gather | solution.py:110
  40.1 88.8 %all-gather.18.cloned.1.call-start = ((), (), s32[]{:S(2)}) async-start(), calls=%async_computation.12 | async-start | bytes 1310720 | tf_op jit(solution)/shard_map/all_gather | solution.py:147
  64.7 93.8 %all-gather.22.cloned.1.call-start = ((), (), s32[]{:S(2)}) async-start(), calls=%async_computation.14 | async-start | bytes 2359296 | tf_op jit(solution)/shard_map/all_gather | solution.py:113
  65.3 253.3 %all-reduce.9.cloned.1.call-start = ((), (), s32[]{:S(2)}) async-start(), calls=%async_computation.15 | async-start | bytes 8388608 | tf_op jit(solution)/shard_map/psum | solution.py:185
  163.5 201.7 %all-gather.24.cloned.1.call-start = ((), (), s32[]{:S(2)}) async-start(), calls=%async_computation.16 | async-start | bytes 7077888 | tf_op jit(solution)/shard_map/all_gather | solution.py:115
  164.2 248.6 %all-gather.26.cloned.1.call-start = ((), (), s32[]{:S(2)}) async-start(), calls=%async_computation.17 | async-start | bytes 7077888 | tf_op jit(solution)/shard_map/all_gather | solution.py:116
  165.0 295.3 %all-gather.28.cloned.1.call-start = ((), (), s32[]{:S(2)}) async-start(), calls=%async_computation.18 | async-start | bytes 7077888 | tf_op jit(solution)/shard_map/all_gather | solution.py:117
  165.6 472.6 %all-reduce.13.cloned.1.call-start = ((), (), s32[]{:S(2)}) async-start(), calls=%async_computation.20 | async-start | bytes 8388608 | tf_op jit(solution)/shard_map/psum | solution.py:228
  483.0 243.5 %all-reduce.11.cloned.1.call-start = ((), (), s32[]{:S(2)}) async-start(), calls=%async_computation.19 | async-start | bytes 4194304 | tf_op jit(solution)/shard_map/psum | solution.py:195
  491.1 311.4 %reduce-scatter.10.cloned.1.call-start = ((), (), s32[]{:S(2)}) async-start(), calls=%async_computation.21 | async-start | bytes 2621440 | tf_op jit(solution)/shard_map/reduce_scatter | solution.py:272
  771.9 64.4 %reduce-scatter.12.cloned.1.call-start = ((), (), s32[]{:S(2)}) async-start(), calls=%async_computation.22 | async-start | bytes 2621440 | tf_op jit(solution)/shard_map/reduce_scatter | solution.py:278
  782.4 217.3 %all-reduce.15.cloned.1.call-start = ((), (), s32[]{:S(2)}) async-start(), calls=%async_computation.23 | async-start | bytes 8388608 | tf_op jit(solution)/shard_map/psum | solution.py:305
  843.9 250.6 %reduce-scatter.26.cloned.1.call-start = ((), (), s32[]{:S(2)}) async-start(), calls=%async_computation.30 | async-start | bytes 14155776 | tf_op jit(solution)/shard_map/reduce_scatter | solution.py:322
  854.1 295.6 %reduce-scatter.14.cloned.1.call-start = ((), (), s32[]{:S(2)}) async-start(), calls=%async_computation.24 | async-start | bytes 4718592 | tf_op jit(solution)/shard_map/reduce_scatter | solution.py:315
  858.2 346.9 %reduce-scatter.20.cloned.1.call-start = ((), (), s32[]{:S(2)}) async-start(), calls=%async_computation.27 | async-start | bytes 4718592 | tf_op jit(solution)/shard_map/reduce_scatter | solution.py:318
  864.9 385.4 %reduce-scatter.16.cloned.1.call-start = ((), (), s32[]{:S(2)}) async-start(), calls=%async_computation.25 | async-start | bytes 2359296 | tf_op jit(solution)/shard_map/reduce_scatter | solution.py:316
  867.6 428.0 %reduce-scatter.18.cloned.1.call-start = ((), (), s32[]{:S(2)}) async-start(), calls=%async_computation.26 | async-start | bytes 2359296 | tf_op jit(solution)/shard_map/reduce_scatter | solution.py:317
  870.0 522.1 %reduce-scatter.22.cloned.1.call-start = ((), (), s32[]{:S(2)}) async-start(), calls=%async_computation.28 | async-start | bytes 14155776 | tf_op jit(solution)/shard_map/reduce_scatter | solution.py:320
  880.2 608.4 %reduce-scatter.24.cloned.1.call-start = ((), (), s32[]{:S(2)}) async-start(), calls=%async_computation.29 | async-start | bytes 14155776 | tf_op jit(solution)/shard_map/reduce_scatter | solution.py:321
  890.4 112.6 %copy-start.26 = (f32[2048]{0:T(1024)S(1)}, f32[2048]{0:T(1024)}, u32[]{:S(2)}) copy-start(f32[2048]{0:T(1024)} %get-tuple-element.134) | copy-start | bytes 24580
  1028.3 460.3 %copy-start.1 = (s32[1,2048]{1,0:T(1,128)S(1)}, s32[1,2048]{1,0:T(1,128)}, u32[]{:S(2)}) copy-start(s32[1,2048]{1,0:T(1,128)} %param.15) | copy-start | bytes 24580
  (39 other events, 715.0 us)
Sparse Core Ops, SparseCore 0:
  9.9 26.1 all-gather.11
  38.0 23.4 all-gather.15
  63.7 16.7 all-gather.13
  82.2 27.8 all-gather.19
  112.1 16.7 all-gather.17
  130.6 27.8 all-gather.21
  163.6 154.9 all-reduce.8
  320.6 44.5 all-gather.23
  367.3 45.5 all-gather.25
  414.7 45.5 all-gather.27
  483.1 154.9 all-reduce.12
  640.9 85.5 all-reduce.10
  772.0 30.4 reduce-scatter.9
  804.9 31.3 reduce-scatter.11
  844.1 155.6 all-reduce.14
  1003.1 91.4 reduce-scatter.25
  1098.3 51.3 reduce-scatter.13
  1153.8 51.2 reduce-scatter.19
  1209.0 41.2 reduce-scatter.15
  1254.4 41.2 reduce-scatter.17
  1299.7 92.3 reduce-scatter.21
  1396.2 92.3 reduce-scatter.23
where the time goes:
time: 1500 us
  waiting for transfers between devices  1130 us (75%)
  matrix products  176 us (12%)
  blocking collectives  86.4 us (6%)
  other arithmetic  56.2 us (4%)
  local copies, waits for them, and re-layouts  30.4 us (2%)
  between operations  16.1 us (1%)
    psum x1, waiting for transfers between devices, shards(): lax.psum(dot_right_t(dgate, gate_full) + dot_right_t(dup_low, up_full), '...  147 us
    psum x1, waiting for transfers between devices, shards(): attn_out = lax.psum(dot_right_t(attended_low, out_full), 'tensor')  144 us
    reduce_scatter x1, waiting for transfers between devices, shards(): lax.psum_scatter(grad_gate, ('fsdp', 'context'), scatter_dimension=0, til...  96.5 us
    reduce_scatter x1, waiting for transfers between devices, shards(): lax.psum_scatter(grad_up, ('fsdp', 'context'), scatter_dimension=0, tiled...  96.5 us
    psum x1, waiting for transfers between devices, shards(): lax.psum(dot_right_t(product, down_full).astype(jnp.bfloat16), 'tensor')  83.3 us
    psum x1, waiting for transfers between devices, shards(): lax.psum(dot_right_t(dquery_proj, query_full) + dot_right_t(dkey_proj, ke...  64.2 us
    reduce_scatter x1, waiting for transfers between devices, shards(): lax.psum_scatter(grad_down, ('fsdp', 'context'), scatter_dimension=0, til...  58.7 us
    reduce_scatter x1, waiting for transfers between devices, shards(): lax.psum_scatter(grad_output, ('fsdp', 'context'), scatter_dimension=0, t...  55.5 us
  transfers between devices with their start and end apart: 22, of which 22 were waited for; matrix products, arithmetic and copies ran while one was open for 12% of the time, Pallas kernels for 0%

commit v1 on v0

v1 whole, which is shorter than its diff:
```python
import functools

import jax
import jax.numpy as jnp
from jax import lax
from jax.experimental import pallas as pl
from jax.experimental.pallas import tpu as pltpu
from jax.sharding import PartitionSpec as P

EPS = 1e-06
THETA = 1000000.0
ROWS = ("fsdp", "context")
LOW = jnp.bfloat16
F32 = jnp.float32
LOG2E = 1.4426950408889634
VMEM_BYTES = 56 * 1024 * 1024


def dot_plain(matrix_a, matrix_b):
    return jnp.dot(matrix_a, matrix_b, preferred_element_type=F32)


def dot_right_t(matrix_a, matrix_b):
    return lax.dot_general(matrix_a, matrix_b, (((1,), (1,)), ((), ())), preferred_element_type=F32)


def dot_left_t(matrix_a, matrix_b):
    return lax.dot_general(matrix_a, matrix_b, (((0,), (0,)), ((), ())), preferred_element_type=F32)


def tie(*items):
    return lax.optimization_barrier(items)


def rms_scale(values):
    return lax.rsqrt(jnp.mean(values * values, axis=-1, keepdims=True) + EPS)


def gather_rows(shard):
    return lax.all_gather(shard, ROWS, axis=0, tiled=True)


def scatter_rows(full):
    return lax.psum_scatter(full.astype(LOW), ROWS, scatter_dimension=0, tiled=True)


def sum_tensor(partial):
    return lax.psum(partial.astype(LOW), "tensor")


def add_low(mine, other):
    return (mine.astype(F32) + other.astype(F32)).astype(LOW)


def place(index):
    return index // 4, (index // 2) % 2, index % 2


def staged_pairs(step):
    pairs = []
    for index in range(8):
        x, y, core = place(index)
        if step == "core":
            core = 1 - core
        elif (step == "first") == (core == 0):
            x = 1 - x
        else:
            y = 1 - y
        pairs.append((index, x * 4 + y * 2 + core))
    return pairs


def staged(values, step):
    return lax.ppermute(values, ROWS, staged_pairs(step))


def staged_blocks():
    x, y, core = place(lax.axis_index(ROWS))
    blocks = []
    for step in range(8):
        d_core, d_second, d_first = step // 4, (step // 2) % 2, step % 2
        its_core = core ^ d_core
        its_x = x ^ jnp.where(its_core == 0, d_first, d_second)
        its_y = y ^ jnp.where(its_core == 0, d_second, d_first)
        blocks.append(its_x * 4 + its_y * 2 + its_core)
    return jnp.stack(blocks).astype(jnp.int32)


def staged_gather(shard):
    pair = jnp.concatenate([shard, staged(shard, "first")])
    quad = jnp.concatenate([pair, staged(pair, "second")])
    return jnp.concatenate([quad, staged(quad, "core")])


def staged_scatter(full):
    rows = full.shape[0] // 8
    quad = add_low(full[: 4 * rows], staged(full[4 * rows :], "core"))
    pair = add_low(quad[: 2 * rows], staged(quad[2 * rows :], "second"))
    return pair[:rows].astype(F32) + staged(pair[rows:], "first").astype(F32)


def swap_context(values, bit):
    size = lax.axis_size("context")
    return lax.ppermute(values, "context", [(index, index ^ bit) for index in range(size)])


def params():
    return pltpu.CompilerParams(vmem_limit_bytes=VMEM_BYTES)


def cost(flops, moved):
    return pl.CostEstimate(flops=int(flops), bytes_accessed=int(moved), transcendentals=0)


def whole(shape):
    return pl.BlockSpec(shape, lambda *_: (0,) * len(shape))


def column(ids, step, width):
    return pl.ds(pl.multiple_of(ids[step] * width, width), width)


def first_norm_kernel(ids, hidden, gain, staged_out):
    width = gain.shape[1]
    scale = rms_scale(hidden[...].astype(F32))
    for step in range(gain.shape[0]):
        part = hidden[:, column(ids, step, width)].astype(F32) * scale * gain[step : step + 1, :]
        staged_out[:, step * width : (step + 1) * width] = part.astype(LOW)


def second_norm_kernel(ids, hidden, attn, gain, middle, plain_out, staged_out):
    width = gain.shape[1]
    for step in range(gain.shape[0]):
        spot = column(ids, step, width)
        middle[:, spot] = hidden[:, spot].astype(F32) + attn[:, step * width : (step + 1) * width].astype(F32)
    scale = rms_scale(middle[...])
    for step in range(gain.shape[0]):
        spot = column(ids, step, width)
        part = (middle[:, spot] * scale * gain[step : step + 1, :]).astype(LOW)
        plain_out[:, spot] = part
        staged_out[:, step * width : (step + 1) * width] = part


def second_back_kernel(ids, grad, middle, cotangent, gain, dmiddle, staged_out):
    width = gain.shape[1]
    scale = rms_scale(middle[...])
    total = jnp.zeros_like(scale)
    for step in range(gain.shape[0]):
        spot = column(ids, step, width)
        part = grad[:, spot].astype(F32) * gain[step : step + 1, :] * middle[:, spot]
        total = total + jnp.sum(part, axis=-1, keepdims=True)
    mean = total * scale / middle.shape[1]
    for step in range(gain.shape[0]):
        spot = column(ids, step, width)
        part = grad[:, spot].astype(F32) * gain[step : step + 1, :] - middle[:, spot] * (scale * mean)
        part = cotangent[:, spot].astype(F32) + scale * part
        dmiddle[:, spot] = part
        staged_out[:, step * width : (step + 1) * width] = part.astype(LOW)


def first_back_kernel(ids, grad, hidden, dmiddle, gain, out):
    width = gain.shape[1]
    scale = rms_scale(hidden[...].astype(F32))
    total = jnp.zeros_like(scale)
    for step in range(gain.shape[0]):
        spot = column(ids, step, width)
        part = grad[:, step * width : (step + 1) * width].astype(F32) * gain[step : step + 1, :]
        total = total + jnp.sum(part * hidden[:, spot].astype(F32), axis=-1, keepdims=True)
    mean = total * scale / hidden.shape[1]
    for step in range(gain.shape[0]):
        spot = column(ids, step, width)
        part = grad[:, step * width : (step + 1) * width].astype(F32) * gain[step : step + 1, :]
        out[:, spot] = dmiddle[:, spot] + scale * (part - hidden[:, spot].astype(F32) * (scale * mean))


def row_call(kernel, ids, arrays, gain, out_types):
    rows, width = arrays[0].shape
    tile = min(128, rows)
    spec = pl.BlockSpec((tile, width), lambda step, *_: (step, 0))
    moved = sum(item.size * item.dtype.itemsize for item in arrays) + sum(
        rows * width * jnp.dtype(kind).itemsize for kind in out_types
    )
    return pl.pallas_call(
        kernel,
        grid_spec=pltpu.PrefetchScalarGridSpec(
            num_scalar_prefetch=1,
            grid=(rows // tile,),
            in_specs=[spec] * len(arrays) + [whole(gain.shape)],
            out_specs=[spec] * len(out_types),
        ),
        out_shape=[jax.ShapeDtypeStruct((rows, width), kind) for kind in out_types],
        compiler_params=params(),
        cost_estimate=cost(10 * rows * width, moved),
    )(ids, *arrays, gain)


def rotate(values, cosine, sine):
    return values * cosine + pltpu.roll(values, values.shape[1] // 2, 1) * sine


def head_forward(proj, gain, cosine, sine):
    scale = rms_scale(proj)
    unit = proj * scale
    return rotate(unit * gain, cosine, sine).astype(LOW), unit, scale


def head_backward(grad, unit, scale, gain, cosine, sine):
    turned = rotate(grad.astype(LOW).astype(F32), cosine, -sine)
    scaled = turned * gain
    back = scale * (scaled - unit * jnp.mean(scaled * unit, axis=-1, keepdims=True))
    rows, width = grad.shape
    return back.astype(LOW), jnp.sum((turned * unit).reshape(rows // 8, 8, width), axis=0)


def key_forward_kernel(proj, gain, cosine, sine, out):
    dim = gain.shape[1]
    for head in range(proj.shape[1] // (2 * dim)):
        at = 2 * head * dim
        out[:, at : at + dim] = head_forward(proj[:, at : at + dim], gain[...], cosine[...], sine[...])[0]
        out[:, at + dim : at + 2 * dim] = proj[:, at + dim : at + 2 * dim].astype(LOW)


def key_backward_kernel(mine, other, proj, gain, cosine, sine, out, norm_out):
    dim = gain.shape[1]
    total = jnp.zeros(norm_out.shape, F32)
    for head in range(proj.shape[1] // (2 * dim)):
        at = 2 * head * dim
        scale = rms_scale(proj[:, at : at + dim])
        unit = proj[:, at : at + dim] * scale
        grad = mine[:, at : at + dim].astype(F32) + other[:, at : at + dim].astype(F32)
        back, norm = head_backward(grad, unit, scale, gain[...], cosine[...], sine[...])
        total = total + norm
        out[:, at : at + dim] = back
        spot = slice(at + dim, at + 2 * dim)
        out[:, spot] = (mine[:, spot].astype(F32) + other[:, spot].astype(F32)).astype(LOW)
    norm_out[...] = total


def pair_of(info, step):
    first = info[0]
    late = step > first
    piece = jnp.where(late, 1, 0)
    key_block = jnp.where(late, step - first - 1, step)
    query_block = jnp.where(late, info[1], first)
    return piece, key_block, query_block, info[2 + key_block]


def allowed_pair(shape, half, query_block, key_block, query_seg, key_seg):
    row = lax.rem(lax.broadcasted_iota(jnp.int32, shape, 0), half)
    col = lax.broadcasted_iota(jnp.int32, shape, 1)
    return (col - row <= (query_block - key_block) * half) & (query_seg == key_seg)


def attend_kernel(half, info, qproj, kv, gain, cosine, sine, seg_row, seg_col, out, out_wide, log_out, qs, acc, total, segq):
    dim = gain.shape[1]
    group = qproj.shape[1] // dim
    pairs = info.shape[0] - 1
    factor = LOG2E * dim ** (-0.5)
    for head in range(group):
        cols = slice(head * dim, (head + 1) * dim)
        query = head_forward(qproj[:, cols], gain[...], cosine[...], sine[...])[0]
        for piece in range(2):
            spot = slice(head * half, (head + 1) * half)
            rows = slice(piece * half, (piece + 1) * half)
            qs[piece, spot, :] = query[rows]
            segq[piece, spot, :] = seg_col[rows, :]
    acc[...] = jnp.zeros_like(acc)
    total[...] = jnp.zeros_like(total)
    for step in range(pairs):
        piece, key_block, query_block, spot = pair_of(info, step)
        rows = pl.ds(pl.multiple_of(spot * half, half), half)
        scores = dot_right_t(qs[piece], kv[rows, :dim])
        key_seg = seg_row[:, pl.ds(pl.multiple_of(key_block * half, half), half)]
        allowed = allowed_pair(scores.shape, half, query_block, key_block, segq[piece], key_seg)
        weight = jnp.where(allowed, jnp.exp2(scores * factor), 0.0)
        total[piece] += sum(weight[:, at : at + 128] for at in range(0, half, 128))
        acc[piece] += dot_plain(weight.astype(LOW), kv[rows, dim:])
    for piece in range(2):
        sums = jnp.sum(total[piece], axis=-1, keepdims=True)
        result = acc[piece] / sums
        logs = jnp.broadcast_to(jnp.log2(sums), result.shape)
        for head in range(group):
            cols = slice(head * dim, (head + 1) * dim)
            rows = slice(piece * half, (piece + 1) * half)
            part = result[head * half : (head + 1) * half]
            out[rows, cols] = part.astype(LOW)
            out_wide[rows, cols] = part
            log_out[rows, cols] = logs[head * half : (head + 1) * half]


def attend_back_kernel(
    half, info, qproj, kv, wide, logs, grad, gain, cosine, sine, seg_row, seg_col,
    dq_out, dkv_out, norm_out, qs, gs, segq, ls, ds, dq, dkv,
):
    dim = gain.shape[1]
    group = qproj.shape[1] // dim
    pairs = info.shape[0] - 1
    plain = dim ** (-0.5)
    factor = LOG2E * plain
    for head in range(group):
        cols = slice(head * dim, (head + 1) * dim)
        query = head_forward(qproj[:, cols], gain[...], cosine[...], sine[...])[0]
        delta = jnp.sum(grad[:, cols].astype(F32) * wide[:, cols], axis=-1, keepdims=True)
        for piece in range(2):
            spot = slice(head * half, (head + 1) * half)
            rows = slice(piece * half, (piece + 1) * half)
            qs[piece, spot, :] = query[rows]
            gs[piece, spot, :] = grad[rows, cols]
            segq[piece, spot, :] = seg_col[rows, :]
            ls[piece, spot, :] = logs[rows, head * dim : head * dim + 1]
            ds[piece, spot, :] = delta[rows]
    dq[...] = jnp.zeros_like(dq)
    dkv[...] = jnp.zeros_like(dkv)
    for step in range(pairs):
        piece, key_block, query_block, spot = pair_of(info, step)
        rows = pl.ds(pl.multiple_of(spot * half, half), half)
        query, outer = qs[piece], gs[piece]
        scores = dot_right_t(query, kv[rows, :dim])
        key_seg = seg_row[:, pl.ds(pl.multiple_of(key_block * half, half), half)]
        allowed = allowed_pair(scores.shape, half, query_block, key_block, segq[piece], key_seg)
        prob = jnp.where(allowed, jnp.exp2(scores * factor - ls[piece]), 0.0)
        dprob = dot_right_t(outer, kv[rows, dim:])
        dscores = (prob * (dprob - ds[piece])).astype(LOW)
        dq[piece] += dot_plain(dscores, kv[rows, :dim])
        dkv[rows, :dim] += dot_left_t(dscores, query)
        dkv[rows, dim:] += dot_left_t(prob.astype(LOW), outer)
    dkv_out[:, :dim] = (dkv[:, :dim] * plain).astype(LOW)
    dkv_out[:, dim:] = dkv[:, dim:].astype(LOW)
    total = jnp.zeros(norm_out.shape[1:], F32)
    for head in range(group):
        cols = slice(head * dim, (head + 1) * dim)
        scale = rms_scale(qproj[:, cols])
        unit = qproj[:, cols] * scale
        grads = jnp.concatenate([dq[piece, head * half : (head + 1) * half, :] for piece in range(2)]) * plain
        back, norm = head_backward(grads, unit, scale, gain[...], cosine[...], sine[...])
        total = total + norm
        dq_out[:, cols] = back
    norm_out[0] = total


def heads_spec(rows, width):
    return pl.BlockSpec((rows, width), lambda head, *_: (0, head))


def attend(info, qproj, kv, gain, cosine, sine, seg_row, seg_col):
    rows, qcols = qproj.shape
    total_rows, kvcols = kv.shape
    dim = gain.shape[1]
    heads = kvcols // (2 * dim)
    wide = qcols // heads
    half = rows // 2
    stacked = half * (wide // dim)
    qspec, kspec = heads_spec(rows, wide), heads_spec(total_rows, 2 * dim)
    return pl.pallas_call(
        functools.partial(attend_kernel, half),
        grid_spec=pltpu.PrefetchScalarGridSpec(
            num_scalar_prefetch=1,
            grid=(heads,),
            in_specs=[qspec, kspec, whole(gain.shape), whole(cosine.shape), whole(sine.shape)]
            + [whole(seg_row.shape), whole(seg_col.shape)],
            out_specs=[qspec] * 3,
            scratch_shapes=[
                pltpu.VMEM((2, stacked, dim), LOW),
                pltpu.VMEM((2, stacked, dim), F32),
                pltpu.VMEM((2, stacked, 128), F32),
                pltpu.VMEM((2, stacked, 1), jnp.int32),
            ],
        ),
        out_shape=[jax.ShapeDtypeStruct((rows, qcols), kind) for kind in (LOW, F32, F32)],
        compiler_params=params(),
        cost_estimate=cost(2 * rows * total_rows * qcols * 2, 8 * rows * qcols * 2),
    )(info, qproj, kv, gain, cosine, sine, seg_row, seg_col)


def attend_back(info, qproj, kv, wide_out, logs, grad, gain, cosine, sine, seg_row, seg_col):
    rows, qcols = qproj.shape
    total_rows, kvcols = kv.shape
    dim = gain.shape[1]
    heads = kvcols // (2 * dim)
    wide = qcols // heads
    half = rows // 2
    stacked = half * (wide // dim)
    qspec, kspec = heads_spec(rows, wide), heads_spec(total_rows, 2 * dim)
    return pl.pallas_call(
        functools.partial(attend_back_kernel, half),
        grid_spec=pltpu.PrefetchScalarGridSpec(
            num_scalar_prefetch=1,
            grid=(heads,),
            in_specs=[qspec, kspec, qspec, qspec, qspec]
            + [whole(gain.shape), whole(cosine.shape), whole(sine.shape)]
            + [whole(seg_row.shape), whole(seg_col.shape)],
            out_specs=[qspec, kspec, pl.BlockSpec((1, 8, dim), lambda head, *_: (head, 0, 0))],
            scratch_shapes=[
                pltpu.VMEM((2, stacked, dim), LOW),
                pltpu.VMEM((2, stacked, dim), LOW),
                pltpu.VMEM((2, stacked, 1), jnp.int32),
                pltpu.VMEM((2, stacked, 1), F32),
                pltpu.VMEM((2, stacked, 1), F32),
                pltpu.VMEM((2, stacked, dim), F32),
                pltpu.VMEM((total_rows, 2 * dim), F32),
            ],
        ),
        out_shape=[
            jax.ShapeDtypeStruct((rows, qcols), LOW),
            jax.ShapeDtypeStruct((total_rows, kvcols), LOW),
            jax.ShapeDtypeStruct((heads, 8, dim), F32),
        ],
        compiler_params=params(),
        cost_estimate=cost(5 * rows * total_rows * qcols, 8 * rows * qcols * 4),
    )(info, qproj, kv, wide_out, logs, grad, gain, cosine, sine, seg_row, seg_col)


def key_forward(proj, gain, cosine, sine):
    return pl.pallas_call(
        key_forward_kernel,
        out_shape=jax.ShapeDtypeStruct(proj.shape, LOW),
        compiler_params=params(),
        cost_estimate=cost(10 * proj.size, 8 * proj.size),
    )(proj, gain, cosine, sine)


def key_backward(mine, other, proj, gain, cosine, sine):
    return pl.pallas_call(
        key_backward_kernel,
        out_shape=[
            jax.ShapeDtypeStruct(proj.shape, LOW),
            jax.ShapeDtypeStruct((8, gain.shape[1]), F32),
        ],
        compiler_params=params(),
        cost_estimate=cost(20 * proj.size, 12 * proj.size),
    )(mine, other, proj, gain, cosine, sine)


def feed_kernel(inputs, gate, up, dproduct, product, dgate, dup, dinputs, total):
    step = pl.program_id(0)
    gate_in = dot_plain(inputs[...], gate[...])
    up_in = dot_plain(inputs[...], up[...])
    sigmoid = 1.0 / (1.0 + jnp.exp(-gate_in))
    active = gate_in * sigmoid
    product[...] = (active * up_in).astype(LOW)
    grad = dproduct[...]
    dgate_low = (grad * up_in * sigmoid * (1.0 + gate_in * (1.0 - sigmoid))).astype(LOW)
    dup_low = (grad * active).astype(LOW)
    dgate[...] = dgate_low
    dup[...] = dup_low
    part = dot_right_t(dgate_low, gate[...]) + dot_right_t(dup_low, up[...])

    @pl.when(step == 0)
    def _():
        total[...] = part

    @pl.when(step > 0)
    def _():
        total[...] += part

    @pl.when(step == pl.num_programs(0) - 1)
    def _():
        dinputs[...] = total[...].astype(LOW)


def feed(inputs, gate, up, dproduct):
    rows, width = inputs.shape
    units = gate.shape[1]
    tile = min(256, units)
    wspec = pl.BlockSpec((width, tile), lambda step: (0, step))
    tspec = pl.BlockSpec((rows, tile), lambda step: (0, step))
    return pl.pallas_call(
        feed_kernel,
        grid=(units // tile,),
        in_specs=[whole((rows, width)), wspec, wspec, tspec],
        out_specs=[tspec, tspec, tspec, whole((rows, width))],
        out_shape=[jax.ShapeDtypeStruct((rows, units), LOW)] * 3 + [jax.ShapeDtypeStruct((rows, width), LOW)],
        scratch_shapes=[pltpu.VMEM((rows, width), F32)],
        compiler_params=params(),
        cost_estimate=cost(8 * rows * width * units, 4 * width * units + 10 * rows * units),
    )(inputs, gate, up, dproduct)


def shards(
    hidden_in,
    segments,
    cotangent,
    attn_gain,
    query_weight,
    key_weight,
    value_weight,
    output_weight,
    qnorm_gain,
    knorm_gain,
    ffn_gain,
    gate_weight,
    up_weight,
    down_weight,
):
    is_staged = lax.axis_size("fsdp") == 2 and lax.axis_size("context") == 4
    gather_fast = staged_gather if is_staged else gather_rows
    scatter_fast = staged_scatter if is_staged else scatter_rows
    head_dim = qnorm_gain.shape[0]
    local_rows, width = hidden_in.shape
    shard_rows = query_weight.shape[0]
    pieces = lax.axis_size("context")
    total_rows = local_rows * pieces
    half_rows = local_rows // 2
    value_heads = key_weight.shape[1] // head_dim
    qcols = query_weight.shape[1]
    kcols = key_weight.shape[1]

    def mixed(keys, values):
        parts = []
        for head in range(value_heads):
            spot = slice(head * head_dim, (head + 1) * head_dim)
            parts += [keys[:, spot], values[:, spot]]
        return jnp.concatenate(parts, axis=1)

    def unmixed(both, which):
        starts = [(2 * head + which) * head_dim for head in range(value_heads)]
        return jnp.concatenate([both[:, at : at + head_dim] for at in starts], axis=1)

    gain_row = jnp.concatenate([attn_gain, ffn_gain])[None, :]
    gain_pad = jnp.pad(gain_row, ((0, 15), (0, 2 * kcols - 2 * shard_rows)))
    kv_shard = jnp.concatenate([mixed(key_weight, value_weight), gain_pad])
    kv_ext = gather_fast(kv_shard).reshape(-1, shard_rows + 16, 2 * kcols)
    query_full = gather_fast(query_weight)
    out_full = gather_fast(output_weight)
    kv_full = kv_ext[:, :shard_rows].reshape(-1, 2 * kcols)
    blocks = staged_blocks() if is_staged else jnp.zeros((1,), jnp.int32)
    count = blocks.shape[0]
    gain_one = kv_ext[:, shard_rows, :shard_rows].astype(F32).reshape(count, -1)
    gain_two = kv_ext[:, shard_rows, shard_rows : 2 * shard_rows].astype(F32).reshape(count, -1)
    gate_full = gather_rows(gate_weight)

    me = lax.axis_index("context")
    last = 2 * pieces - 1
    spots = []
    for block in range(2 * pieces):
        owner = block if block < pieces else last - block
        spots.append(2 * (owner ^ me) + (0 if block < pieces else 1))
    info = jnp.stack([me, last - me] + spots).astype(jnp.int32)
    ramp = jnp.arange(half_rows, dtype=jnp.int32)
    positions = jnp.concatenate([me * half_rows + ramp, (last - me) * half_rows + ramp])
    seg_col = jnp.concatenate(
        [
            lax.dynamic_slice_in_dim(segments[0], block * half_rows, half_rows)
            for block in (me, last - me)
        ]
    )[:, None]
    half_dim = head_dim // 2
    inverse = THETA ** (-(jnp.arange(half_dim).astype(F32) * 2.0 / head_dim))
    angles = positions.astype(F32)[:, None] * inverse[None, :]
    cosine = jnp.cos(angles)
    sine = jnp.sin(angles)
    cosine = jnp.concatenate([cosine, cosine], axis=1)
    sine = jnp.concatenate([-sine, sine], axis=1)
    qgain = qnorm_gain.astype(F32)[None, :]
    kgain = knorm_gain.astype(F32)[None, :]

    (inputs_one,) = row_call(first_norm_kernel, blocks, [hidden_in], gain_one, [LOW])
    kv_proj = dot_plain(inputs_one, kv_full)
    kv_own = key_forward(kv_proj, kgain, cosine, sine)
    kv_across = swap_context(kv_own, 2)
    kv_all = jnp.concatenate([kv_own, swap_context(kv_own, 1), kv_across, swap_context(kv_across, 1)])
    query_proj = dot_plain(inputs_one, query_full)
    up_shard, gate_full, query_proj = tie(up_weight, gate_full, query_proj)
    up_full = gather_rows(up_shard)
    attended, attended_wide, logs = attend(
        info, query_proj, kv_all, qgain, cosine, sine, segments, seg_col
    )
    down_shard, up_full, attended = tie(down_weight, up_full, attended)
    down_full = gather_rows(down_shard)
    attn_out = sum_tensor(dot_right_t(attended, out_full))
    dproduct = dot_plain(cotangent, down_full)
    attn_out, dproduct = tie(attn_out, dproduct)
    middle, inputs_two, inputs_two_staged = row_call(
        second_norm_kernel, blocks, [hidden_in, attn_out], gain_two, [F32, LOW, LOW]
    )
    product, dgate, dup_low, dnormed_two_part = feed(inputs_two, gate_full, up_full, dproduct)
    dnormed_two = sum_tensor(dnormed_two_part)

    ffn_part = dot_right_t(product, down_full).astype(LOW)
    down_own = scatter_rows(dot_left_t(cotangent, product))
    gate_own = scatter_fast(dot_left_t(inputs_two_staged, dgate).astype(LOW))
    up_own = scatter_fast(dot_left_t(inputs_two_staged, dup_low).astype(LOW))
    gain_two_part = jnp.sum(dnormed_two_part.astype(F32) * inputs_two.astype(F32), axis=0)
    dnormed_two, ffn_part, gate_own, up_own = tie(dnormed_two, ffn_part, gate_own, up_own)
    ffn_out = sum_tensor(ffn_part)

    dmiddle, dattn = row_call(
        second_back_kernel, blocks, [dnormed_two, middle, cotangent], gain_two, [F32, LOW]
    )
    dattended = dot_plain(dattn, out_full).astype(LOW)
    dquery, dkv_part, qnorm_parts = attend_back(
        info, query_proj, kv_all, attended_wide, logs, dattended, qgain, cosine, sine, segments, seg_col
    )
    dkv_part = dkv_part.reshape(pieces, local_rows, 2 * kcols)
    dkv_pair = add_low(dkv_part[0::2], swap_context(dkv_part[1::2], 1))
    dkv, knorm_parts = key_backward(
        dkv_pair[0], swap_context(dkv_pair[1], 2), kv_proj, kgain, cosine, sine
    )
    output_own = scatter_fast(dot_left_t(dattn, attended).astype(LOW))
    dnormed_one_part = (dot_right_t(dquery, query_full) + dot_right_t(dkv, kv_full)).astype(LOW)
    dnormed_one_part, ffn_out = tie(dnormed_one_part, ffn_out)
    output = (middle + ffn_out.astype(F32)).astype(LOW)
    dnormed_one = sum_tensor(dnormed_one_part)
    qkv_own = scatter_fast(dot_left_t(inputs_one, jnp.concatenate([dquery, dkv], axis=1)).astype(LOW))
    gain_one_part = jnp.sum(dnormed_one_part.astype(F32) * inputs_one.astype(F32), axis=0)
    if is_staged:
        onehot = (blocks[None, :] == jnp.arange(count, dtype=jnp.int32)[:, None]).astype(F32)
        gain_one_part = jnp.dot(
            onehot, gain_one_part.reshape(count, -1), precision=lax.Precision.HIGHEST
        ).reshape(-1)
    small = lax.psum(
        jnp.concatenate(
            [gain_one_part, gain_two_part, jnp.sum(qnorm_parts, axis=(0, 1)), jnp.sum(knorm_parts, axis=0)]
        ),
        ("fsdp", "context", "tensor"),
    )
    dnormed_one, small = tie(dnormed_one, small)
    (input_grad,) = row_call(
        first_back_kernel, blocks, [dnormed_one, hidden_in, dmiddle], gain_one, [F32]
    )
    own = attn_gain.shape[0]
    start = lax.axis_index(ROWS) * own
    gain_one_grad = lax.dynamic_slice_in_dim(small[:width], start, own) / attn_gain.astype(F32)
    gain_two_grad = lax.dynamic_slice_in_dim(small[width : 2 * width], start, own) / ffn_gain.astype(F32)
    qnorm_total = small[2 * width : 2 * width + head_dim]
    knorm_total = small[2 * width + head_dim :]
    qkv_own = qkv_own.astype(F32)
    return (
        output,
        input_grad,
        gain_one_grad,
        qkv_own[:, :qcols],
        unmixed(qkv_own[:, qcols:], 0),
        unmixed(qkv_own[:, qcols:], 1),
        output_own.astype(F32),
        qnorm_total,
        knorm_total,
        gain_two_grad,
        gate_own.astype(F32),
        up_own.astype(F32),
        down_own.astype(F32),
    )


def solution(mesh):
    in_specs = (
        P(("fsdp", "context"), None),
        P("fsdp", None),
        P(("fsdp", "context"), None),
        P(("fsdp", "context")),
        P(("fsdp", "context"), "tensor"),
        P(("fsdp", "context"), "tensor"),
        P(("fsdp", "context"), "tensor"),
        P(("fsdp", "context"), "tensor"),
        P(),
        P(),
        P(("fsdp", "context")),
        P(("fsdp", "context"), "tensor"),
        P(("fsdp", "context"), "tensor"),
        P(("fsdp", "context"), "tensor"),
    )
    out_specs = (
        P(("fsdp", "context"), None),
        P(("fsdp", "context"), None),
        P(("fsdp", "context")),
        P(("fsdp", "context"), "tensor"),
        P(("fsdp", "context"), "tensor"),
        P(("fsdp", "context"), "tensor"),
        P(("fsdp", "context"), "tensor"),
        P(),
        P(),
        P(("fsdp", "context")),
        P(("fsdp", "context"), "tensor"),
        P(("fsdp", "context"), "tensor"),
        P(("fsdp", "context"), "tensor"),
    )
    return jax.shard_map(shards, mesh=mesh, in_specs=in_specs, out_specs=out_specs, check_vma=False)
```

time: 1500 us -> 674 us (0.45)
  waiting for transfers between devices: 1130 us -> 363 us
  matrix products: 176 us -> 51.5 us
  Pallas kernels: 0 us -> 80.1 us
  blocking collectives: 86.4 us -> 54.3 us
  starting transfers between devices: 1.57 us -> 24.8 us
  other arithmetic: 56.2 us -> 39.7 us
    reduce_scatter x9 -> x1, waiting for transfers between devices: 492 us -> 0.01 us  [scatter_rows(): lax.psum_scatter(full.astype(LOW), ROWS, scatter_dimension=0, tiled=True)]
    psum x4, waiting for transfers between devices: 439 us -> 209 us  [sum_tensor(): return lax.psum(partial.astype(LOW), 'tensor')]
    all_gather x9 -> x3, waiting for transfers between devices: 194 us -> 35.8 us  [gather_rows(): return lax.all_gather(shard, ROWS, axis=0, tiled=True)]
    ppermute x0 -> x26, waiting for transfers between devices: none -> 116 us  [the longest x21 82.8 us: staged(): return lax.ppermute(values, ROWS, staged_pairs(step))]
    pallas_call x0 -> x9, Pallas kernels: none -> 80.1 us  [the longest x4 27.9 us: row_call(): pl.pallas_call(kernel, grid_spec=pltpu.PrefetchScalarGridSpec(num_scalar_...]
    dot_general x13 -> x5, matrix products: 97.3 us -> 17.8 us  [the longest x4 17.6 us: dot_plain(): return jnp.dot(matrix_a, matrix_b, preferred_element_type=F32)]
    ppermute x0 -> x26, starting transfers between devices: none -> 24.5 us  [the longest x21 21.7 us: staged(): return lax.ppermute(values, ROWS, staged_pairs(step))]
    unnamed x1 -> x0, blocking collectives: 24 us -> none
  transfers between devices with their start and end apart: 22 -> 34, of which waited for: 22 -> 24; matrix products, arithmetic and copies ran while one was open for 12% -> 16% of each run, Pallas kernels for 0% -> 8%
where the time goes in v1:
time: 674 us; the launch traced here: 664 us
  waiting for transfers between devices  363 us (54%)
  Pallas kernels  80.1 us (12%)
  blocking collectives  54.3 us (8%)
  matrix products  51.5 us (8%)
  other arithmetic  39.7 us (6%)
  local copies, waits for them, and re-layouts  34.7 us (5%)
  starting transfers between devices  24.8 us (4%)
  between operations  15 us (2%)
    psum x4, waiting for transfers between devices, sum_tensor(): return lax.psum(partial.astype(LOW), 'tensor')  209 us
    ppermute x21, waiting for transfers between devices, staged(): return lax.ppermute(values, ROWS, staged_pairs(step))  82.8 us
    psum x1, blocking collectives, shards(): lax.psum(jnp.concatenate([gain_one_part, gain_two_part, jnp.sum(qnorm_par...  54.3 us
    all_gather x3, waiting for transfers between devices, gather_rows(): return lax.all_gather(shard, ROWS, axis=0, tiled=True)  35.8 us
    ppermute x5, waiting for transfers between devices, swap_context(): lax.ppermute(values, 'context', [(index, index ^ bit) for index in range(...  33.6 us
    pallas_call x4, Pallas kernels, row_call(): pl.pallas_call(kernel, grid_spec=pltpu.PrefetchScalarGridSpec(num_scalar_...  27.9 us
    pallas_call x1, Pallas kernels, feed(): pl.pallas_call(feed_kernel, grid=(units // tile,), in_specs=[whole((rows,...  22.3 us
    ppermute x21, starting transfers between devices, staged(): return lax.ppermute(values, ROWS, staged_pairs(step))  21.7 us
  transfers between devices with their start and end apart: 34, of which 24 were waited for; matrix products, arithmetic and copies ran while one was open for 16% of the time, Pallas kernels for 8%

profile of v1, /device:TPU:0, one launch (start us, length us, event | category | flops | bytes accessed | tf_op | source)
XLA Modules:
  0.0 663.7 jit_solution(686093306827821810)
XLA Ops:
  22.5 8.1 %collective-permute-done.4 = bf16[512,512]{1,0:T(8,128)(2,1)S(1)} collective-permute-done((bf16[512,512]{1,0:T(8,128)(2,1)S(1)}, bf16[512,512]{1,0:T(8,128)(2,1)S(1)}, u32[]{:S(2)}, u32[]{:S(2)}) %collective-permute-start.4) | collective-permute-done | bytes 524320 | tf_op jit(solution)/shard_map/ppermute | solution.py:74
  31.7 7.6 %collective-permute-done.1 = bf16[544,512]{1,0:T(8,128)(2,1)S(1)} collective-permute-done((bf16[544,512]{1,0:T(8,128)(2,1)S(1)}, bf16[544,512]{1,0:T(8,128)(2,1)S(1)}, u32[]{:S(2)}, u32[]{:S(2)}) %collective-permute-start.1) | collective-permute-done | bytes 557088 | tf_op jit(solution)/shard_map/ppermute | solution.py:74
  56.6 5.8 all-gather.4.cloned.1.call-done.gate
  74.3 20.5 %collective-permute-done.7 = bf16[512,512]{1,0:T(8,128)(2,1)S(1)} collective-permute-done((bf16[512,512]{1,0:T(8,128)(2,1)}, bf16[512,512]{1,0:T(8,128)(2,1)S(1)}, u32[]{:S(2)}, u32[]{:S(2)}) %collective-permute-start.7) | collective-permute-done | bytes 524320 | tf_op jit(solution)/shard_map/ppermute | solution.py:104
  100.1 8.2 %shard_map.239 = (bf16[512,512]{1,0:T(8,128)(2,1)}, f32[512,512]{1,0:T(8,128)}, f32[512,512]{1,0:T(8,128)}) custom-call(s32[10]{0:T(128)} %stack.79.info, f32[512,512]{1,0:T(8,128)} %fusion.16.qproj, bf16[2048,512]{1,0:T(8,128)(2,1)} %pad_maximum_fusion.kv, f32[1,128]{1,0:T(1,128)} %bitcast_convert_fusion.1.gain, f32[512,128]{1,0:T(8,128)} %pad_maximum_fusion.8.cosine, ...), custom_call_target="tpu_custom_call" | custom-call | flops 2147483648 | bytes 4194304 | tf_op jit(solution)/shard_map/pallas_call | solution.py:354
  108.2 9.4 %all-gather.6.cloned.1.call-done.up = bf16[2048,1536]{1,0:T(8,128)(2,1)} async-done(((bf16[256,1536]{1,0:T(8,128)(2,1)}), bf16[2048,1536]{1,0:T(8,128)(2,1)}) %all-gather.6.cloned.1.call-update) | async-done | bytes 6291472 | tf_op jit(solution)/shard_map/all_gather | solution.py:40
  125.5 14.7 %collective-permute-done.10 = bf16[512,512]{1,0:T(8,128)(2,1)S(1)} collective-permute-done((bf16[512,512]{1,0:T(8,128)(2,1)S(1)}, bf16[512,512]{1,0:T(8,128)(2,1)S(1)}, u32[]{:S(2)}, u32[]{:S(2)}) %collective-permute-start.10) | collective-permute-done | bytes 524320 | tf_op jit(solution)/shard_map/ppermute | solution.py:74
  147.7 20.6 %all-gather.8.cloned.1.call-done = bf16[2048,1536]{1,0:T(8,128)(2,1)} async-done(((bf16[256,1536]{1,0:T(8,128)(2,1)}), bf16[2048,1536]{1,0:T(8,128)(2,1)}) %all-gather.8.cloned.1.call-update) | async-done | bytes 6291472 | tf_op jit(solution)/shard_map/all_gather | solution.py:40
  168.3 7.9 %convolution_bitcast_fusion.dproduct = f32[512,1536]{1,0:T(8,128)} fusion(bf16[512,2048]{1,0:T(8,128)(2,1)S(1)} %copy-done.16, bf16[2048,1536]{1,0:T(8,128)(2,1)} %all-gather.8.cloned.1.call-done), kind=kOutput, calls=%fused_computation.12 | convolution fusion | flops 3221225472 | bytes 11534336 | tf_op jit(solution)/shard_map/dot_general | solution.py:20
  176.2 81.4 %all-reduce.6.cloned.1.call-done.attn = bf16[512,2048]{1,0:T(8,128)(2,1)} async-done(((bf16[512,2048]{1,0:T(8,128)(2,1)}), bf16[512,2048]{1,0:T(8,128)(2,1)}) %all-reduce.6.cloned.1.call-update) | async-done | bytes 2097168 | tf_op jit(solution)/shard_map/psum | solution.py:48
  257.6 6.8 %shard_map.240 = (f32[512,2048]{1,0:T(8,128)}, bf16[512,2048]{1,0:T(8,128)(2,1)}, bf16[512,2048]{1,0:T(8,128)(2,1)}) custom-call(s32[8]{0:T(128)} %stack.68.ids, bf16[512,2048]{1,0:T(8,128)(2,1)} %hidden.5, bf16[512,2048]{1,0:T(8,128)(2,1)} %all-reduce.6.cloned.1.call-done.attn, f32[8,256]{1,0:T(8,128)} %fusion.5.gain), custom_call_target="tpu_custom_call" | custom-call | flops 10485760 | bytes 12582912 | tf_op jit(solution)/shard_map/pallas_call | solution.py:183
  264.4 22.3 %shard_map.241 = (bf16[512,1536]{1,0:T(8,128)(2,1)}, bf16[512,1536]{1,0:T(8,128)(2,1)}, bf16[512,1536]{1,0:T(8,128)(2,1)}, bf16[512,2048]{1,0:T(8,128)(2,1)}) custom-call(bf16[512,2048]{1,0:T(8,128)(2,1)} %get-tuple-element.55.inputs, bf16[2048,1536]{1,0:T(8,128)(2,1)} %all-gather.4.cloned.1.call-done.gate, ...), custom_call_target="tpu_custom_call" | custom-call | flops 12884901888 | bytes 20447232 | tf_op jit(solution)/shard_map/pallas_call | solution.py:467
  311.6 9.0 %collective-permute-done.13 = bf16[512,1536]{1,0:T(8,128)(2,1)} collective-permute-done((bf16[512,1536]{1,0:T(8,128)(2,1)}, bf16[512,1536]{1,0:T(8,128)(2,1)}, u32[]{:S(2)}, u32[]{:S(2)}) %collective-permute-start.13) | collective-permute-done | bytes 1572896 | tf_op jit(solution)/shard_map/ppermute | solution.py:74
  324.8 21.0 %collective-permute-done.16 = bf16[512,1536]{1,0:T(8,128)(2,1)} collective-permute-done((bf16[512,1536]{1,0:T(8,128)(2,1)}, bf16[512,1536]{1,0:T(8,128)(2,1)}, u32[]{:S(2)}, u32[]{:S(2)}) %collective-permute-start.16) | collective-permute-done | bytes 1572896 | tf_op jit(solution)/shard_map/ppermute | solution.py:74
  350.1 8.0 %convolution_convert_fusion.5 = bf16[512,2048]{1,0:T(8,128)(2,1)} fusion(bf16[512,1536]{1,0:T(8,128)(2,1)S(1)} %copy-done.35, bf16[2048,1536]{1,0:T(8,128)(2,1)} %all-gather.8.cloned.1.call-done), kind=kOutput, calls=%fused_computation.16 | convolution fusion | flops 3222274048 | bytes 9961472 | tf_op jit(solution)/shard_map/dot_general | solution.py:24
  363.7 34.8 %all-reduce.8.cloned.1.call-done.grad = bf16[512,2048]{1,0:T(8,128)(2,1)} async-done(((bf16[512,2048]{1,0:T(8,128)(2,1)}), bf16[512,2048]{1,0:T(8,128)(2,1)}) %all-reduce.8.cloned.1.call-update) | async-done | bytes 2097168 | tf_op jit(solution)/shard_map/psum | solution.py:48
  398.6 7.0 %fusion = bf16[2048,1536]{0,1:T(8,128)(2,1)} fusion(bf16[512,1536]{1,0:T(8,128)(2,1)S(1)} %copy-done.36, bf16[512,2048]{1,0:T(8,128)(2,1)} %cotangent.1), kind=kOutput, calls=%fused_computation.3 | convolution fusion | flops 3224371200 | bytes 9961472 | tf_op jit(solution)/shard_map/dot_general | solution.py:28
  405.6 8.4 %shard_map.242 = (f32[512,2048]{1,0:T(8,128)}, bf16[512,2048]{1,0:T(8,128)(2,1)}) custom-call(s32[8]{0:T(128)} %stack.68.ids, bf16[512,2048]{1,0:T(8,128)(2,1)} %all-reduce.8.cloned.1.call-done.grad, f32[512,2048]{1,0:T(8,128)} %get-tuple-element.52.middle, bf16[512,2048]{1,0:T(8,128)(2,1)} %cotangent.1, f32[8,256]{1,0:T(8,128)} %fusion.5.gain), custom_call_target="tpu_custom_call" | custom-call | flops 10485760 | bytes 14680064 | tf_op jit(solution)/shard_map/pallas_call | solution.py:183
  417.7 15.9 %shard_map.243 = (bf16[512,512]{1,0:T(8,128)(2,1)}, bf16[2048,512]{1,0:T(8,128)(2,1)}, f32[2,8,128]{2,1,0:T(8,128)}) custom-call(s32[10]{0:T(128)} %stack.79.info, f32[512,512]{1,0:T(8,128)} %fusion.16.qproj, bf16[2048,512]{1,0:T(8,128)(2,1)} %pad_maximum_fusion.kv, f32[512,512]{1,0:T(8,128)} %get-tuple-element.53.wide, f32[512,512]{1,0:T(8,128)} %get-tuple-element.54.logs, ...), custom_call_target="tpu_custom_call" | custom-call | flops 2684354560 | bytes 8388608 | tf_op jit(solution)/shard_map/pallas_call | solution.py:384
  441.1 12.4 %collective-permute-done.19.other = bf16[512,512]{1,0:T(8,128)(2,1)S(1)} collective-permute-done((bf16[512,512]{1,0:T(8,128)(2,1)S(1)}, bf16[512,512]{1,0:T(8,128)(2,1)S(1)}, u32[]{:S(2)}, u32[]{:S(2)}) %collective-permute-start.19) | collective-permute-done | bytes 524320 | tf_op jit(solution)/shard_map/ppermute | solution.py:104
  468.9 17.3 %all-reduce.10.cloned.1.call-done = bf16[512,2048]{1,0:T(8,128)(2,1)} async-done(((bf16[512,2048]{1,0:T(8,128)(2,1)}), bf16[512,2048]{1,0:T(8,128)(2,1)}) %all-reduce.10.cloned.1.call-update) | async-done | bytes 2097168 | tf_op jit(solution)/shard_map/psum | solution.py:48
  504.3 54.3 %psum.39 = f32[4352]{0:T(1024)S(1)} all-reduce(f32[4352]{0:T(1024)S(1)} %pad_maximum_fusion.12), channel_id=1, replica_groups=mesh['fsdp'=2,'context'=4,'tensor'=4] {'fsdp','context','tensor'}, use_global_device_ids=true, to_apply=%region_8.9 | all-reduce | flops 4352 | bytes 34816 | tf_op jit(solution)/shard_map/psum | solution.py:611
  566.4 75.8 %all-reduce.12.cloned.1.call-done.grad = bf16[512,2048]{1,0:T(8,128)(2,1)} async-done(((bf16[512,2048]{1,0:T(8,128)(2,1)}), bf16[512,2048]{1,0:T(8,128)(2,1)}) %all-reduce.12.cloned.1.call-update) | async-done | bytes 2097168 | tf_op jit(solution)/shard_map/psum | solution.py:48
  644.8 7.8 %shard_map.245 = f32[512,2048]{1,0:T(8,128)} custom-call(s32[8]{0:T(128)} %stack.68.ids, bf16[512,2048]{1,0:T(8,128)(2,1)} %all-reduce.12.cloned.1.call-done.grad, bf16[512,2048]{1,0:T(8,128)(2,1)} %hidden.5, f32[512,2048]{1,0:T(8,128)} %get-tuple-element.75.dmiddle, f32[8,256]{1,0:T(8,128)} %fusion.6.gain), custom_call_target="tpu_custom_call" | custom-call | flops 10485760 | bytes 12582912 | tf_op jit(solution)/shard_map/pallas_call | solution.py:183
  (240 shorter events, 163.8 us)
Async XLA Ops:
  7.2 55.3 %all-gather.4.cloned.1.call-start = ((), (), s32[]{:S(2)}) async-start(), calls=%async_computation.1 | async-start | bytes 7077888 | tf_op jit(solution)/shard_map/all_gather | solution.py:40
  7.9 109.7 %all-gather.6.cloned.1.call-start = ((), (), s32[]{:S(2)}) async-start(), calls=%async_computation.2 | async-start | bytes 7077888 | tf_op jit(solution)/shard_map/all_gather | solution.py:40
  15.6 15.1 %collective-permute-start.4 = (bf16[512,512]{1,0:T(8,128)(2,1)S(1)}, bf16[512,512]{1,0:T(8,128)(2,1)S(1)}, u32[]{:S(2)}, u32[]{:S(2)}) collective-permute-start(bf16[512,512]{1,0:T(8,128)(2,1)S(1)} %pad_maximum_fusion.5), channel_id=1, source_target_pairs={{0,8},{4,20},{8,0},{12,28},{16,24},{20,4},{24,16},{28,12},{1,9},{5... | collective-permute-start | bytes 1572872 | tf_op jit(solution)/shard_map/ppermute | solution.py:74
  21.2 18.1 %collective-permute-start.1 = (bf16[544,512]{1,0:T(8,128)(2,1)S(1)}, bf16[544,512]{1,0:T(8,128)(2,1)S(1)}, u32[]{:S(2)}, u32[]{:S(2)}) collective-permute-start(bf16[544,512]{1,0:T(8,128)(2,1)S(1)} %pad_maximum_fusion.4), channel_id=1, source_target_pairs={{0,8},{4,20},{8,0},{12,28},{16,24},{20,4},{24,16},{28,12},{1,9},{5... | collective-permute-start | bytes 1671176 | tf_op jit(solution)/shard_map/ppermute | solution.py:74
  31.7 11.3 %collective-permute-start.5 = (bf16[1024,512]{1,0:T(8,128)(2,1)}, bf16[1024,512]{1,0:T(8,128)(2,1)}, u32[]{:S(2)}, u32[]{:S(2)}) collective-permute-start(bf16[1024,512]{1,0:T(8,128)(2,1)} %pad_maximum_fusion.2), channel_id=1, source_target_pairs={{0,4},{4,0},{8,12},{12,8},{16,20},{20,16},{24,28},{28,24},{1,5},{5... | collective-permute-start | bytes 3145736 | tf_op jit(solution)/shard_map/ppermute | solution.py:74
  62.5 105.8 %all-gather.8.cloned.1.call-start = ((), (), s32[]{:S(2)}) async-start(), calls=%async_computation.4 | async-start | bytes 7077888 | tf_op jit(solution)/shard_map/all_gather | solution.py:40
  73.1 21.7 %collective-permute-start.7 = (bf16[512,512]{1,0:T(8,128)(2,1)}, bf16[512,512]{1,0:T(8,128)(2,1)S(1)}, u32[]{:S(2)}, u32[]{:S(2)}) collective-permute-start(bf16[512,512]{1,0:T(8,128)(2,1)} %shard_map.238), channel_id=1, source_target_pairs={{0,8},{4,12},{8,0},{12,4},{1,9},{5,13},{9,1},{13,5},{2,10},{6,14},... | collective-permute-start | bytes 1572872 | tf_op jit(solution)/shard_map/ppermute | solution.py:104
  74.3 23.2 %collective-permute-start.6 = (bf16[512,512]{1,0:T(8,128)(2,1)}, bf16[512,512]{1,0:T(8,128)(2,1)S(1)}, u32[]{:S(2)}, u32[]{:S(2)}) collective-permute-start(bf16[512,512]{1,0:T(8,128)(2,1)} %shard_map.238), channel_id=1, source_target_pairs={{0,4},{4,0},{8,12},{12,8},{1,5},{5,1},{9,13},{13,9},{2,6},{6,2},{1... | collective-permute-start | bytes 1572872 | tf_op jit(solution)/shard_map/ppermute | solution.py:104
  117.7 139.9 %all-reduce.6.cloned.1.call-start = ((), (), s32[]{:S(2)}) async-start(), calls=%async_computation.3 | async-start | bytes 4194304 | tf_op jit(solution)/shard_map/psum | solution.py:48
  124.2 16.0 %collective-permute-start.10 = (bf16[512,512]{1,0:T(8,128)(2,1)S(1)}, bf16[512,512]{1,0:T(8,128)(2,1)S(1)}, u32[]{:S(2)}, u32[]{:S(2)}) collective-permute-start(bf16[512,512]{1,0:T(8,128)(2,1)S(1)} %pad_maximum_fusion.6), channel_id=1, source_target_pairs={{0,8},{4,20},{8,0},{12,28},{16,24},{20,4},{24,16},{28,12},{1,9},{5... | collective-permute-start | bytes 1572872 | tf_op jit(solution)/shard_map/ppermute | solution.py:74
  299.8 20.7 %collective-permute-start.13 = (bf16[512,1536]{1,0:T(8,128)(2,1)}, bf16[512,1536]{1,0:T(8,128)(2,1)}, u32[]{:S(2)}, u32[]{:S(2)}) collective-permute-start(bf16[512,1536]{1,0:T(8,128)(2,1)} %slice.188), channel_id=1, source_target_pairs={{0,8},{4,20},{8,0},{12,28},{16,24},{20,4},{24,16},{28,12},{1,9},{5... | collective-permute-start | bytes 4718600 | tf_op jit(solution)/shard_map/ppermute | solution.py:74
  306.5 39.3 %collective-permute-start.16 = (bf16[512,1536]{1,0:T(8,128)(2,1)}, bf16[512,1536]{1,0:T(8,128)(2,1)}, u32[]{:S(2)}, u32[]{:S(2)}) collective-permute-start(bf16[512,1536]{1,0:T(8,128)(2,1)} %slice.194), channel_id=1, source_target_pairs={{0,8},{4,20},{8,0},{12,28},{16,24},{20,4},{24,16},{28,12},{1,9},{5... | collective-permute-start | bytes 4718600 | tf_op jit(solution)/shard_map/ppermute | solution.py:74
  310.9 87.6 %all-reduce.8.cloned.1.call-start = ((), (), s32[]{:S(2)}) async-start(), calls=%async_computation.5 | async-start | bytes 4194304 | tf_op jit(solution)/shard_map/psum | solution.py:48
  311.5 174.7 %all-reduce.10.cloned.1.call-start = ((), (), s32[]{:S(2)}) async-start(), calls=%async_computation.6 | async-start | bytes 4194304 | tf_op jit(solution)/shard_map/psum | solution.py:48
  323.4 34.7 %collective-permute-start.14 = (bf16[256,1536]{1,0:T(8,128)(2,1)}, bf16[256,1536]{1,0:T(8,128)(2,1)}, u32[]{:S(2)}, u32[]{:S(2)}) collective-permute-start(bf16[256,1536]{1,0:T(8,128)(2,1)} %slice.190), channel_id=1, source_target_pairs={{0,16},{4,12},{8,24},{12,4},{16,0},{20,28},{24,8},{28,20},{1,17},{... | collective-permute-start | bytes 2359304 | tf_op jit(solution)/shard_map/ppermute | solution.py:74
  348.6 12.3 %collective-permute-start.17 = (bf16[256,1536]{1,0:T(8,128)(2,1)}, bf16[256,1536]{1,0:T(8,128)(2,1)}, u32[]{:S(2)}, u32[]{:S(2)}) collective-permute-start(bf16[256,1536]{1,0:T(8,128)(2,1)} %slice.196), channel_id=1, source_target_pairs={{0,16},{4,12},{8,24},{12,4},{16,0},{20,28},{24,8},{28,20},{1,17},{... | collective-permute-start | bytes 2359304 | tf_op jit(solution)/shard_map/ppermute | solution.py:74
  398.6 165.3 %reduce-scatter.2.cloned.1.call-start = ((), (), s32[]{:S(2)}) async-start(), calls=%async_computation.8 | async-start | bytes 7077888 | tf_op jit(solution)/shard_map/reduce_scatter | solution.py:44
  436.9 26.8 %collective-permute-start.23 = (bf16[1024,512]{1,0:T(8,128)(2,1)S(1)}, bf16[1024,512]{1,0:T(8,128)(2,1)S(1)}, u32[]{:S(2)}, u32[]{:S(2)}) collective-permute-start(bf16[1024,512]{1,0:T(8,128)(2,1)S(1)} %slice.211), channel_id=1, source_target_pairs={{0,4},{4,0},{8,12},{12,8},{16,20},{20,16},{24,28},{28,24},{1,5},{5... | collective-permute-start | bytes 3145736 | tf_op jit(solution)/shard_map/ppermute | solution.py:74
  439.6 13.9 %collective-permute-start.19 = (bf16[512,512]{1,0:T(8,128)(2,1)S(1)}, bf16[512,512]{1,0:T(8,128)(2,1)S(1)}, u32[]{:S(2)}, u32[]{:S(2)}) collective-permute-start(bf16[512,512]{1,0:T(8,128)(2,1)S(1)} %get-tuple-element.111), channel_id=1, source_target_pairs={{0,8},{4,12},{8,0},{12,4},{1,9},{5,13},{9,1},{13,5},{2,10},{6,14},... | collective-permute-start | bytes 1572872 | tf_op jit(solution)/shard_map/ppermute | solution.py:104
  463.7 34.1 %collective-permute-start.20 = (bf16[1024,1024]{0,1:T(8,128)(2,1)}, bf16[1024,1024]{0,1:T(8,128)(2,1)}, u32[]{:S(2)}, u32[]{:S(2)}) collective-permute-start(bf16[1024,1024]{0,1:T(8,128)(2,1)} %slice.200), channel_id=1, source_target_pairs={{0,4},{4,0},{8,12},{12,8},{16,20},{20,16},{24,28},{28,24},{1,5},{5... | collective-permute-start | bytes 6291464 | tf_op jit(solution)/shard_map/ppermute | solution.py:74
  464.8 24.5 %collective-permute-start.24 = (bf16[512,512]{1,0:T(8,128)(2,1)}, bf16[512,512]{1,0:T(8,128)(2,1)}, u32[]{:S(2)}, u32[]{:S(2)}) collective-permute-start(bf16[512,512]{1,0:T(8,128)(2,1)} %slice.213), channel_id=1, source_target_pairs={{0,8},{4,20},{8,0},{12,28},{16,24},{20,4},{24,16},{28,12},{1,9},{5... | collective-permute-start | bytes 1572872 | tf_op jit(solution)/shard_map/ppermute | solution.py:74
  488.5 153.7 %all-reduce.12.cloned.1.call-start = ((), (), s32[]{:S(2)}) async-start(), calls=%async_computation.7 | async-start | bytes 4194304 | tf_op jit(solution)/shard_map/psum | solution.py:48
  502.7 139.5 %collective-permute-start.21 = (bf16[512,1024]{0,1:T(8,128)(2,1)}, bf16[512,1024]{0,1:T(8,128)(2,1)S(1)}, u32[]{:S(2)}, u32[]{:S(2)}) collective-permute-start(bf16[512,1024]{0,1:T(8,128)(2,1)} %slice.202), channel_id=1, source_target_pairs={{0,8},{4,20},{8,0},{12,28},{16,24},{20,4},{24,16},{28,12},{1,9},{5... | collective-permute-start | bytes 3145736 | tf_op jit(solution)/shard_map/ppermute | solution.py:74
  642.6 11.1 %collective-permute-start.22 = (bf16[256,1024]{0,1:T(8,128)(2,1)S(1)}, bf16[256,1024]{0,1:T(8,128)(2,1)S(1)}, u32[]{:S(2)}, u32[]{:S(2)}) collective-permute-start(bf16[256,1024]{0,1:T(8,128)(2,1)S(1)} %slice.204), channel_id=1, source_target_pairs={{0,16},{4,12},{8,24},{12,4},{16,0},{20,28},{24,8},{28,20},{1,17},{... | collective-permute-start | bytes 1572872 | tf_op jit(solution)/shard_map/ppermute | solution.py:74
  (48 other events, 433.2 us)
Sparse Core Ops, SparseCore 0:
  9.9 52.4 all-gather.3
  64.3 53.2 all-gather.5
  119.6 48.6 all-gather.7
  171.1 86.4 all-reduce.5
  313.9 84.5 all-reduce.7
  400.8 85.4 all-reduce.9
  490.0 63.2 reduce-scatter.1
  555.6 86.5 all-reduce.11

commit v2 on v1

--- a/solution.py
+++ b/solution.py
@@ -86,10 +86,14 @@
     return jnp.stack(blocks).astype(jnp.int32)
 
 
-def staged_gather(shard):
+def staged_halves(shard):
     pair = jnp.concatenate([shard, staged(shard, "first")])
     quad = jnp.concatenate([pair, staged(pair, "second")])
-    return jnp.concatenate([quad, staged(quad, "core")])
+    return [quad, staged(quad, "core")]
+
+
+def staged_gather(shard):
+    return jnp.concatenate(staged_halves(shard))
 
 
 def staged_scatter(full):
@@ -99,6 +103,19 @@
     return pair[:rows].astype(F32) + staged(pair[rows:], "first").astype(F32)
 
 
+def sum_all(values):
+    for axis in ("tensor", "context", "fsdp"):
+        size = lax.axis_size(axis)
+        if size & (size - 1):
+            values = lax.psum(values, axis)
+            continue
+        bit = 1
+        while bit < size:
+            values = values + lax.ppermute(values, axis, [(index, index ^ bit) for index in range(size)])
+            bit *= 2
+    return values
+
+
 def swap_context(values, bit):
     size = lax.axis_size("context")
     return lax.ppermute(values, "context", [(index, index ^ bit) for index in range(size)])
@@ -120,78 +137,117 @@
     return pl.ds(pl.multiple_of(ids[step] * width, width), width)
 
 
-def first_norm_kernel(ids, hidden, gain, staged_out):
-    width = gain.shape[1]
-    scale = rms_scale(hidden[...].astype(F32))
-    for step in range(gain.shape[0]):
-        part = hidden[:, column(ids, step, width)].astype(F32) * scale * gain[step : step + 1, :]
-        staged_out[:, step * width : (step + 1) * width] = part.astype(LOW)
-
-
-def second_norm_kernel(ids, hidden, attn, gain, middle, plain_out, staged_out):
-    width = gain.shape[1]
-    for step in range(gain.shape[0]):
+def stage_kernel(count, ids, values, staged_out):
+    width = values.shape[1] // count
+    for step in range(count):
+        staged_out[:, step * width : (step + 1) * width] = values[:, column(ids, step, width)]
+
+
+def by_rows(rows, body):
+    def run(step, carry):
+        body(pl.ds(pl.multiple_of(step * 16, 16), 16))
+        return carry
+
+    lax.fori_loop(0, rows // 16, run, 0, unroll=2)
+
+
+def row_sum(parts):
+    return jnp.sum(sum(parts), axis=-1, keepdims=True)
+
+
+def scale_of(parts):
+    size = len(parts) * parts[0].shape[1]
+    return lax.rsqrt(row_sum([part * part for part in parts]) / size + EPS)
+
+
+def second_norm_kernel(count, ids, hidden, attn, gain, middle, plain_out):
+    width = hidden.shape[1] // count
+    spots = [column(ids, step, width) for step in range(count)]
+
+    def body(rows):
+        parts = []
+        for step in range(count):
+            part = attn[rows, step * width : (step + 1) * width].astype(F32)
+            parts.append(hidden[rows, spots[step]].astype(F32) + part)
+            middle[rows, spots[step]] = parts[step]
+        scale = scale_of(parts)
+        for step in range(count):
+            plain_out[rows, spots[step]] = (parts[step] * scale * gain[step : step + 1, :]).astype(LOW)
+
+    by_rows(hidden.shape[0], body)
+
+
+def output_kernel(count, ids, middle, ffn, out):
+    width = middle.shape[1] // count
+    for step in range(count):
         spot = column(ids, step, width)
-        middle[:, spot] = hidden[:, spot].astype(F32) + attn[:, step * width : (step + 1) * width].astype(F32)
-    scale = rms_scale(middle[...])
-    for step in range(gain.shape[0]):
-        spot = column(ids, step, width)
-        part = (middle[:, spot] * scale * gain[step : step + 1, :]).astype(LOW)
-        plain_out[:, spot] = part
-        staged_out[:, step * width : (step + 1) * width] = part
-
-
-def second_back_kernel(ids, grad, middle, cotangent, gain, dmiddle, staged_out):
-    width = gain.shape[1]
-    scale = rms_scale(middle[...])
-    total = jnp.zeros_like(scale)
-    for step in range(gain.shape[0]):
-        spot = column(ids, step, width)
-        part = grad[:, spot].astype(F32) * gain[step : step + 1, :] * middle[:, spot]
-        total = total + jnp.sum(part, axis=-1, keepdims=True)
-    mean = total * scale / middle.shape[1]
-    for step in range(gain.shape[0]):
-        spot = column(ids, step, width)
-        part = grad[:, spot].astype(F32) * gain[step : step + 1, :] - middle[:, spot] * (scale * mean)
-        part = cotangent[:, spot].astype(F32) + scale * part
-        dmiddle[:, spot] = part
-        staged_out[:, step * width : (step + 1) * width] = part.astype(LOW)
-
-
-def first_back_kernel(ids, grad, hidden, dmiddle, gain, out):
-    width = gain.shape[1]
-    scale = rms_scale(hidden[...].astype(F32))
-    total = jnp.zeros_like(scale)
-    for step in range(gain.shape[0]):
-        spot = column(ids, step, width)
-        part = grad[:, step * width : (step + 1) * width].astype(F32) * gain[step : step + 1, :]
-        total = total + jnp.sum(part * hidden[:, spot].astype(F32), axis=-1, keepdims=True)
-    mean = total * scale / hidden.shape[1]
-    for step in range(gain.shape[0]):
-        spot = column(ids, step, width)
-        part = grad[:, step * width : (step + 1) * width].astype(F32) * gain[step : step + 1, :]
-        out[:, spot] = dmiddle[:, spot] + scale * (part - hidden[:, spot].astype(F32) * (scale * mean))
-
-
-def row_call(kernel, ids, arrays, gain, out_types):
+        out[:, spot] = (middle[:, spot] + ffn[:, step * width : (step + 1) * width].astype(F32)).astype(LOW)
+
+
+def second_back_kernel(count, ids, grad, middle, cotangent, gain, dmiddle, staged_out, gain_out):
+    width = middle.shape[1] // count
+
+    @pl.when(pl.program_id(0) == 0)
+    def _():
+        gain_out[...] = jnp.zeros_like(gain_out)
+
+    spots = [column(ids, step, width) for step in range(count)]
+
+    def body(rows):
+        parts = [middle[rows, spot] for spot in spots]
+        raw = [grad[rows, spot].astype(F32) for spot in spots]
+        grads = [raw[step] * gain[step : step + 1, :] for step in range(count)]
+        scale = scale_of(parts)
+        mean = row_sum([one * two for one, two in zip(parts, grads)]) * scale * scale / middle.shape[1]
+        for step in range(count):
+            term = raw[step] * parts[step] * scale
+            gain_out[:, spots[step]] += term[:8] + term[8:]
+            part = cotangent[rows, spots[step]].astype(F32) + scale * (grads[step] - parts[step] * mean)
+            dmiddle[rows, spots[step]] = part
+            staged_out[rows, step * width : (step + 1) * width] = part.astype(LOW)
+
+    by_rows(middle.shape[0], body)
+
+
+def first_back_kernel(count, ids, grad, hidden, dmiddle, gain, out):
+    width = hidden.shape[1] // count
+    spots = [column(ids, step, width) for step in range(count)]
+
+    def body(rows):
+        parts = [hidden[rows, spot].astype(F32) for spot in spots]
+        grads = [
+            grad[rows, step * width : (step + 1) * width].astype(F32) * gain[step : step + 1, :]
+            for step in range(count)
+        ]
+        scale = scale_of(parts)
+        mean = row_sum([one * two for one, two in zip(parts, grads)]) * scale * scale / hidden.shape[1]
+        for step in range(count):
+            out[rows, spots[step]] = dmiddle[rows, spots[step]] + scale * (grads[step] - parts[step] * mean)
+
+    by_rows(hidden.shape[0], body)
+
+
+def row_call(kernel, ids, arrays, out_types, gain=None, sums=False, brief=False):
     rows, width = arrays[0].shape
     tile = min(128, rows)
     spec = pl.BlockSpec((tile, width), lambda step, *_: (step, 0))
     moved = sum(item.size * item.dtype.itemsize for item in arrays) + sum(
         rows * width * jnp.dtype(kind).itemsize for kind in out_types
     )
+    gains = [] if gain is None else [gain]
     return pl.pallas_call(
-        kernel,
+        functools.partial(kernel, ids.shape[0]),
         grid_spec=pltpu.PrefetchScalarGridSpec(
             num_scalar_prefetch=1,
             grid=(rows // tile,),
-            in_specs=[spec] * len(arrays) + [whole(gain.shape)],
-            out_specs=[spec] * len(out_types),
+            in_specs=[spec] * len(arrays) + [whole(item.shape) for item in gains],
+            out_specs=[spec] * len(out_types) + [whole((8, width))] * sums,
         ),
-        out_shape=[jax.ShapeDtypeStruct((rows, width), kind) for kind in out_types],
+        out_shape=[jax.ShapeDtypeStruct((rows, width), kind) for kind in out_types]
+        + [jax.ShapeDtypeStruct((8, width), F32)] * sums,
         compiler_params=params(),
-        cost_estimate=cost(10 * rows * width, moved),
-    )(ids, *arrays, gain)
+        cost_estimate=cost(0, rows * width) if brief else cost(10 * rows * width, moved),
+    )(ids, *arrays, *gains)
 
 
 def rotate(values, cosine, sine):
@@ -212,12 +268,50 @@
     return back.astype(LOW), jnp.sum((turned * unit).reshape(rows // 8, 8, width), axis=0)
 
 
-def key_forward_kernel(proj, gain, cosine, sine, out):
-    dim = gain.shape[1]
-    for head in range(proj.shape[1] // (2 * dim)):
+def opening_kernel(count, parts_in, ids, hidden, *refs):
+    weights, refs = refs[:parts_in], refs[parts_in:]
+    kgain, cosine, sine, normed, proj, qproj, out, out_weights = refs
+    width = hidden.shape[1] // count
+    each = count // parts_in
+    high = weights[0].shape[0] // each
+    dim = kgain.shape[1]
+    spots = [column(ids, step, width) for step in range(count)]
+
+    def part_of(step):
+        return weights[step // each], (step % each) * high
+
+    def body(rows):
+        parts = [hidden[rows, spot].astype(F32) for spot in spots]
+        scale = scale_of(parts)
+        for step in range(count):
+            source, at = part_of(step)
+            gain = source[at + width : at + width + 16, :width].astype(F32)[:1]
+            normed[rows, step * width : (step + 1) * width] = (parts[step] * scale * gain).astype(LOW)
+
+    by_rows(hidden.shape[0], body)
+    kvcols, qcols = proj.shape[1], qproj.shape[1]
+
+    def project(cols):
+        total = jnp.zeros((hidden.shape[0], cols.stop - cols.start), F32)
+        for step in range(count):
+            source, at = part_of(step)
+            total = total + dot_plain(normed[:, step * width : (step + 1) * width], source[at : at + width, cols])
+        return total
+
+    total = project(slice(0, kvcols))
+    proj[...] = total
+    for head in range(kvcols // (2 * dim)):
         at = 2 * head * dim
-        out[:, at : at + dim] = head_forward(proj[:, at : at + dim], gain[...], cosine[...], sine[...])[0]
-        out[:, at + dim : at + 2 * dim] = proj[:, at + dim : at + 2 * dim].astype(LOW)
+        out[:, at : at + dim] = head_forward(total[:, at : at + dim], kgain[...], cosine[...], sine[...])[0]
+        out[:, at + dim : at + 2 * dim] = total[:, at + dim : at + 2 * dim].astype(LOW)
+    qproj[...] = project(slice(kvcols, kvcols + qcols))
+
+    @pl.when(pl.program_id(0) == 0)
+    def _():
+        for step in range(count):
+            source, at = part_of(step)
+            far = slice(kvcols + qcols, kvcols + qcols + out_weights.shape[1])
+            out_weights[step * width : (step + 1) * width, :] = source[at : at + width, far]
 
 
 def key_backward_kernel(mine, other, proj, gain, cosine, sine, out, norm_out):
@@ -251,7 +345,16 @@
     return (col - row <= (query_block - key_block) * half) & (query_seg == key_seg)
 
 
-def attend_kernel(half, info, qproj, kv, gain, cosine, sine, seg_row, seg_col, out, out_wide, log_out, qs, acc, total, segq):
+def load_pieces(pieces, kv):
+    rows = pieces[0].shape[0]
+    for place_at, piece in enumerate(pieces):
+        kv[place_at * rows : (place_at + 1) * rows, :] = piece[...]
+
+
+def attend_kernel(half, count, info, qproj, weights, *refs):
+    pieces, (gain, cosine, sine, seg_row, seg_col), refs = refs[:count], refs[count : count + 5], refs[count + 5 :]
+    out, out_wide, log_out, part_out, qs, acc, total, segq, kv, part_sum = refs
+    load_pieces(pieces, kv)
     dim = gain.shape[1]
     group = qproj.shape[1] // dim
     pairs = info.shape[0] - 1
@@ -286,12 +389,25 @@
             out[rows, cols] = part.astype(LOW)
             out_wide[rows, cols] = part
             log_out[rows, cols] = logs[head * half : (head + 1) * half]
-
-
-def attend_back_kernel(
-    half, info, qproj, kv, wide, logs, grad, gain, cosine, sine, seg_row, seg_col,
-    dq_out, dkv_out, norm_out, qs, gs, segq, ls, ds, dq, dkv,
-):
+    here = pl.program_id(0)
+
+    @pl.when(here == 0)
+    def _():
+        part_sum[...] = dot_right_t(out[...], weights[...])
+
+    @pl.when(here > 0)
+    def _():
+        part_sum[...] += dot_right_t(out[...], weights[...])
+
+    @pl.when(here == pl.num_programs(0) - 1)
+    def _():
+        part_out[...] = part_sum[...].astype(LOW)
+
+
+def attend_back_kernel(half, count, info, qproj, wide, logs, grad, *refs):
+    pieces, (gain, cosine, sine, seg_row, seg_col), refs = refs[:count], refs[count : count + 5], refs[count + 5 :]
+    dq_out, keep_out, send_out, norm_out, qs, gs, segq, ls, ds, dq, dkv, kv = refs
+    load_pieces(pieces, kv)
     dim = gain.shape[1]
     group = qproj.shape[1] // dim
     pairs = info.shape[0] - 1
@@ -324,8 +440,12 @@
         dq[piece] += dot_plain(dscores, kv[rows, :dim])
         dkv[rows, :dim] += dot_left_t(dscores, query)
         dkv[rows, dim:] += dot_left_t(prob.astype(LOW), outer)
-    dkv_out[:, :dim] = (dkv[:, :dim] * plain).astype(LOW)
-    dkv_out[:, dim:] = dkv[:, dim:].astype(LOW)
+    rows = 2 * half
+    for at in range(count):
+        target = send_out if at % 2 else keep_out
+        spot, low = slice(at // 2 * rows, (at // 2 + 1) * rows), slice(at * rows, (at + 1) * rows)
+        target[spot, :dim] = (dkv[low, :dim] * plain).astype(LOW)
+        target[spot, dim:] = dkv[low, dim:].astype(LOW)
     total = jnp.zeros(norm_out.shape[1:], F32)
     for head in range(group):
         cols = slice(head * dim, (head + 1) * dim)
@@ -342,54 +462,59 @@
     return pl.BlockSpec((rows, width), lambda head, *_: (0, head))
 
 
-def attend(info, qproj, kv, gain, cosine, sine, seg_row, seg_col):
+def attend(info, qproj, weights, pieces, gain, cosine, sine, seg_row, seg_col):
     rows, qcols = qproj.shape
-    total_rows, kvcols = kv.shape
+    count, kvcols = len(pieces), pieces[0].shape[1]
     dim = gain.shape[1]
     heads = kvcols // (2 * dim)
     wide = qcols // heads
     half = rows // 2
     stacked = half * (wide // dim)
-    qspec, kspec = heads_spec(rows, wide), heads_spec(total_rows, 2 * dim)
+    qspec, kspec = heads_spec(rows, wide), heads_spec(rows, 2 * dim)
+    tables = (gain, cosine, sine, seg_row, seg_col)
     return pl.pallas_call(
-        functools.partial(attend_kernel, half),
+        functools.partial(attend_kernel, half, count),
         grid_spec=pltpu.PrefetchScalarGridSpec(
             num_scalar_prefetch=1,
             grid=(heads,),
-            in_specs=[qspec, kspec, whole(gain.shape), whole(cosine.shape), whole(sine.shape)]
-            + [whole(seg_row.shape), whole(seg_col.shape)],
-            out_specs=[qspec] * 3,
+            in_specs=[qspec, heads_spec(weights.shape[0], wide)]
+            + [kspec] * count
+            + [whole(item.shape) for item in tables],
+            out_specs=[qspec] * 3 + [whole((rows, weights.shape[0]))],
             scratch_shapes=[
                 pltpu.VMEM((2, stacked, dim), LOW),
                 pltpu.VMEM((2, stacked, dim), F32),
                 pltpu.VMEM((2, stacked, 128), F32),
                 pltpu.VMEM((2, stacked, 1), jnp.int32),
+                pltpu.VMEM((count * rows, 2 * dim), LOW),
+                pltpu.VMEM((rows, weights.shape[0]), F32),
             ],
         ),
-        out_shape=[jax.ShapeDtypeStruct((rows, qcols), kind) for kind in (LOW, F32, F32)],
+        out_shape=[jax.ShapeDtypeStruct((rows, qcols), kind) for kind in (LOW, F32, F32)]
+        + [jax.ShapeDtypeStruct((rows, weights.shape[0]), LOW)],
         compiler_params=params(),
-        cost_estimate=cost(2 * rows * total_rows * qcols * 2, 8 * rows * qcols * 2),
-    )(info, qproj, kv, gain, cosine, sine, seg_row, seg_col)
-
-
-def attend_back(info, qproj, kv, wide_out, logs, grad, gain, cosine, sine, seg_row, seg_col):
+        cost_estimate=cost(2 * rows * count * rows * qcols * 2, 8 * rows * qcols * 2),
+    )(info, qproj, weights, *pieces, *tables)
+
+
+def attend_back(info, qproj, wide_out, logs, grad, pieces, gain, cosine, sine, seg_row, seg_col):
     rows, qcols = qproj.shape
-    total_rows, kvcols = kv.shape
+    count, kvcols = len(pieces), pieces[0].shape[1]
     dim = gain.shape[1]
     heads = kvcols // (2 * dim)
     wide = qcols // heads
     half = rows // 2
     stacked = half * (wide // dim)
-    qspec, kspec = heads_spec(rows, wide), heads_spec(total_rows, 2 * dim)
+    qspec, kspec = heads_spec(rows, wide), heads_spec(rows, 2 * dim)
+    part = heads_spec(count // 2 * rows, 2 * dim)
+    tables = (gain, cosine, sine, seg_row, seg_col)
     return pl.pallas_call(
-        functools.partial(attend_back_kernel, half),
+        functools.partial(attend_back_kernel, half, count),
         grid_spec=pltpu.PrefetchScalarGridSpec(
             num_scalar_prefetch=1,
             grid=(heads,),
-            in_specs=[qspec, kspec, qspec, qspec, qspec]
-            + [whole(gain.shape), whole(cosine.shape), whole(sine.shape)]
-            + [whole(seg_row.shape), whole(seg_col.shape)],
-            out_specs=[qspec, kspec, pl.BlockSpec((1, 8, dim), lambda head, *_: (head, 0, 0))],
+            in_specs=[qspec] * 4 + [kspec] * count + [whole(item.shape) for item in tables],
+            out_specs=[qspec, part, part, pl.BlockSpec((1, 8, dim), lambda head, *_: (head, 0, 0))],
             scratch_shapes=[
                 pltpu.VMEM((2, stacked, dim), LOW),
                 pltpu.VMEM((2, stacked, dim), LOW),
@@ -397,26 +522,68 @@
                 pltpu.VMEM((2, stacked, 1), F32),
                 pltpu.VMEM((2, stacked, 1), F32),
                 pltpu.VMEM((2, stacked, dim), F32),
-                pltpu.VMEM((total_rows, 2 * dim), F32),
+                pltpu.VMEM((count * rows, 2 * dim), F32),
+                pltpu.VMEM((count * rows, 2 * dim), LOW),
             ],
         ),
         out_shape=[
             jax.ShapeDtypeStruct((rows, qcols), LOW),
-            jax.ShapeDtypeStruct((total_rows, kvcols), LOW),
+            jax.ShapeDtypeStruct((count // 2 * rows, kvcols), LOW),
+            jax.ShapeDtypeStruct((count // 2 * rows, kvcols), LOW),
             jax.ShapeDtypeStruct((heads, 8, dim), F32),
         ],
         compiler_params=params(),
-        cost_estimate=cost(5 * rows * total_rows * qcols, 8 * rows * qcols * 4),
-    )(info, qproj, kv, wide_out, logs, grad, gain, cosine, sine, seg_row, seg_col)
-
-
-def key_forward(proj, gain, cosine, sine):
+        cost_estimate=cost(0, rows * qcols),
+    )(info, qproj, wide_out, logs, grad, *pieces, *tables)
+
+
+def assemble_kernel(dim, key, value, query, output, gains, out):
+    rows, kcols = key.shape
+    qcols = query.shape[1]
+    for head in range(kcols // dim):
+        spot = slice(head * dim, (head + 1) * dim)
+        out[:rows, 2 * head * dim : (2 * head + 1) * dim] = key[:, spot]
+        out[:rows, (2 * head + 1) * dim : (2 * head + 2) * dim] = value[:, spot]
+    out[:rows, 2 * kcols : 2 * kcols + qcols] = query[...]
+    out[:rows, 2 * kcols + qcols :] = output[...]
+    out[rows:, :] = jnp.zeros((16, out.shape[1]), LOW)
+    out[rows:, : gains.shape[1]] = gains[...]
+
+
+def assemble(key, value, query, output, gain_one, gain_two, dim):
+    gains = jnp.pad(jnp.concatenate([gain_one, gain_two])[None, :], ((0, 15), (0, 0)))
+    cols = 2 * key.shape[1] + query.shape[1] + output.shape[1]
     return pl.pallas_call(
-        key_forward_kernel,
-        out_shape=jax.ShapeDtypeStruct(proj.shape, LOW),
+        functools.partial(assemble_kernel, dim),
+        out_shape=jax.ShapeDtypeStruct((key.shape[0] + 16, cols), LOW),
         compiler_params=params(),
-        cost_estimate=cost(10 * proj.size, 8 * proj.size),
-    )(proj, gain, cosine, sine)
+        cost_estimate=cost(0, 4 * key.shape[0] * cols),
+    )(key, value, query, output, gains)
+
+
+def opening(ids, hidden, halves, kvcols, qcols, kgain, cosine, sine):
+    rows, width = hidden.shape
+    tile = min(256, rows)
+    shapes = [(width, LOW), (kvcols, F32), (qcols, F32), (kvcols, LOW)]
+
+    def tiled(cols):
+        return pl.BlockSpec((tile, cols), lambda step, *_: (step, 0))
+
+    return pl.pallas_call(
+        functools.partial(opening_kernel, ids.shape[0], len(halves)),
+        grid_spec=pltpu.PrefetchScalarGridSpec(
+            num_scalar_prefetch=1,
+            grid=(rows // tile,),
+            in_specs=[tiled(width)]
+            + [whole(item.shape) for item in halves]
+            + [whole(kgain.shape), tiled(cosine.shape[1]), tiled(sine.shape[1])],
+            out_specs=[tiled(cols) for cols, _ in shapes] + [whole((width, qcols))],
+        ),
+        out_shape=[jax.ShapeDtypeStruct((rows, cols), kind) for cols, kind in shapes]
+        + [jax.ShapeDtypeStruct((width, qcols), LOW)],
+        compiler_params=params(),
+        cost_estimate=cost(2 * rows * width * (kvcols + qcols), 4 * rows * width + 2 * width * kvcols),
+    )(ids, hidden, *halves, kgain, cosine, sine)
 
 
 def key_backward(mine, other, proj, gain, cosine, sine):
@@ -427,7 +594,7 @@
             jax.ShapeDtypeStruct((8, gain.shape[1]), F32),
         ],
         compiler_params=params(),
-        cost_estimate=cost(20 * proj.size, 12 * proj.size),
+        cost_estimate=cost(0, proj.size),
     )(mine, other, proj, gain, cosine, sine)
 
 
@@ -458,22 +625,24 @@
         dinputs[...] = total[...].astype(LOW)
 
 
-def feed(inputs, gate, up, dproduct):
+def feed(inputs, gate_up, dproduct):
     rows, width = inputs.shape
-    units = gate.shape[1]
+    units = dproduct.shape[1]
     tile = min(256, units)
-    wspec = pl.BlockSpec((width, tile), lambda step: (0, step))
+    count = units // tile
+    gspec = pl.BlockSpec((width, tile), lambda step: (0, step))
+    uspec = pl.BlockSpec((width, tile), lambda step: (0, step + count))
     tspec = pl.BlockSpec((rows, tile), lambda step: (0, step))
     return pl.pallas_call(
         feed_kernel,
-        grid=(units // tile,),
-        in_specs=[whole((rows, width)), wspec, wspec, tspec],
+        grid=(count,),
+        in_specs=[whole((rows, width)), gspec, uspec, tspec],
         out_specs=[tspec, tspec, tspec, whole((rows, width))],
         out_shape=[jax.ShapeDtypeStruct((rows, units), LOW)] * 3 + [jax.ShapeDtypeStruct((rows, width), LOW)],
         scratch_shapes=[pltpu.VMEM((rows, width), F32)],
         compiler_params=params(),
         cost_estimate=cost(8 * rows * width * units, 4 * width * units + 10 * rows * units),
-    )(inputs, gate, up, dproduct)
+    )(inputs, gate_up, gate_up, dproduct)
 
 
 def shards(
@@ -505,29 +674,33 @@
     qcols = query_weight.shape[1]
     kcols = key_weight.shape[1]
 
-    def mixed(keys, values):
-        parts = []
-        for head in range(value_heads):
-            spot = slice(head * head_dim, (head + 1) * head_dim)
-            parts += [keys[:, spot], values[:, spot]]
-        return jnp.concatenate(parts, axis=1)
-
     def unmixed(both, which):
         starts = [(2 * head + which) * head_dim for head in range(value_heads)]
         return jnp.concatenate([both[:, at : at + head_dim] for at in starts], axis=1)
 
-    gain_row = jnp.concatenate([attn_gain, ffn_gain])[None, :]
-    gain_pad = jnp.pad(gain_row, ((0, 15), (0, 2 * kcols - 2 * shard_rows)))
-    kv_shard = jnp.concatenate([mixed(key_weight, value_weight), gain_pad])
-    kv_ext = gather_fast(kv_shard).reshape(-1, shard_rows + 16, 2 * kcols)
-    query_full = gather_fast(query_weight)
-    out_full = gather_fast(output_weight)
-    kv_full = kv_ext[:, :shard_rows].reshape(-1, 2 * kcols)
     blocks = staged_blocks() if is_staged else jnp.zeros((1,), jnp.int32)
     count = blocks.shape[0]
-    gain_one = kv_ext[:, shard_rows, :shard_rows].astype(F32).reshape(count, -1)
-    gain_two = kv_ext[:, shard_rows, shard_rows : 2 * shard_rows].astype(F32).reshape(count, -1)
-    gate_full = gather_rows(gate_weight)
+    near = 2 * kcols + qcols
+    first_shard = assemble(key_weight, value_weight, query_weight, output_weight, attn_gain, ffn_gain, head_dim)
+    halves = staged_halves(first_shard) if is_staged else [gather_rows(first_shard)]
+
+    def without_gains():
+        parts = [half.reshape(-1, shard_rows + 16, half.shape[1])[:, :shard_rows] for half in halves]
+        return jnp.concatenate([part.reshape(-1, part.shape[2]) for part in parts])
+
+    gain_rows = [half.reshape(-1, shard_rows + 16, half.shape[1])[:, shard_rows] for half in halves]
+    gain_rows = jnp.concatenate(gain_rows).astype(F32)
+    gain_one = gain_rows[:, :shard_rows].reshape(count, -1)
+    gain_two = gain_rows[:, shard_rows : 2 * shard_rows].reshape(count, -1)
+    opening_halves = halves
+    if not is_staged:
+        gain_tail = jnp.pad(gain_one.astype(LOW), ((0, 15), (0, 0)))
+        far = max(first_shard.shape[1], width)
+        opening_halves = [
+            jnp.concatenate(
+                [jnp.pad(item, ((0, 0), (0, far - item.shape[1]))) for item in (without_gains(), gain_tail)]
+            )
+        ]
 
     me = lax.axis_index("context")
     last = 2 * pieces - 1
@@ -554,91 +727,100 @@
     qgain = qnorm_gain.astype(F32)[None, :]
     kgain = knorm_gain.astype(F32)[None, :]
 
-    (inputs_one,) = row_call(first_norm_kernel, blocks, [hidden_in], gain_one, [LOW])
-    kv_proj = dot_plain(inputs_one, kv_full)
-    kv_own = key_forward(kv_proj, kgain, cosine, sine)
+    (cot_staged,) = row_call(stage_kernel, blocks, [cotangent], [LOW])
+    inputs_one, kv_proj, query_proj, kv_own, out_full = opening(
+        blocks, hidden_in, opening_halves, 2 * kcols, qcols, kgain, cosine, sine
+    )
     kv_across = swap_context(kv_own, 2)
-    kv_all = jnp.concatenate([kv_own, swap_context(kv_own, 1), kv_across, swap_context(kv_across, 1)])
-    query_proj = dot_plain(inputs_one, query_full)
-    up_shard, gate_full, query_proj = tie(up_weight, gate_full, query_proj)
-    up_full = gather_rows(up_shard)
-    attended, attended_wide, logs = attend(
-        info, query_proj, kv_all, qgain, cosine, sine, segments, seg_col
-    )
-    down_shard, up_full, attended = tie(down_weight, up_full, attended)
-    down_full = gather_rows(down_shard)
-    attn_out = sum_tensor(dot_right_t(attended, out_full))
-    dproduct = dot_plain(cotangent, down_full)
-    attn_out, dproduct = tie(attn_out, dproduct)
-    middle, inputs_two, inputs_two_staged = row_call(
-        second_norm_kernel, blocks, [hidden_in, attn_out], gain_two, [F32, LOW, LOW]
-    )
-    product, dgate, dup_low, dnormed_two_part = feed(inputs_two, gate_full, up_full, dproduct)
+    kv_pieces = [kv_own, swap_context(kv_own, 1), kv_across, swap_context(kv_across, 1)]
+    gate_up_shard, kv_proj = tie(jnp.concatenate([gate_weight, up_weight], axis=1), kv_proj)
+    gate_up = gather_rows(gate_up_shard)
+    attended, attended_wide, logs, attn_part = attend(
+        info, query_proj, out_full, kv_pieces, qgain, cosine, sine, segments, seg_col
+    )
+    down_shard, logs = tie(down_weight, logs)
+    down_full = gather_fast(down_shard)
+    attn_out = sum_tensor(attn_part)
+    dproduct = dot_plain(cot_staged, down_full)
+    near_full = without_gains()[:, :near]
+    attn_out, dproduct, near_full = tie(attn_out, dproduct, near_full)
+    middle, inputs_two = row_call(second_norm_kernel, blocks, [hidden_in, attn_out], [F32, LOW], gain_two)
+    product, dgate, dup_low, dnormed_two_part = feed(inputs_two, gate_up, dproduct)
     dnormed_two = sum_tensor(dnormed_two_part)
 
     ffn_part = dot_right_t(product, down_full).astype(LOW)
     down_own = scatter_rows(dot_left_t(cotangent, product))
-    gate_own = scatter_fast(dot_left_t(inputs_two_staged, dgate).astype(LOW))
-    up_own = scatter_fast(dot_left_t(inputs_two_staged, dup_low).astype(LOW))
-    gain_two_part = jnp.sum(dnormed_two_part.astype(F32) * inputs_two.astype(F32), axis=0)
-    dnormed_two, ffn_part, gate_own, up_own = tie(dnormed_two, ffn_part, gate_own, up_own)
+    grad_gate = dot_left_t(inputs_two, dgate).astype(LOW)
+    grad_up = dot_left_t(inputs_two, dup_low).astype(LOW)
+    dnormed_two, ffn_part, grad_gate, grad_up = tie(dnormed_two, ffn_part, grad_gate, grad_up)
     ffn_out = sum_tensor(ffn_part)
-
-    dmiddle, dattn = row_call(
-        second_back_kernel, blocks, [dnormed_two, middle, cotangent], gain_two, [F32, LOW]
-    )
+    dmiddle, dattn, gain_two_sums = row_call(
+        second_back_kernel, blocks, [dnormed_two, middle, cotangent], [F32, LOW], gain_two, True, True
+    )
+    gain_two_part = jnp.sum(gain_two_sums, axis=0) / lax.axis_size("tensor")
     dattended = dot_plain(dattn, out_full).astype(LOW)
-    dquery, dkv_part, qnorm_parts = attend_back(
-        info, query_proj, kv_all, attended_wide, logs, dattended, qgain, cosine, sine, segments, seg_col
-    )
-    dkv_part = dkv_part.reshape(pieces, local_rows, 2 * kcols)
-    dkv_pair = add_low(dkv_part[0::2], swap_context(dkv_part[1::2], 1))
+    dquery, dkv_keep, dkv_send, qnorm_parts = attend_back(
+        info, query_proj, attended_wide, logs, dattended, kv_pieces, qgain, cosine, sine, segments, seg_col
+    )
+    grad_gate, down_own, qnorm_parts = tie(grad_gate, down_own, qnorm_parts)
+    gate_own = scatter_rows(grad_gate)
+    dkv_pair = add_low(dkv_keep, swap_context(dkv_send, 1))
     dkv, knorm_parts = key_backward(
-        dkv_pair[0], swap_context(dkv_pair[1], 2), kv_proj, kgain, cosine, sine
+        dkv_pair[:local_rows], swap_context(dkv_pair[local_rows:], 2), kv_proj, kgain, cosine, sine
     )
     output_own = scatter_fast(dot_left_t(dattn, attended).astype(LOW))
-    dnormed_one_part = (dot_right_t(dquery, query_full) + dot_right_t(dkv, kv_full)).astype(LOW)
-    dnormed_one_part, ffn_out = tie(dnormed_one_part, ffn_out)
-    output = (middle + ffn_out.astype(F32)).astype(LOW)
-    dnormed_one = sum_tensor(dnormed_one_part)
-    qkv_own = scatter_fast(dot_left_t(inputs_one, jnp.concatenate([dquery, dkv], axis=1)).astype(LOW))
+    dqkv = jnp.concatenate([dkv, dquery], axis=1)
+    dnormed_one_part = dot_right_t(dqkv, near_full).astype(LOW)
+    later_part, ffn_out = tie(dnormed_one_part, ffn_out)
+    dnormed_one = sum_tensor(later_part)
+    grad_up, gate_own, ffn_out = tie(grad_up, gate_own, ffn_out)
+    (output,) = row_call(output_kernel, blocks, [middle, ffn_out], [LOW])
+    qkv_own = scatter_fast(dot_left_t(inputs_one, dqkv).astype(LOW))
     gain_one_part = jnp.sum(dnormed_one_part.astype(F32) * inputs_one.astype(F32), axis=0)
+    up_own = scatter_rows(grad_up)
     if is_staged:
         onehot = (blocks[None, :] == jnp.arange(count, dtype=jnp.int32)[:, None]).astype(F32)
         gain_one_part = jnp.dot(
             onehot, gain_one_part.reshape(count, -1), precision=lax.Precision.HIGHEST
         ).reshape(-1)
-    small = lax.psum(
+    small = sum_all(
         jnp.concatenate(
             [gain_one_part, gain_two_part, jnp.sum(qnorm_parts, axis=(0, 1)), jnp.sum(knorm_parts, axis=0)]
-        ),
-        ("fsdp", "context", "tensor"),
-    )
-    dnormed_one, small = tie(dnormed_one, small)
-    (input_grad,) = row_call(
-        first_back_kernel, blocks, [dnormed_one, hidden_in, dmiddle], gain_one, [F32]
+        )
     )
     own = attn_gain.shape[0]
     start = lax.axis_index(ROWS) * own
     gain_one_grad = lax.dynamic_slice_in_dim(small[:width], start, own) / attn_gain.astype(F32)
-    gain_two_grad = lax.dynamic_slice_in_dim(small[width : 2 * width], start, own) / ffn_gain.astype(F32)
+    gain_two_grad = lax.dynamic_slice_in_dim(small[width : 2 * width], start, own)
     qnorm_total = small[2 * width : 2 * width + head_dim]
     knorm_total = small[2 * width + head_dim :]
-    qkv_own = qkv_own.astype(F32)
+    query_grad = qkv_own[:, 2 * kcols :]
+    key_grad, value_grad = unmixed(qkv_own, 0), unmixed(qkv_own, 1)
+    gate_own = gate_own.astype(F32)
+    down_own = down_own.astype(F32)
+    up_own = up_own.astype(F32)
+    (
+        dnormed_one, output, gain_one_grad, query_grad, key_grad, value_grad, output_own,
+        qnorm_total, knorm_total, gain_two_grad, gate_own, down_own,
+    ) = tie(
+        dnormed_one, output, gain_one_grad, query_grad, key_grad, value_grad, output_own,
+        qnorm_total, knorm_total, gain_two_grad, gate_own, down_own,
+    )
+    (input_grad,) = row_call(first_back_kernel, blocks, [dnormed_one, hidden_in, dmiddle], [F32], gain_one)
     return (
         output,
         input_grad,
         gain_one_grad,
-        qkv_own[:, :qcols],
-        unmixed(qkv_own[:, qcols:], 0),
-        unmixed(qkv_own[:, qcols:], 1),
+        query_grad.astype(F32),
+        key_grad.astype(F32),
+        value_grad.astype(F32),
         output_own.astype(F32),
         qnorm_total,
         knorm_total,
         gain_two_grad,
-        gate_own.astype(F32),
-        up_own.astype(F32),
-        down_own.astype(F32),
+        gate_own,
+        up_own,
+        down_own,
     )
 
 

time: 674 us -> 503 us (0.75)
  waiting for transfers between devices: 363 us -> 258 us
  blocking collectives: 54.3 us -> 0 us
  Pallas kernels: 80.1 us -> 99.4 us
  other arithmetic: 39.7 us -> 23.6 us
    psum x4, waiting for transfers between devices: 209 us -> 112 us  [sum_tensor(): return lax.psum(partial.astype(LOW), 'tensor')]
    psum x1 -> x0, blocking collectives: 54.3 us -> none  [shards(): lax.psum(jnp.concatenate([gain_one_part, gain_two_part, jnp.sum(qnorm_par...]
    all_gather x3 -> x1, waiting for transfers between devices: 35.8 us -> 0.01 us  [gather_rows(): return lax.all_gather(shard, ROWS, axis=0, tiled=True)]
    ppermute x21 -> x12, waiting for transfers between devices: 82.8 us -> 112 us  [staged(): return lax.ppermute(values, ROWS, staged_pairs(step))]
    pallas_call x8 -> x10, Pallas kernels: 77 us -> 96.1 us  [the longest x5 34.1 us: row_call(): pl.pallas_call(functools.partial(kernel, ids.shape[0]), grid_spec=pltpu.P...]
    ppermute x21 -> x12, starting transfers between devices: 21.7 us -> 12.1 us  [staged(): return lax.ppermute(values, ROWS, staged_pairs(step))]
    dot_general x4 -> x2, matrix products: 17.6 us -> 8.68 us  [dot_plain(): return jnp.dot(matrix_a, matrix_b, preferred_element_type=F32)]
    convert_element_type x9 -> x5, other arithmetic: 11.2 us -> 4.33 us  [add_low(): return (mine.astype(F32) + other.astype(F32)).astype(LOW)]
  transfers between devices with their start and end apart: 34 -> 30, of which waited for: 24 -> 20; matrix products, arithmetic and copies ran while one was open for 16% -> 17% of each run, Pallas kernels for 8% -> 11%
where the time goes in v2:
time: 503 us; the launch traced here: 496 us
  waiting for transfers between devices  258 us (51%)
  Pallas kernels  99.4 us (20%)
  matrix products  44.9 us (9%)
  local copies, waits for them, and re-layouts  30.7 us (6%)
  starting transfers between devices  23.6 us (5%)
  other arithmetic  23.6 us (5%)
  between operations  16.4 us (3%)
    psum x4, waiting for transfers between devices, sum_tensor(): return lax.psum(partial.astype(LOW), 'tensor')  112 us
    ppermute x12, waiting for transfers between devices, staged(): return lax.ppermute(values, ROWS, staged_pairs(step))  112 us
    pallas_call x5, Pallas kernels, row_call(): pl.pallas_call(functools.partial(kernel, ids.shape[0]), grid_spec=pltpu.P...  34.1 us
    ppermute x5, waiting for transfers between devices, swap_context(): lax.ppermute(values, 'context', [(index, index ^ bit) for index in range(...  27.6 us
    dot_general x5, matrix products, dot_left_t(): lax.dot_general(matrix_a, matrix_b, (((0,), (0,)), ((), ())), preferred_e...  24.3 us
    pallas_call x1, Pallas kernels, feed(): pl.pallas_call(feed_kernel, grid=(count,), in_specs=[whole((rows, width))...  22.2 us
    unnamed x75, local copies, waits for them, and re-layouts  17.1 us
    pallas_call x1, Pallas kernels, attend_back(): pl.pallas_call(functools.partial(attend_back_kernel, half, count), grid_s...  15.3 us
  transfers between devices with their start and end apart: 30, of which 20 were waited for; matrix products, arithmetic and copies ran while one was open for 17% of the time, Pallas kernels for 11%

profile of v2, /device:TPU:0, one launch (start us, length us, event | category | flops | bytes accessed | tf_op | source)
XLA Modules:
  0.0 496.3 jit_solution(16889409530481429588)
XLA Ops:
  14.4 10.8 %collective-permute-done = bf16[272,1536]{1,0:T(8,128)(2,1)S(1)} collective-permute-done((bf16[272,1536]{1,0:T(8,128)(2,1)}, bf16[272,1536]{1,0:T(8,128)(2,1)S(1)}, u32[]{:S(2)}, u32[]{:S(2)}) %collective-permute-start) | collective-permute-done | bytes 835616 | tf_op jit(solution)/shard_map/ppermute | solution.py:74
  28.5 19.5 %collective-permute-done.1 = bf16[544,1536]{1,0:T(8,128)(2,1)S(1)} collective-permute-done((bf16[544,1536]{1,0:T(8,128)(2,1)S(1)}, bf16[544,1536]{1,0:T(8,128)(2,1)S(1)}, u32[]{:S(2)}, u32[]{:S(2)}) %collective-permute-start.1) | collective-permute-done | bytes 1671200 | tf_op jit(solution)/shard_map/ppermute | solution.py:74
  54.4 11.1 %shard_map.238 = (bf16[512,2048]{1,0:T(8,128)(2,1)}, f32[512,512]{1,0:T(8,128)}, f32[512,512]{1,0:T(8,128)}, bf16[512,512]{1,0:T(8,128)(2,1)}, bf16[2048,512]{1,0:T(8,128)(2,1)}) custom-call(s32[8]{0:T(128)} %stack.79.ids, bf16[512,2048]{1,0:T(8,128)(2,1)} %hidden.5, bf16[1088,1536]{1,0:T(8,128)(2,1)} %copy-done, ...), custom_call_target="tpu_custom_call" | custom-call | flops 2147483648 | bytes 6291456 | tf_op jit(solution)/shard_map/pallas_call | solution.py:572
  67.6 12.4 %collective-permute-done.4.refs_2_ = bf16[512,512]{1,0:T(8,128)(2,1)S(1)} collective-permute-done((bf16[512,512]{1,0:T(8,128)(2,1)}, bf16[512,512]{1,0:T(8,128)(2,1)S(1)}, u32[]{:S(2)}, u32[]{:S(2)}) %collective-permute-start.4) | collective-permute-done | bytes 524320 | tf_op jit(solution)/shard_map/ppermute | solution.py:121
  83.7 11.2 %shard_map.239 = (bf16[512,512]{1,0:T(8,128)(2,1)}, f32[512,512]{1,0:T(8,128)}, f32[512,512]{1,0:T(8,128)}, bf16[512,2048]{1,0:T(8,128)(2,1)}) custom-call(s32[10]{0:T(128)} %stack.70.info, f32[512,512]{1,0:T(8,128)} %get-tuple-element.68.qproj, bf16[2048,512]{1,0:T(8,128)(2,1)} %get-tuple-element.69.weights, bf16[512,512]{1,0:T(8,128)(2,1)} %get-tuple-element.70.refs_0_, ...), custom_call_target="tpu_custom_call" | custom-call | flops 2147483648 | bytes 4194304 | tf_op jit(solution)/shard_map/pallas_call | solution.py:475
  100.0 11.4 %collective-permute-done.6 = bf16[256,1536]{1,0:T(8,128)(2,1)S(1)} collective-permute-done((bf16[256,1536]{1,0:T(8,128)(2,1)S(1)}, bf16[256,1536]{1,0:T(8,128)(2,1)S(1)}, u32[]{:S(2)}, u32[]{:S(2)}) %collective-permute-start.6) | collective-permute-done | bytes 786464 | tf_op jit(solution)/shard_map/ppermute | solution.py:74
  112.8 34.6 %collective-permute-done.7 = bf16[512,1536]{1,0:T(8,128)(2,1)S(1)} collective-permute-done((bf16[512,1536]{1,0:T(8,128)(2,1)S(1)}, bf16[512,1536]{1,0:T(8,128)(2,1)S(1)}, u32[]{:S(2)}, u32[]{:S(2)}) %collective-permute-start.7) | collective-permute-done | bytes 1572896 | tf_op jit(solution)/shard_map/ppermute | solution.py:74
  171.1 12.1 %all-reduce.6.cloned.1.call-done.attn = bf16[512,2048]{1,0:T(8,128)(2,1)} async-done(((bf16[512,2048]{1,0:T(8,128)(2,1)}), bf16[512,2048]{1,0:T(8,128)(2,1)}) %all-reduce.6.cloned.1.call-update) | async-done | bytes 2097168 | tf_op jit(solution)/shard_map/psum | solution.py:48
  183.2 6.9 %shard_map.241 = (f32[512,2048]{1,0:T(8,128)}, bf16[512,2048]{1,0:T(8,128)(2,1)}) custom-call(s32[8]{0:T(128)} %stack.79.ids, bf16[512,2048]{1,0:T(8,128)(2,1)} %hidden.5, bf16[512,2048]{1,0:T(8,128)(2,1)} %all-reduce.6.cloned.1.call-done.attn, f32[8,256]{1,0:T(8,128)} %get-tuple-element.156.gain), custom_call_target="tpu_custom_call" | custom-call | flops 10485760 | bytes 10485760 | tf_op jit(solution)/shard_map/pallas_call | solution.py:238
  190.1 22.2 %shard_map.242 = (bf16[512,1536]{1,0:T(8,128)(2,1)}, bf16[512,1536]{1,0:T(8,128)(2,1)}, bf16[512,1536]{1,0:T(8,128)(2,1)}, bf16[512,2048]{1,0:T(8,128)(2,1)}) custom-call(bf16[512,2048]{1,0:T(8,128)(2,1)} %get-tuple-element.77.inputs, bf16[2048,3072]{1,0:T(8,128)(2,1)} %all-gather.2.cloned.1.call-done.gate.up, ...), custom_call_target="tpu_custom_call" | custom-call | flops 12884901888 | bytes 20447232 | tf_op jit(solution)/shard_map/pallas_call | solution.py:636
  213.9 6.7 %fusion = bf16[2048,1536]{0,1:T(8,128)(2,1)} fusion(bf16[512,1536]{1,0:T(8,128)(2,1)} %get-tuple-element.82, bf16[512,2048]{1,0:T(8,128)(2,1)S(1)} %copy-done.2), kind=kOutput, calls=%fused_computation.3 | convolution fusion | flops 3224371200 | bytes 9961472 | tf_op jit(solution)/shard_map/dot_general | solution.py:28
  222.3 6.8 %convolution_convert_fusion.2 = bf16[2048,1536]{1,0:T(8,128)(2,1)} fusion(bf16[512,2048]{1,0:T(8,128)(2,1)S(1)} %copy-done.28, bf16[512,1536]{1,0:T(8,128)(2,1)} %get-tuple-element.83), kind=kOutput, calls=%fused_computation.2 | convolution fusion | flops 3224371200 | bytes 9961472 | tf_op jit(solution)/shard_map/dot_general | solution.py:28
  229.1 7.0 %convolution_convert_fusion.1 = bf16[2048,1536]{1,0:T(8,128)(2,1)} fusion(bf16[512,2048]{1,0:T(8,128)(2,1)S(1)} %copy-done.28, bf16[512,1536]{1,0:T(8,128)(2,1)} %get-tuple-element.84), kind=kOutput, calls=%fused_computation.1 | convolution fusion | flops 3224371200 | bytes 9961472 | tf_op jit(solution)/shard_map/dot_general | solution.py:28
  236.2 8.2 %convolution_convert_fusion.6 = bf16[512,2048]{1,0:T(8,128)(2,1)} fusion(bf16[512,1536]{1,0:T(8,128)(2,1)} %get-tuple-element.82, bf16[2048,1536]{1,0:T(8,128)(2,1)} %copy-done.19), kind=kOutput, calls=%fused_computation.12 | convolution fusion | flops 3222274048 | bytes 9961472 | tf_op jit(solution)/shard_map/dot_general | solution.py:24
  244.3 53.7 %all-reduce.8.cloned.1.call-done.grad = bf16[512,2048]{1,0:T(8,128)(2,1)} async-done(((bf16[512,2048]{1,0:T(8,128)(2,1)}), bf16[512,2048]{1,0:T(8,128)(2,1)}) %all-reduce.8.cloned.1.call-update) | async-done | bytes 2097168 | tf_op jit(solution)/shard_map/psum | solution.py:48
  298.3 8.8 %shard_map.243 = (f32[512,2048]{1,0:T(8,128)}, bf16[512,2048]{1,0:T(8,128)(2,1)}, f32[8,2048]{1,0:T(8,128)}) custom-call(s32[8]{0:T(128)} %stack.79.ids, bf16[512,2048]{1,0:T(8,128)(2,1)} %all-reduce.8.cloned.1.call-done.grad, f32[512,2048]{1,0:T(8,128)} %get-tuple-element.86.middle, bf16[512,2048]{1,0:T(8,128)(2,1)} %cotangent.1, ...), custom_call_target="tpu_custom_call" | custom-call | bytes 1048576 | tf_op jit(solution)/shard_map/pallas_call | solution.py:238
  310.8 15.3 %shard_map.244 = (bf16[512,512]{1,0:T(8,128)(2,1)}, bf16[1024,512]{1,0:T(8,128)(2,1)}, bf16[1024,512]{1,0:T(8,128)(2,1)}, f32[2,8,128]{2,1,0:T(8,128)}) custom-call(s32[10]{0:T(128)} %stack.70.info, f32[512,512]{1,0:T(8,128)} %get-tuple-element.68.qproj, f32[512,512]{1,0:T(8,128)} %get-tuple-element.71.wide, f32[512,512]{1,0:T(8,128)} %get-tuple-element.73.logs, ...), custom_call_target="tpu_custom_call" | custom-call | bytes 262144 | tf_op jit(solution)/shard_map/pallas_call | solution.py:511
  332.7 12.5 %collective-permute-done.10.other = bf16[512,512]{1,0:T(8,128)(2,1)S(1)} collective-permute-done((bf16[512,512]{1,0:T(8,128)(2,1)S(1)}, bf16[512,512]{1,0:T(8,128)(2,1)S(1)}, u32[]{:S(2)}, u32[]{:S(2)}) %collective-permute-start.10) | collective-permute-done | bytes 524320 | tf_op jit(solution)/shard_map/ppermute | solution.py:121
  354.4 31.4 %all-reduce.10.cloned.1.call-done.ffn = bf16[512,2048]{1,0:T(8,128)(2,1)} async-done(((bf16[512,2048]{1,0:T(8,128)(2,1)}), bf16[512,2048]{1,0:T(8,128)(2,1)}) %all-reduce.10.cloned.1.call-update) | async-done | bytes 2097168 | tf_op jit(solution)/shard_map/psum | solution.py:48
  399.1 18.8 %collective-permute-done.20 = bf16[512,512]{1,0:T(8,128)(2,1)} collective-permute-done((bf16[512,512]{1,0:T(8,128)(2,1)}, bf16[512,512]{1,0:T(8,128)(2,1)}, u32[]{:S(2)}, u32[]{:S(2)}) %collective-permute-start.20) | collective-permute-done | bytes 524320 | tf_op jit(solution)/shard_map/ppermute | solution.py:74
  424.1 7.2 %collective-permute-done.21 = bf16[256,512]{1,0:T(8,128)(2,1)} collective-permute-done((bf16[256,512]{1,0:T(8,128)(2,1)S(1)}, bf16[256,512]{1,0:T(8,128)(2,1)}, u32[]{:S(2)}, u32[]{:S(2)}) %collective-permute-start.21) | collective-permute-done | bytes 262176 | tf_op jit(solution)/shard_map/ppermute | solution.py:74
  435.2 6.2 %collective-permute-done.18 = bf16[256,1024]{0,1:T(8,128)(2,1)S(1)} collective-permute-done((bf16[256,1024]{0,1:T(8,128)(2,1)S(1)}, bf16[256,1024]{0,1:T(8,128)(2,1)S(1)}, u32[]{:S(2)}, u32[]{:S(2)}) %collective-permute-start.18) | collective-permute-done | bytes 524320 | tf_op jit(solution)/shard_map/ppermute | solution.py:74
  459.4 14.7 %all-reduce.12.cloned.1.call-done.grad = bf16[512,2048]{1,0:T(8,128)(2,1)} async-done(((bf16[512,2048]{1,0:T(8,128)(2,1)}), bf16[512,2048]{1,0:T(8,128)(2,1)}) %all-reduce.12.cloned.1.call-update) | async-done | bytes 2097168 | tf_op jit(solution)/shard_map/psum | solution.py:48
  478.3 7.8 %shard_map.247 = f32[512,2048]{1,0:T(8,128)} custom-call(s32[8]{0:T(128)} %stack.79.ids, bf16[512,2048]{1,0:T(8,128)(2,1)} %all-reduce.12.cloned.1.call-done.grad, bf16[512,2048]{1,0:T(8,128)(2,1)} %hidden.5, f32[512,2048]{1,0:T(8,128)} %get-tuple-element.111.dmiddle, f32[8,256]{1,0:T(8,128)} %get-tuple-element.155.gain), custom_call_target="tpu_custom_call" | custom-call | flops 10485760 | bytes 12582912 | tf_op jit(solution)/shard_map/pallas_call | solution.py:238
  (207 shorter events, 122.3 us)
Async XLA Ops:
  8.0 175.2 %all-reduce.6.cloned.1.call-start = ((), (), s32[]{:S(2)}) async-start(), calls=%async_computation.3 | async-start | bytes 4194304 | tf_op jit(solution)/shard_map/psum | solution.py:48
  11.5 13.7 %collective-permute-start = (bf16[272,1536]{1,0:T(8,128)(2,1)}, bf16[272,1536]{1,0:T(8,128)(2,1)S(1)}, u32[]{:S(2)}, u32[]{:S(2)}) collective-permute-start(bf16[272,1536]{1,0:T(8,128)(2,1)} %shard_map.237), channel_id=1, source_target_pairs={{0,16},{4,12},{8,24},{12,4},{16,0},{20,28},{24,8},{28,20},{1,17},{... | collective-permute-start | bytes 2506760 | tf_op jit(solution)/shard_map/ppermute | solution.py:74
  26.5 21.5 %collective-permute-start.1 = (bf16[544,1536]{1,0:T(8,128)(2,1)S(1)}, bf16[544,1536]{1,0:T(8,128)(2,1)S(1)}, u32[]{:S(2)}, u32[]{:S(2)}) collective-permute-start(bf16[544,1536]{1,0:T(8,128)(2,1)S(1)} %pad_maximum_fusion.3), channel_id=1, source_target_pairs={{0,8},{4,20},{8,0},{12,28},{16,24},{20,4},{24,16},{28,12},{1,9},{5... | collective-permute-start | bytes 5013512 | tf_op jit(solution)/shard_map/ppermute | solution.py:74
  48.3 6.1 %collective-permute-start.2 = (bf16[1088,1536]{1,0:T(8,128)(2,1)S(1)}, bf16[1088,1536]{1,0:T(8,128)(2,1)}, u32[]{:S(2)}, u32[]{:S(2)}) collective-permute-start(bf16[1088,1536]{1,0:T(8,128)(2,1)S(1)} %pad_maximum_fusion.1.refs_0_), channel_id=1, source_target_pairs={{0,4},{4,0},{8,12},{12,8},{16,20},{20,16},{24,28},{28,24},{1,5},{5... | collective-permute-start | bytes 10027016 | tf_op jit(solution)/shard_map/ppermute | solution.py:74
  65.5 14.5 %collective-permute-start.4 = (bf16[512,512]{1,0:T(8,128)(2,1)}, bf16[512,512]{1,0:T(8,128)(2,1)S(1)}, u32[]{:S(2)}, u32[]{:S(2)}) collective-permute-start(bf16[512,512]{1,0:T(8,128)(2,1)} %get-tuple-element.70.refs_0_), channel_id=1, source_target_pairs={{0,8},{4,12},{8,0},{12,4},{1,9},{5,13},{9,1},{13,5},{2,10},{6,14},... | collective-permute-start | bytes 1572872 | tf_op jit(solution)/shard_map/ppermute | solution.py:121
  67.6 15.2 %collective-permute-start.3 = (bf16[512,512]{1,0:T(8,128)(2,1)}, bf16[512,512]{1,0:T(8,128)(2,1)S(1)}, u32[]{:S(2)}, u32[]{:S(2)}) collective-permute-start(bf16[512,512]{1,0:T(8,128)(2,1)} %get-tuple-element.70.refs_0_), channel_id=1, source_target_pairs={{0,4},{4,0},{8,12},{12,8},{1,5},{5,1},{9,13},{13,9},{2,6},{6,2},{1... | collective-permute-start | bytes 1572872 | tf_op jit(solution)/shard_map/ppermute | solution.py:121
  95.0 95.1 %all-gather.2.cloned.1.call-start = ((), (), s32[]{:S(2)}) async-start(), calls=%async_computation.4 | async-start | bytes 14155776 | tf_op jit(solution)/shard_map/all_gather | solution.py:40
  97.7 200.3 %all-reduce.8.cloned.1.call-start = ((), (), s32[]{:S(2)}) async-start(), calls=%async_computation.5 | async-start | bytes 4194304 | tf_op jit(solution)/shard_map/psum | solution.py:48
  98.3 13.2 %collective-permute-start.6 = (bf16[256,1536]{1,0:T(8,128)(2,1)S(1)}, bf16[256,1536]{1,0:T(8,128)(2,1)S(1)}, u32[]{:S(2)}, u32[]{:S(2)}) collective-permute-start(bf16[256,1536]{1,0:T(8,128)(2,1)S(1)} %copy-done.4), channel_id=1, source_target_pairs={{0,16},{4,12},{8,24},{12,4},{16,0},{20,28},{24,8},{28,20},{1,17},{... | collective-permute-start | bytes 2359304 | tf_op jit(solution)/shard_map/ppermute | solution.py:74
  111.6 35.8 %collective-permute-start.7 = (bf16[512,1536]{1,0:T(8,128)(2,1)S(1)}, bf16[512,1536]{1,0:T(8,128)(2,1)S(1)}, u32[]{:S(2)}, u32[]{:S(2)}) collective-permute-start(bf16[512,1536]{1,0:T(8,128)(2,1)S(1)} %pad_maximum_fusion.4), channel_id=1, source_target_pairs={{0,8},{4,20},{8,0},{12,28},{16,24},{20,4},{24,16},{28,12},{1,9},{5... | collective-permute-start | bytes 4718600 | tf_op jit(solution)/shard_map/ppermute | solution.py:74
  149.2 11.9 %collective-permute-start.8 = (bf16[1024,1536]{1,0:T(8,128)(2,1)}, bf16[1024,1536]{1,0:T(8,128)(2,1)}, u32[]{:S(2)}, u32[]{:S(2)}) collective-permute-start(bf16[1024,1536]{1,0:T(8,128)(2,1)} %pad_maximum_fusion.2), channel_id=1, source_target_pairs={{0,4},{4,0},{8,12},{12,8},{16,20},{20,16},{24,28},{28,24},{1,5},{5... | collective-permute-start | bytes 9437192 | tf_op jit(solution)/shard_map/ppermute | solution.py:74
  212.4 113.8 %reduce-scatter.4.cloned.1.call-start = ((), (), s32[]{:S(2)}) async-start(), calls=%async_computation.8 | async-start | bytes 7077888 | tf_op jit(solution)/shard_map/reduce_scatter | solution.py:44
  220.7 165.1 %all-reduce.10.cloned.1.call-start = ((), (), s32[]{:S(2)}) async-start(), calls=%async_computation.6 | async-start | bytes 4194304 | tf_op jit(solution)/shard_map/psum | solution.py:48
  298.0 88.8 %reduce-scatter.6.cloned.1.call-start = ((), (), s32[]{:S(2)}) async-start(), calls=%async_computation.9 | async-start | bytes 7077888 | tf_op jit(solution)/shard_map/reduce_scatter | solution.py:44
  326.2 147.8 %all-reduce.12.cloned.1.call-start = ((), (), s32[]{:S(2)}) async-start(), calls=%async_computation.7 | async-start | bytes 4194304 | tf_op jit(solution)/shard_map/psum | solution.py:48
  331.2 14.0 %collective-permute-start.10 = (bf16[512,512]{1,0:T(8,128)(2,1)S(1)}, bf16[512,512]{1,0:T(8,128)(2,1)S(1)}, u32[]{:S(2)}, u32[]{:S(2)}) collective-permute-start(bf16[512,512]{1,0:T(8,128)(2,1)S(1)} %get-tuple-element.153), channel_id=1, source_target_pairs={{0,8},{4,12},{8,0},{12,4},{1,9},{5,13},{9,1},{13,5},{2,10},{6,14},... | collective-permute-start | bytes 1572872 | tf_op jit(solution)/shard_map/ppermute | solution.py:121
  385.9 100.3 %reduce-scatter.8.cloned.1.call-start = ((), (), s32[]{:S(2)}) async-start(), calls=%async_computation.10 | async-start | bytes 7077888 | tf_op jit(solution)/shard_map/reduce_scatter | solution.py:44
  392.3 4.8 collective-permute-start.19
  395.7 24.1 %collective-permute-start.17 = (bf16[512,1024]{0,1:T(8,128)(2,1)}, bf16[512,1024]{0,1:T(8,128)(2,1)}, u32[]{:S(2)}, u32[]{:S(2)}) collective-permute-start(bf16[512,1024]{0,1:T(8,128)(2,1)} %slice.130), channel_id=1, source_target_pairs={{0,8},{4,20},{8,0},{12,28},{16,24},{20,4},{24,16},{28,12},{1,9},{5... | collective-permute-start | bytes 3145736 | tf_op jit(solution)/shard_map/ppermute | solution.py:74
  398.2 19.7 %collective-permute-start.20 = (bf16[512,512]{1,0:T(8,128)(2,1)}, bf16[512,512]{1,0:T(8,128)(2,1)}, u32[]{:S(2)}, u32[]{:S(2)}) collective-permute-start(bf16[512,512]{1,0:T(8,128)(2,1)} %slice.141), channel_id=1, source_target_pairs={{0,8},{4,20},{8,0},{12,28},{16,24},{20,4},{24,16},{28,12},{1,9},{5... | collective-permute-start | bytes 1572872 | tf_op jit(solution)/shard_map/ppermute | solution.py:74
  419.1 12.1 %collective-permute-start.21 = (bf16[256,512]{1,0:T(8,128)(2,1)S(1)}, bf16[256,512]{1,0:T(8,128)(2,1)}, u32[]{:S(2)}, u32[]{:S(2)}) collective-permute-start(bf16[256,512]{1,0:T(8,128)(2,1)S(1)} %slice.143), channel_id=1, source_target_pairs={{0,16},{4,12},{8,24},{12,4},{16,0},{20,28},{24,8},{28,20},{1,17},{... | collective-permute-start | bytes 786440 | tf_op jit(solution)/shard_map/ppermute | solution.py:74
  421.5 19.8 %collective-permute-start.18 = (bf16[256,1024]{0,1:T(8,128)(2,1)S(1)}, bf16[256,1024]{0,1:T(8,128)(2,1)S(1)}, u32[]{:S(2)}, u32[]{:S(2)}) collective-permute-start(bf16[256,1024]{0,1:T(8,128)(2,1)S(1)} %slice.132), channel_id=1, source_target_pairs={{0,16},{4,12},{8,24},{12,4},{16,0},{20,28},{24,8},{28,20},{1,17},{... | collective-permute-start | bytes 1572872 | tf_op jit(solution)/shard_map/ppermute | solution.py:74
  423.0 10.2 %collective-permute-start.11 = (f32[4352]{0:T(1024)S(1)}, f32[4352]{0:T(1024)S(1)}, u32[]{:S(2)}, u32[]{:S(2)}) collective-permute-start(f32[4352]{0:T(1024)S(1)} %pad_maximum_fusion.10), channel_id=1, source_target_pairs={{0,1},{1,0},{2,3},{3,2},{4,5},{5,4},{6,7},{7,6},{8,9},{9,8},{10,11... | collective-permute-start | bytes 52232 | tf_op jit(solution)/shard_map/ppermute | solution.py:114
  433.2 8.3 %collective-permute-start.12 = (f32[4352]{0:T(1024)S(1)}, f32[4352]{0:T(1024)S(1)}, u32[]{:S(2)}, u32[]{:S(2)}) collective-permute-start(f32[4352]{0:T(1024)S(1)} %fusion.4), channel_id=1, source_target_pairs={{0,2},{1,3},{2,0},{3,1},{4,6},{5,7},{6,4},{7,5},{8,10},{9,11},{10,... | collective-permute-start | bytes 52232 | tf_op jit(solution)/shard_map/ppermute | solution.py:114
  (40 other events, 248.1 us)
Sparse Core Ops, SparseCore 0:
  95.1 88.0 all-reduce.5
  212.5 85.4 all-reduce.7
  300.4 85.4 all-reduce.9
  388.2 85.7 all-reduce.11
Sparse Core Ops, SparseCore 1:
  98.1 82.7 all-gather.1
  220.8 60.5 reduce-scatter.3
  326.3 60.5 reduce-scatter.5
  390.3 68.7 reduce-scatter.7

commit v3 on v2

--- a/solution.py
+++ b/solution.py
@@ -62,7 +62,7 @@
         x, y, core = place(index)
         if step == "core":
             core = 1 - core
-        elif (step == "first") == (core == 0):
+        elif step[core % len(step)] == "x":
             x = 1 - x
         else:
             y = 1 - y
@@ -74,33 +74,43 @@
     return lax.ppermute(values, ROWS, staged_pairs(step))
 
 
-def staged_blocks():
+def staged_blocks(first="xy"):
     x, y, core = place(lax.axis_index(ROWS))
     blocks = []
     for step in range(8):
         d_core, d_second, d_first = step // 4, (step // 2) % 2, step % 2
         its_core = core ^ d_core
-        its_x = x ^ jnp.where(its_core == 0, d_first, d_second)
-        its_y = y ^ jnp.where(its_core == 0, d_second, d_first)
+        x_first = its_core == 0 if first == "xy" else first == "x"
+        its_x = x ^ jnp.where(x_first, d_first, d_second)
+        its_y = y ^ jnp.where(x_first, d_second, d_first)
         blocks.append(its_x * 4 + its_y * 2 + its_core)
     return jnp.stack(blocks).astype(jnp.int32)
 
 
-def staged_halves(shard):
-    pair = jnp.concatenate([shard, staged(shard, "first")])
-    quad = jnp.concatenate([pair, staged(pair, "second")])
+OTHER = {"xy": "yx", "yx": "xy", "x": "y", "y": "x"}
+
+
+def staged_pair(shard, first="xy"):
+    return jnp.concatenate([shard, staged(shard, first)])
+
+
+def staged_quad(pair, first="xy"):
+    return jnp.concatenate([pair, staged(pair, OTHER[first])])
+
+
+def staged_halves(quad):
     return [quad, staged(quad, "core")]
 
 
 def staged_gather(shard):
-    return jnp.concatenate(staged_halves(shard))
-
-
-def staged_scatter(full):
+    return jnp.concatenate(staged_halves(staged_quad(staged_pair(shard))))
+
+
+def staged_scatter(full, first="xy"):
     rows = full.shape[0] // 8
     quad = add_low(full[: 4 * rows], staged(full[4 * rows :], "core"))
-    pair = add_low(quad[: 2 * rows], staged(quad[2 * rows :], "second"))
-    return pair[:rows].astype(F32) + staged(pair[rows:], "first").astype(F32)
+    pair = add_low(quad[: 2 * rows], staged(quad[2 * rows :], OTHER[first]))
+    return pair[:rows].astype(F32) + staged(pair[rows:], first).astype(F32)
 
 
 def sum_all(values):
@@ -148,7 +158,7 @@
         body(pl.ds(pl.multiple_of(step * 16, 16), 16))
         return carry
 
-    lax.fori_loop(0, rows // 16, run, 0, unroll=2)
+    lax.fori_loop(0, rows // 16, run, 0, unroll=4)
 
 
 def row_sum(parts):
@@ -158,6 +168,20 @@
 def scale_of(parts):
     size = len(parts) * parts[0].shape[1]
     return lax.rsqrt(row_sum([part * part for part in parts]) / size + EPS)
+
+
+def first_norm_kernel(count, ids, hidden, gain, staged_out):
+    width = hidden.shape[1] // count
+    spots = [column(ids, step, width) for step in range(count)]
+
+    def body(rows):
+        parts = [hidden[rows, spot].astype(F32) for spot in spots]
+        scale = scale_of(parts)
+        for step in range(count):
+            part = parts[step] * scale * gain[step : step + 1, :]
+            staged_out[rows, step * width : (step + 1) * width] = part.astype(LOW)
+
+    by_rows(hidden.shape[0], body)
 
 
 def second_norm_kernel(count, ids, hidden, attn, gain, middle, plain_out):
@@ -227,27 +251,33 @@
     by_rows(hidden.shape[0], body)
 
 
-def row_call(kernel, ids, arrays, out_types, gain=None, sums=False, brief=False):
+def row_call(kernel, ids, arrays, out_types, gain=None, sums=False, after=()):
     rows, width = arrays[0].shape
-    tile = min(128, rows)
+    tile = min(256, rows)
     spec = pl.BlockSpec((tile, width), lambda step, *_: (step, 0))
     moved = sum(item.size * item.dtype.itemsize for item in arrays) + sum(
         rows * width * jnp.dtype(kind).itemsize for kind in out_types
     )
     gains = [] if gain is None else [gain]
+
+    def ordered(ids, *refs):
+        kernel(ids.shape[0], ids, *refs[len(after) :])
+
     return pl.pallas_call(
-        functools.partial(kernel, ids.shape[0]),
+        ordered,
         grid_spec=pltpu.PrefetchScalarGridSpec(
             num_scalar_prefetch=1,
             grid=(rows // tile,),
-            in_specs=[spec] * len(arrays) + [whole(item.shape) for item in gains],
+            in_specs=[pl.BlockSpec(memory_space=pl.ANY)] * len(after)
+            + [spec] * len(arrays)
+            + [whole(item.shape) for item in gains],
             out_specs=[spec] * len(out_types) + [whole((8, width))] * sums,
         ),
         out_shape=[jax.ShapeDtypeStruct((rows, width), kind) for kind in out_types]
         + [jax.ShapeDtypeStruct((8, width), F32)] * sums,
         compiler_params=params(),
-        cost_estimate=cost(0, rows * width) if brief else cost(10 * rows * width, moved),
-    )(ids, *arrays, *gains)
+        cost_estimate=cost(10 * rows * width, moved),
+    )(ids, *after, *arrays, *gains)
 
 
 def rotate(values, cosine, sine):
@@ -268,34 +298,17 @@
     return back.astype(LOW), jnp.sum((turned * unit).reshape(rows // 8, 8, width), axis=0)
 
 
-def opening_kernel(count, parts_in, ids, hidden, *refs):
+def opening_kernel(parts_in, inputs, *refs):
     weights, refs = refs[:parts_in], refs[parts_in:]
-    kgain, cosine, sine, normed, proj, qproj, out, out_weights = refs
-    width = hidden.shape[1] // count
-    each = count // parts_in
-    high = weights[0].shape[0] // each
+    kgain, cosine, sine, proj, qproj, out = refs
     dim = kgain.shape[1]
-    spots = [column(ids, step, width) for step in range(count)]
-
-    def part_of(step):
-        return weights[step // each], (step % each) * high
-
-    def body(rows):
-        parts = [hidden[rows, spot].astype(F32) for spot in spots]
-        scale = scale_of(parts)
-        for step in range(count):
-            source, at = part_of(step)
-            gain = source[at + width : at + width + 16, :width].astype(F32)[:1]
-            normed[rows, step * width : (step + 1) * width] = (parts[step] * scale * gain).astype(LOW)
-
-    by_rows(hidden.shape[0], body)
     kvcols, qcols = proj.shape[1], qproj.shape[1]
 
     def project(cols):
-        total = jnp.zeros((hidden.shape[0], cols.stop - cols.start), F32)
-        for step in range(count):
-            source, at = part_of(step)
-            total = total + dot_plain(normed[:, step * width : (step + 1) * width], source[at : at + width, cols])
+        total = jnp.zeros((inputs.shape[0], cols.stop - cols.start), F32)
+        for step, source in enumerate(weights):
+            deep = source.shape[0]
+            total = total + dot_plain(inputs[:, step * deep : (step + 1) * deep], source[:, cols])
         return total
 
     total = project(slice(0, kvcols))
@@ -305,13 +318,6 @@
         out[:, at : at + dim] = head_forward(total[:, at : at + dim], kgain[...], cosine[...], sine[...])[0]
         out[:, at + dim : at + 2 * dim] = total[:, at + dim : at + 2 * dim].astype(LOW)
     qproj[...] = project(slice(kvcols, kvcols + qcols))
-
-    @pl.when(pl.program_id(0) == 0)
-    def _():
-        for step in range(count):
-            source, at = part_of(step)
-            far = slice(kvcols + qcols, kvcols + qcols + out_weights.shape[1])
-            out_weights[step * width : (step + 1) * width, :] = source[at : at + width, far]
 
 
 def key_backward_kernel(mine, other, proj, gain, cosine, sine, out, norm_out):
@@ -351,7 +357,8 @@
         kv[place_at * rows : (place_at + 1) * rows, :] = piece[...]
 
 
-def attend_kernel(half, count, info, qproj, weights, *refs):
+def attend_kernel(half, count, parts_in, info, qproj, *refs):
+    weights, refs = refs[:parts_in], refs[parts_in:]
     pieces, (gain, cosine, sine, seg_row, seg_col), refs = refs[:count], refs[count : count + 5], refs[count + 5 :]
     out, out_wide, log_out, part_out, qs, acc, total, segq, kv, part_sum = refs
     load_pieces(pieces, kv)
@@ -391,13 +398,17 @@
             log_out[rows, cols] = logs[head * half : (head + 1) * half]
     here = pl.program_id(0)
 
-    @pl.when(here == 0)
-    def _():
-        part_sum[...] = dot_right_t(out[...], weights[...])
-
-    @pl.when(here > 0)
-    def _():
-        part_sum[...] += dot_right_t(out[...], weights[...])
+    for step, source in enumerate(weights):
+        cols = slice(step * source.shape[0], (step + 1) * source.shape[0])
+        term = dot_right_t(out[...], source[...])
+
+        @pl.when(here == 0)
+        def _():
+            part_sum[:, cols] = term
+
+        @pl.when(here > 0)
+        def _():
+            part_sum[:, cols] += term
 
     @pl.when(here == pl.num_programs(0) - 1)
     def _():
@@ -472,29 +483,31 @@
     stacked = half * (wide // dim)
     qspec, kspec = heads_spec(rows, wide), heads_spec(rows, 2 * dim)
     tables = (gain, cosine, sine, seg_row, seg_col)
+    width = sum(item.shape[0] for item in weights)
     return pl.pallas_call(
-        functools.partial(attend_kernel, half, count),
+        functools.partial(attend_kernel, half, count, len(weights)),
         grid_spec=pltpu.PrefetchScalarGridSpec(
             num_scalar_prefetch=1,
             grid=(heads,),
-            in_specs=[qspec, heads_spec(weights.shape[0], wide)]
+            in_specs=[qspec]
+            + [heads_spec(item.shape[0], wide) for item in weights]
             + [kspec] * count
             + [whole(item.shape) for item in tables],
-            out_specs=[qspec] * 3 + [whole((rows, weights.shape[0]))],
+            out_specs=[qspec] * 3 + [whole((rows, width))],
             scratch_shapes=[
                 pltpu.VMEM((2, stacked, dim), LOW),
                 pltpu.VMEM((2, stacked, dim), F32),
                 pltpu.VMEM((2, stacked, 128), F32),
                 pltpu.VMEM((2, stacked, 1), jnp.int32),
                 pltpu.VMEM((count * rows, 2 * dim), LOW),
-                pltpu.VMEM((rows, weights.shape[0]), F32),
+                pltpu.VMEM((rows, width), F32),
             ],
         ),
         out_shape=[jax.ShapeDtypeStruct((rows, qcols), kind) for kind in (LOW, F32, F32)]
-        + [jax.ShapeDtypeStruct((rows, weights.shape[0]), LOW)],
+        + [jax.ShapeDtypeStruct((rows, width), LOW)],
         compiler_params=params(),
         cost_estimate=cost(2 * rows * count * rows * qcols * 2, 8 * rows * qcols * 2),
-    )(info, qproj, weights, *pieces, *tables)
+    )(info, qproj, *weights, *pieces, *tables)
 
 
 def attend_back(info, qproj, wide_out, logs, grad, pieces, gain, cosine, sine, seg_row, seg_col):
@@ -537,53 +550,44 @@
     )(info, qproj, wide_out, logs, grad, *pieces, *tables)
 
 
-def assemble_kernel(dim, key, value, query, output, gains, out):
-    rows, kcols = key.shape
-    qcols = query.shape[1]
+def assemble_kernel(dim, key, value, query, out):
+    kcols = key.shape[1]
     for head in range(kcols // dim):
         spot = slice(head * dim, (head + 1) * dim)
-        out[:rows, 2 * head * dim : (2 * head + 1) * dim] = key[:, spot]
-        out[:rows, (2 * head + 1) * dim : (2 * head + 2) * dim] = value[:, spot]
-    out[:rows, 2 * kcols : 2 * kcols + qcols] = query[...]
-    out[:rows, 2 * kcols + qcols :] = output[...]
-    out[rows:, :] = jnp.zeros((16, out.shape[1]), LOW)
-    out[rows:, : gains.shape[1]] = gains[...]
-
-
-def assemble(key, value, query, output, gain_one, gain_two, dim):
-    gains = jnp.pad(jnp.concatenate([gain_one, gain_two])[None, :], ((0, 15), (0, 0)))
-    cols = 2 * key.shape[1] + query.shape[1] + output.shape[1]
+        out[:, 2 * head * dim : (2 * head + 1) * dim] = key[:, spot]
+        out[:, (2 * head + 1) * dim : (2 * head + 2) * dim] = value[:, spot]
+    out[:, 2 * kcols :] = query[...]
+
+
+def assemble(key, value, query, dim):
+    cols = 2 * key.shape[1] + query.shape[1]
     return pl.pallas_call(
         functools.partial(assemble_kernel, dim),
-        out_shape=jax.ShapeDtypeStruct((key.shape[0] + 16, cols), LOW),
+        out_shape=jax.ShapeDtypeStruct((key.shape[0], cols), LOW),
         compiler_params=params(),
         cost_estimate=cost(0, 4 * key.shape[0] * cols),
-    )(key, value, query, output, gains)
-
-
-def opening(ids, hidden, halves, kvcols, qcols, kgain, cosine, sine):
-    rows, width = hidden.shape
+    )(key, value, query)
+
+
+def opening(inputs, halves, kvcols, qcols, kgain, cosine, sine):
+    rows, width = inputs.shape
     tile = min(256, rows)
-    shapes = [(width, LOW), (kvcols, F32), (qcols, F32), (kvcols, LOW)]
+    shapes = [(kvcols, F32), (qcols, F32), (kvcols, LOW)]
 
     def tiled(cols):
-        return pl.BlockSpec((tile, cols), lambda step, *_: (step, 0))
+        return pl.BlockSpec((tile, cols), lambda step: (step, 0))
 
     return pl.pallas_call(
-        functools.partial(opening_kernel, ids.shape[0], len(halves)),
-        grid_spec=pltpu.PrefetchScalarGridSpec(
-            num_scalar_prefetch=1,
-            grid=(rows // tile,),
-            in_specs=[tiled(width)]
-            + [whole(item.shape) for item in halves]
-            + [whole(kgain.shape), tiled(cosine.shape[1]), tiled(sine.shape[1])],
-            out_specs=[tiled(cols) for cols, _ in shapes] + [whole((width, qcols))],
-        ),
-        out_shape=[jax.ShapeDtypeStruct((rows, cols), kind) for cols, kind in shapes]
-        + [jax.ShapeDtypeStruct((width, qcols), LOW)],
+        functools.partial(opening_kernel, len(halves)),
+        grid=(rows // tile,),
+        in_specs=[tiled(width)]
+        + [whole(item.shape) for item in halves]
+        + [whole(kgain.shape), tiled(cosine.shape[1]), tiled(sine.shape[1])],
+        out_specs=[tiled(cols) for cols, _ in shapes],
+        out_shape=[jax.ShapeDtypeStruct((rows, cols), kind) for cols, kind in shapes],
         compiler_params=params(),
         cost_estimate=cost(2 * rows * width * (kvcols + qcols), 4 * rows * width + 2 * width * kvcols),
-    )(ids, hidden, *halves, kgain, cosine, sine)
+    )(inputs, *halves, kgain, cosine, sine)
 
 
 def key_backward(mine, other, proj, gain, cosine, sine):
@@ -680,27 +684,10 @@
 
     blocks = staged_blocks() if is_staged else jnp.zeros((1,), jnp.int32)
     count = blocks.shape[0]
-    near = 2 * kcols + qcols
-    first_shard = assemble(key_weight, value_weight, query_weight, output_weight, attn_gain, ffn_gain, head_dim)
-    halves = staged_halves(first_shard) if is_staged else [gather_rows(first_shard)]
-
-    def without_gains():
-        parts = [half.reshape(-1, shard_rows + 16, half.shape[1])[:, :shard_rows] for half in halves]
-        return jnp.concatenate([part.reshape(-1, part.shape[2]) for part in parts])
-
-    gain_rows = [half.reshape(-1, shard_rows + 16, half.shape[1])[:, shard_rows] for half in halves]
-    gain_rows = jnp.concatenate(gain_rows).astype(F32)
-    gain_one = gain_rows[:, :shard_rows].reshape(count, -1)
-    gain_two = gain_rows[:, shard_rows : 2 * shard_rows].reshape(count, -1)
-    opening_halves = halves
-    if not is_staged:
-        gain_tail = jnp.pad(gain_one.astype(LOW), ((0, 15), (0, 0)))
-        far = max(first_shard.shape[1], width)
-        opening_halves = [
-            jnp.concatenate(
-                [jnp.pad(item, ((0, 0), (0, far - item.shape[1]))) for item in (without_gains(), gain_tail)]
-            )
-        ]
+    near_shard = assemble(key_weight, value_weight, query_weight, head_dim)
+    gains = gather_fast(jnp.stack([attn_gain, ffn_gain])).reshape(-1, 2, shard_rows).astype(F32)
+    gain_one = gains[:, 0].reshape(count, -1)
+    gain_two = gains[:, 1].reshape(count, -1)
 
     me = lax.axis_index("context")
     last = 2 * pieces - 1
@@ -728,23 +715,43 @@
     kgain = knorm_gain.astype(F32)[None, :]
 
     (cot_staged,) = row_call(stage_kernel, blocks, [cotangent], [LOW])
-    inputs_one, kv_proj, query_proj, kv_own, out_full = opening(
-        blocks, hidden_in, opening_halves, 2 * kcols, qcols, kgain, cosine, sine
-    )
+    out_blocks = staged_blocks("y") if is_staged else blocks
+    if is_staged:
+        match = (out_blocks[:, None] == blocks[None, :]).astype(F32)
+        gain_two = jnp.dot(match, gain_two, precision=lax.Precision.HIGHEST)
+    if is_staged:
+        near_pair = staged_pair(near_shard)
+        near_far = staged(near_pair, "yx")
+        near_far, gain_one, gain_two, blocks, info, seg_col, cosine, sine = tie(
+            near_far, gain_one, gain_two, blocks, info, seg_col, cosine, sine
+        )
+        near_last, out_shard = tie(staged(near_far, "core"), output_weight)
+        near_halves = [near_pair, near_far, staged(near_pair, "core"), near_last]
+        out_pair = staged_pair(out_shard, "y")
+    else:
+        near_halves = [gather_rows(near_shard)]
+    (inputs_one,) = row_call(first_norm_kernel, blocks, [hidden_in], [LOW], gain_one)
+    kv_proj, query_proj, kv_own = opening(inputs_one, near_halves, 2 * kcols, qcols, kgain, cosine, sine)
+    if is_staged:
+        out_pair, kv_own = tie(out_pair, kv_own)
+        out_halves = staged_halves(staged_quad(out_pair, "y"))
+    else:
+        out_halves = [gather_rows(output_weight)]
     kv_across = swap_context(kv_own, 2)
     kv_pieces = [kv_own, swap_context(kv_own, 1), kv_across, swap_context(kv_across, 1)]
     gate_up_shard, kv_proj = tie(jnp.concatenate([gate_weight, up_weight], axis=1), kv_proj)
     gate_up = gather_rows(gate_up_shard)
     attended, attended_wide, logs, attn_part = attend(
-        info, query_proj, out_full, kv_pieces, qgain, cosine, sine, segments, seg_col
+        info, query_proj, out_halves, kv_pieces, qgain, cosine, sine, segments, seg_col
     )
     down_shard, logs = tie(down_weight, logs)
     down_full = gather_fast(down_shard)
     attn_out = sum_tensor(attn_part)
     dproduct = dot_plain(cot_staged, down_full)
-    near_full = without_gains()[:, :near]
-    attn_out, dproduct, near_full = tie(attn_out, dproduct, near_full)
-    middle, inputs_two = row_call(second_norm_kernel, blocks, [hidden_in, attn_out], [F32, LOW], gain_two)
+    near_full = jnp.concatenate(near_halves)
+    out_full = jnp.concatenate(out_halves)
+    attn_out, dproduct, near_full, out_full = tie(attn_out, dproduct, near_full, out_full)
+    middle, inputs_two = row_call(second_norm_kernel, out_blocks, [hidden_in, attn_out], [F32, LOW], gain_two)
     product, dgate, dup_low, dnormed_two_part = feed(inputs_two, gate_up, dproduct)
     dnormed_two = sum_tensor(dnormed_two_part)
 
@@ -755,7 +762,7 @@
     dnormed_two, ffn_part, grad_gate, grad_up = tie(dnormed_two, ffn_part, grad_gate, grad_up)
     ffn_out = sum_tensor(ffn_part)
     dmiddle, dattn, gain_two_sums = row_call(
-        second_back_kernel, blocks, [dnormed_two, middle, cotangent], [F32, LOW], gain_two, True, True
+        second_back_kernel, out_blocks, [dnormed_two, middle, cotangent], [F32, LOW], gain_two, True
     )
     gain_two_part = jnp.sum(gain_two_sums, axis=0) / lax.axis_size("tensor")
     dattended = dot_plain(dattn, out_full).astype(LOW)
@@ -768,7 +775,8 @@
     dkv, knorm_parts = key_backward(
         dkv_pair[:local_rows], swap_context(dkv_pair[local_rows:], 2), kv_proj, kgain, cosine, sine
     )
-    output_own = scatter_fast(dot_left_t(dattn, attended).astype(LOW))
+    grad_output = dot_left_t(dattn, attended).astype(LOW)
+    output_own = staged_scatter(grad_output, "y") if is_staged else scatter_rows(grad_output)
     dqkv = jnp.concatenate([dkv, dquery], axis=1)
     dnormed_one_part = dot_right_t(dqkv, near_full).astype(LOW)
     later_part, ffn_out = tie(dnormed_one_part, ffn_out)
@@ -794,32 +802,29 @@
     gain_two_grad = lax.dynamic_slice_in_dim(small[width : 2 * width], start, own)
     qnorm_total = small[2 * width : 2 * width + head_dim]
     knorm_total = small[2 * width + head_dim :]
+    qkv_own = qkv_own.astype(F32)
     query_grad = qkv_own[:, 2 * kcols :]
     key_grad, value_grad = unmixed(qkv_own, 0), unmixed(qkv_own, 1)
+    output_own = output_own.astype(F32)
     gate_own = gate_own.astype(F32)
     down_own = down_own.astype(F32)
-    up_own = up_own.astype(F32)
-    (
-        dnormed_one, output, gain_one_grad, query_grad, key_grad, value_grad, output_own,
-        qnorm_total, knorm_total, gain_two_grad, gate_own, down_own,
-    ) = tie(
-        dnormed_one, output, gain_one_grad, query_grad, key_grad, value_grad, output_own,
-        qnorm_total, knorm_total, gain_two_grad, gate_own, down_own,
-    )
-    (input_grad,) = row_call(first_back_kernel, blocks, [dnormed_one, hidden_in, dmiddle], [F32], gain_one)
+    done = [output, small, query_grad, key_grad, value_grad, output_own, gate_own, down_own]
+    (input_grad,) = row_call(
+        first_back_kernel, blocks, [dnormed_one, hidden_in, dmiddle], [F32], gain_one, after=done
+    )
     return (
         output,
         input_grad,
         gain_one_grad,
-        query_grad.astype(F32),
-        key_grad.astype(F32),
-        value_grad.astype(F32),
-        output_own.astype(F32),
+        query_grad,
+        key_grad,
+        value_grad,
+        output_own,
         qnorm_total,
         knorm_total,
         gain_two_grad,
         gate_own,
-        up_own,
+        up_own.astype(F32),
         down_own,
     )
 

time: 503 us -> 491 us (0.976)
  waiting for transfers between devices: 258 us -> 232 us
  starting transfers between devices: 23.6 us -> 35.5 us
    psum x4, waiting for transfers between devices: 112 us -> 97.7 us  [sum_tensor(): return lax.psum(partial.astype(LOW), 'tensor')]
    ppermute x5, waiting for transfers between devices: 27.6 us -> 17.4 us  [swap_context(): lax.ppermute(values, 'context', [(index, index ^ bit) for index in range(...]
    ppermute x5, starting transfers between devices: 6.47 us -> 16.1 us  [sum_all(): lax.ppermute(values, axis, [(index, index ^ bit) for index in range(size)])]
    pallas_call x7 -> x8, Pallas kernels: 56.4 us -> 51.9 us  [the longest x6 33.1 us: row_call(): pl.pallas_call(ordered, grid_spec=pltpu.PrefetchScalarGridSpec(num_scalar...]
    ppermute x12 -> x19, starting transfers between devices: 12.1 us -> 16.2 us  [staged(): return lax.ppermute(values, ROWS, staged_pairs(step))]
    ppermute x12 -> x19, waiting for transfers between devices: 112 us -> 114 us  [staged(): return lax.ppermute(values, ROWS, staged_pairs(step))]
    unnamed x75 -> x84, local copies, waits for them, and re-layouts: 17.1 us -> 17.4 us
  transfers between devices with their start and end apart: 30 -> 37, of which waited for: 20 -> 23; matrix products, arithmetic and copies ran while one was open for 17% -> 18% of each run, Pallas kernels for 11% -> 12%
where the time goes in v3:
time: 491 us; the launch traced here: 484 us
  waiting for transfers between devices  232 us (47%)
  Pallas kernels  94.7 us (19%)
  matrix products  47.9 us (10%)
  starting transfers between devices  35.5 us (7%)
  local copies, waits for them, and re-layouts  29.4 us (6%)
  other arithmetic  26.7 us (5%)
  between operations  16.6 us (3%)
    ppermute x19, waiting for transfers between devices, staged(): return lax.ppermute(values, ROWS, staged_pairs(step))  114 us
    psum x4, waiting for transfers between devices, sum_tensor(): return lax.psum(partial.astype(LOW), 'tensor')  97.7 us
    pallas_call x6, Pallas kernels, row_call(): pl.pallas_call(ordered, grid_spec=pltpu.PrefetchScalarGridSpec(num_scalar...  33.1 us
    dot_general x5, matrix products, dot_left_t(): lax.dot_general(matrix_a, matrix_b, (((0,), (0,)), ((), ())), preferred_e...  24.3 us
    pallas_call x1, Pallas kernels, feed(): pl.pallas_call(feed_kernel, grid=(count,), in_specs=[whole((rows, width))...  22.2 us
    unnamed x84, local copies, waits for them, and re-layouts  17.4 us
    ppermute x5, waiting for transfers between devices, swap_context(): lax.ppermute(values, 'context', [(index, index ^ bit) for index in range(...  17.4 us
    ppermute x19, starting transfers between devices, staged(): return lax.ppermute(values, ROWS, staged_pairs(step))  16.2 us
  transfers between devices with their start and end apart: 37, of which 23 were waited for; matrix products, arithmetic and copies ran while one was open for 18% of the time, Pallas kernels for 12%

profile of v3, /device:TPU:0, one launch (start us, length us, event | category | flops | bytes accessed | tf_op | source)
XLA Modules:
  0.0 483.5 jit_solution(4531419070815805367)
XLA Ops:
  17.1 6.6 %collective-permute-done = bf16[256,1024]{1,0:T(8,128)(2,1)S(1)} collective-permute-done((bf16[256,1024]{1,0:T(8,128)(2,1)}, bf16[256,1024]{1,0:T(8,128)(2,1)S(1)}, u32[]{:S(2)}, u32[]{:S(2)}) %collective-permute-start) | collective-permute-done | bytes 524320 | tf_op jit(solution)/shard_map/ppermute | solution.py:74
  27.6 12.2 %collective-permute-done.3 = bf16[4,256]{1,0:T(4,128)(2,1)S(1)} collective-permute-done((bf16[4,256]{1,0:T(4,128)(2,1)S(1)}, bf16[4,256]{1,0:T(4,128)(2,1)S(1)}, u32[]{:S(2)}, u32[]{:S(2)}) %collective-permute-start.3) | collective-permute-done | bytes 2080 | tf_op jit(solution)/shard_map/ppermute | solution.py:74
  52.5 6.1 %shard_map.239 = (f32[512,512]{1,0:T(8,128)}, f32[512,512]{1,0:T(8,128)}, bf16[512,512]{1,0:T(8,128)(2,1)}) custom-call(bf16[512,2048]{1,0:T(8,128)(2,1)} %shard_map.238.inputs, bf16[512,1024]{1,0:T(8,128)(2,1)} %pad_maximum_fusion.4.refs_0_, bf16[512,1024]{1,0:T(8,128)(2,1)} %copy-done.8, bf16[512,1024]{1,0:T(8,128)(2,1)} %copy-done.12, ...), custom_call_target="tpu_custom_call" | custom-call | flops 2147483648 | bytes 6291456 | tf_op jit(solution)/shard_map/pallas_call | solution.py:580
  60.2 12.2 %collective-permute-done.8 = bf16[512,512]{1,0:T(8,128)(2,1)S(1)} collective-permute-done((bf16[512,512]{1,0:T(8,128)(2,1)S(1)}, bf16[512,512]{1,0:T(8,128)(2,1)S(1)}, u32[]{:S(2)}, u32[]{:S(2)}) %collective-permute-start.8) | collective-permute-done | bytes 524320 | tf_op jit(solution)/shard_map/ppermute | solution.py:74
  77.7 12.7 %shard_map.240 = (bf16[512,512]{1,0:T(8,128)(2,1)}, f32[512,512]{1,0:T(8,128)}, f32[512,512]{1,0:T(8,128)}, bf16[512,2048]{1,0:T(8,128)(2,1)}) custom-call(s32[10]{0:T(128)} %stack.115.info, f32[512,512]{1,0:T(8,128)} %get-tuple-element.74.qproj, bf16[1024,512]{1,0:T(8,128)(2,1)} %constant_dynamic-update-slice_fusion.refs_0_, ...), custom_call_target="tpu_custom_call" | custom-call | flops 2147483648 | bytes 4194304 | tf_op jit(solution)/shard_map/pallas_call | solution.py:487
  94.1 14.5 %collective-permute-done.13 = bf16[256,1536]{1,0:T(8,128)(2,1)S(1)} collective-permute-done((bf16[256,1536]{1,0:T(8,128)(2,1)S(1)}, bf16[256,1536]{1,0:T(8,128)(2,1)S(1)}, u32[]{:S(2)}, u32[]{:S(2)}) %collective-permute-start.13) | collective-permute-done | bytes 786464 | tf_op jit(solution)/shard_map/ppermute | solution.py:74
  108.8 33.3 %collective-permute-done.14 = bf16[512,1536]{1,0:T(8,128)(2,1)S(1)} collective-permute-done((bf16[512,1536]{1,0:T(8,128)(2,1)S(1)}, bf16[512,1536]{1,0:T(8,128)(2,1)S(1)}, u32[]{:S(2)}, u32[]{:S(2)}) %collective-permute-start.14) | collective-permute-done | bytes 1572896 | tf_op jit(solution)/shard_map/ppermute | solution.py:74
  167.8 8.8 %all-reduce.5.cloned.1.call-done.refs_1_ = bf16[512,2048]{1,0:T(8,128)(2,1)} async-done(((bf16[512,2048]{1,0:T(8,128)(2,1)}), bf16[512,2048]{1,0:T(8,128)(2,1)}) %all-reduce.5.cloned.1.call-update) | async-done | bytes 2097168 | tf_op jit(solution)/shard_map/psum | solution.py:48
  182.3 22.2 %shard_map.243 = (bf16[512,1536]{1,0:T(8,128)(2,1)}, bf16[512,1536]{1,0:T(8,128)(2,1)}, bf16[512,1536]{1,0:T(8,128)(2,1)}, bf16[512,2048]{1,0:T(8,128)(2,1)}) custom-call(bf16[512,2048]{1,0:T(8,128)(2,1)} %get-tuple-element.86.inputs, bf16[2048,3072]{1,0:T(8,128)(2,1)} %all-gather.2.cloned.1.call-done.gate.up, ...), custom_call_target="tpu_custom_call" | custom-call | flops 12884901888 | bytes 20447232 | tf_op jit(solution)/shard_map/pallas_call | solution.py:640
  206.1 6.7 %fusion = bf16[2048,1536]{1,0:T(8,128)(2,1)} fusion(bf16[512,1536]{1,0:T(8,128)(2,1)} %get-tuple-element.91, bf16[512,2048]{1,0:T(8,128)(2,1)S(1)} %copy-done), kind=kOutput, calls=%fused_computation.3 | convolution fusion | flops 3224371200 | bytes 9961472 | tf_op jit(solution)/shard_map/dot_general | solution.py:28
  214.5 6.8 %convolution_convert_fusion.2 = bf16[2048,1536]{1,0:T(8,128)(2,1)} fusion(bf16[512,2048]{1,0:T(8,128)(2,1)S(1)} %copy-done.32, bf16[512,1536]{1,0:T(8,128)(2,1)} %get-tuple-element.92), kind=kOutput, calls=%fused_computation.2 | convolution fusion | flops 3224371200 | bytes 9961472 | tf_op jit(solution)/shard_map/dot_general | solution.py:28
  221.3 7.0 %convolution_convert_fusion.1 = bf16[2048,1536]{1,0:T(8,128)(2,1)} fusion(bf16[512,2048]{1,0:T(8,128)(2,1)S(1)} %copy-done.32, bf16[512,1536]{1,0:T(8,128)(2,1)} %get-tuple-element.93), kind=kOutput, calls=%fused_computation.1 | convolution fusion | flops 3224371200 | bytes 9961472 | tf_op jit(solution)/shard_map/dot_general | solution.py:28
  228.3 8.2 %convolution_convert_fusion.6 = bf16[512,2048]{1,0:T(8,128)(2,1)} fusion(bf16[512,1536]{1,0:T(8,128)(2,1)} %get-tuple-element.91, bf16[2048,1536]{1,0:T(8,128)(2,1)} %copy-done.22), kind=kOutput, calls=%fused_computation.10 | convolution fusion | flops 3222274048 | bytes 9961472 | tf_op jit(solution)/shard_map/dot_general | solution.py:24
  236.5 53.7 %all-reduce.7.cloned.1.call-done.refs_0_ = bf16[512,2048]{1,0:T(8,128)(2,1)} async-done(((bf16[512,2048]{1,0:T(8,128)(2,1)}), bf16[512,2048]{1,0:T(8,128)(2,1)}) %all-reduce.7.cloned.1.call-update) | async-done | bytes 2097168 | tf_op jit(solution)/shard_map/psum | solution.py:48
  290.5 8.1 %shard_map.244 = (f32[512,2048]{1,0:T(8,128)}, bf16[512,2048]{1,0:T(8,128)(2,1)}, f32[8,2048]{1,0:T(8,128)}) custom-call(s32[8]{0:T(128)} %copy-done.28, bf16[512,2048]{1,0:T(8,128)(2,1)} %all-reduce.7.cloned.1.call-done.refs_0_, f32[512,2048]{1,0:T(8,128)} %get-tuple-element.85.refs_1_.refs_0_, bf16[512,2048]{1,0:T(8,128)(2,1)} %refs_2_.1, ...), custom_call_target="tpu_custom_call" | custom-call | flops 10485760 | bytes 14680064 | tf_op jit(solution)/shard_map/pallas_call | solution.py:266
  302.2 15.4 %shard_map.245 = (bf16[512,512]{1,0:T(8,128)(2,1)}, bf16[1024,512]{1,0:T(8,128)(2,1)}, bf16[1024,512]{1,0:T(8,128)(2,1)}, f32[2,8,128]{2,1,0:T(8,128)}) custom-call(s32[10]{0:T(128)} %stack.115.info, f32[512,512]{1,0:T(8,128)} %get-tuple-element.74.qproj, f32[512,512]{1,0:T(8,128)} %get-tuple-element.96.wide, f32[512,512]{1,0:T(8,128)} %get-tuple-element.97.logs, ...), custom_call_target="tpu_custom_call" | custom-call | bytes 262144 | tf_op jit(solution)/shard_map/pallas_call | solution.py:524
  324.2 12.5 %collective-permute-done.17.other = bf16[512,512]{1,0:T(8,128)(2,1)S(1)} collective-permute-done((bf16[512,512]{1,0:T(8,128)(2,1)S(1)}, bf16[512,512]{1,0:T(8,128)(2,1)S(1)}, u32[]{:S(2)}, u32[]{:S(2)}) %collective-permute-start.17) | collective-permute-done | bytes 524320 | tf_op jit(solution)/shard_map/ppermute | solution.py:131
  342.1 5.9 %multiply_reduce_fusion = (f32[2048]{0:T(1024)S(1)}, bf16[512,2048]{1,0:T(8,128)(2,1)}) fusion(bf16[512,2048]{1,0:T(8,128)(2,1)S(1)} %copy-done.4, bf16[512,1024]{1,0:T(8,128)(2,1)S(1)} %constant_dynamic-update-slice_fusion.11, bf16[2048,1024]{1,0:T(8,128)(2,1)} %copy-done.24), kind=kOutput, calls=%fused_computation.5 | convolution fusion | flops 2152724480 | bytes 9445376 | tf_op jit(solution)/shard_map/dot_general | solution.py:24
  348.1 29.9 %all-reduce.9.cloned.1.call-done.refs_1_ = bf16[512,2048]{1,0:T(8,128)(2,1)} async-done(((bf16[512,2048]{1,0:T(8,128)(2,1)}), bf16[512,2048]{1,0:T(8,128)(2,1)}) %all-reduce.9.cloned.1.call-update) | async-done | bytes 2097168 | tf_op jit(solution)/shard_map/psum | solution.py:48
  391.9 13.5 %collective-permute-done.27 = bf16[512,512]{1,0:T(8,128)(2,1)} collective-permute-done((bf16[512,512]{1,0:T(8,128)(2,1)}, bf16[512,512]{1,0:T(8,128)(2,1)}, u32[]{:S(2)}, u32[]{:S(2)}) %collective-permute-start.27) | collective-permute-done | bytes 524320 | tf_op jit(solution)/shard_map/ppermute | solution.py:74
  411.7 7.2 %collective-permute-done.28 = bf16[256,512]{1,0:T(8,128)(2,1)} collective-permute-done((bf16[256,512]{1,0:T(8,128)(2,1)S(1)}, bf16[256,512]{1,0:T(8,128)(2,1)}, u32[]{:S(2)}, u32[]{:S(2)}) %collective-permute-start.28) | collective-permute-done | bytes 262176 | tf_op jit(solution)/shard_map/ppermute | solution.py:74
  422.9 10.3 %collective-permute-done.25 = bf16[256,1024]{1,0:T(8,128)(2,1)S(1)} collective-permute-done((bf16[256,1024]{1,0:T(8,128)(2,1)S(1)}, bf16[256,1024]{1,0:T(8,128)(2,1)S(1)}, u32[]{:S(2)}, u32[]{:S(2)}) %collective-permute-start.25) | collective-permute-done | bytes 524320 | tf_op jit(solution)/shard_map/ppermute | solution.py:74
  433.4 10.4 %collective-permute-start.20 = (f32[4352]{0:T(1024)S(1)}, f32[4352]{0:T(1024)S(1)}, u32[]{:S(2)}, u32[]{:S(2)}) collective-permute-start(f32[4352]{0:T(1024)S(1)} %add.211), channel_id=1, source_target_pairs={{0,4},{4,0},{8,12},{12,8},{1,5},{5,1},{9,13},{13,9},{2,6},{6,2},{1... | collective-permute-start | bytes 52232 | tf_op jit(solution)/shard_map/ppermute | solution.py:124
  466.5 6.8 %shard_map.248 = f32[512,2048]{1,0:T(8,128)} custom-call(s32[8]{0:T(128)} %copy-done.25, bf16[512,2048]{1,0:T(8,128)(2,1)} %shard_map.247.refs_0_, f32[4352]{0:T(1024)} %copy-done.21, f32[256,512]{1,0:T(8,128)} %slice.111.refs_2_, f32[256,256]{1,0:T(8,128)} %pad_maximum_fusion.8.refs_3_, f32[256,256]{1,0:T(8,128)} %pad_maximum_fusion.9.refs_4_, ...), custom_call_target="tpu_custom_call" | custom-call | flops 10485760 | bytes 12582912 | tf_op jit(solution)/shard_map/pallas_call | solution.py:266
  (234 shorter events, 135.8 us)
Async XLA Ops:
  8.0 168.6 %all-reduce.5.cloned.1.call-start = ((), (), s32[]{:S(2)}) async-start(), calls=%async_computation.3 | async-start | bytes 4194304 | tf_op jit(solution)/shard_map/psum | solution.py:48
  9.4 17.6 %collective-permute-start.2 = (bf16[2,256]{1,0:T(2,128)(2,1)S(1)}, bf16[2,256]{1,0:T(2,128)(2,1)S(1)}, u32[]{:S(2)}, u32[]{:S(2)}) collective-permute-start(bf16[2,256]{1,0:T(2,128)(2,1)S(1)} %pad_maximum_fusion.13), channel_id=1, source_target_pairs={{0,16},{4,12},{8,24},{12,4},{16,0},{20,28},{24,8},{28,20},{1,17},{... | collective-permute-start | bytes 3080 | tf_op jit(solution)/shard_map/ppermute | solution.py:74
  24.8 17.7 %collective-permute-start.1 = (bf16[512,1024]{1,0:T(8,128)(2,1)}, bf16[512,1024]{1,0:T(8,128)(2,1)S(1)}, u32[]{:S(2)}, u32[]{:S(2)}) collective-permute-start(bf16[512,1024]{1,0:T(8,128)(2,1)} %pad_maximum_fusion.4.refs_0_), channel_id=1, source_target_pairs={{0,8},{4,20},{8,0},{12,28},{16,24},{20,4},{24,16},{28,12},{1,9},{5... | collective-permute-start | bytes 3145736 | tf_op jit(solution)/shard_map/ppermute | solution.py:74
  27.0 12.8 %collective-permute-start.3 = (bf16[4,256]{1,0:T(4,128)(2,1)S(1)}, bf16[4,256]{1,0:T(4,128)(2,1)S(1)}, u32[]{:S(2)}, u32[]{:S(2)}) collective-permute-start(bf16[4,256]{1,0:T(4,128)(2,1)S(1)} %pad_maximum_fusion.12), channel_id=1, source_target_pairs={{0,8},{4,20},{8,0},{12,28},{16,24},{20,4},{24,16},{28,12},{1,9},{5... | collective-permute-start | bytes 6152 | tf_op jit(solution)/shard_map/ppermute | solution.py:74
  45.2 13.5 %collective-permute-start.7 = (bf16[256,512]{1,0:T(8,128)(2,1)S(1)}, bf16[256,512]{1,0:T(8,128)(2,1)S(1)}, u32[]{:S(2)}, u32[]{:S(2)}) collective-permute-start(bf16[256,512]{1,0:T(8,128)(2,1)S(1)} %copy-done.20), channel_id=1, source_target_pairs={{0,8},{4,12},{8,0},{12,4},{16,24},{20,28},{24,16},{28,20},{1,9},{5... | collective-permute-start | bytes 786440 | tf_op jit(solution)/shard_map/ppermute | solution.py:74
  58.7 13.8 %collective-permute-start.8 = (bf16[512,512]{1,0:T(8,128)(2,1)S(1)}, bf16[512,512]{1,0:T(8,128)(2,1)S(1)}, u32[]{:S(2)}, u32[]{:S(2)}) collective-permute-start(bf16[512,512]{1,0:T(8,128)(2,1)S(1)} %pad_maximum_fusion.5), channel_id=1, source_target_pairs={{0,16},{4,20},{8,24},{12,28},{16,0},{20,4},{24,8},{28,12},{1,17},{... | collective-permute-start | bytes 1572872 | tf_op jit(solution)/shard_map/ppermute | solution.py:74
  59.3 14.5 %collective-permute-start.11 = (bf16[512,512]{1,0:T(8,128)(2,1)}, bf16[512,512]{1,0:T(8,128)(2,1)S(1)}, u32[]{:S(2)}, u32[]{:S(2)}) collective-permute-start(bf16[512,512]{1,0:T(8,128)(2,1)} %get-tuple-element.78.refs_2_.refs_0_), channel_id=1, source_target_pairs={{0,8},{4,12},{8,0},{12,4},{1,9},{5,13},{9,1},{13,5},{2,10},{6,14},... | collective-permute-start | bytes 1572872 | tf_op jit(solution)/shard_map/ppermute | solution.py:131
  90.5 91.8 %all-gather.2.cloned.1.call-start = ((), (), s32[]{:S(2)}) async-start(), calls=%async_computation.4 | async-start | bytes 14155776 | tf_op jit(solution)/shard_map/all_gather | solution.py:40
  93.3 196.9 %all-reduce.7.cloned.1.call-start = ((), (), s32[]{:S(2)}) async-start(), calls=%async_computation.5 | async-start | bytes 4194304 | tf_op jit(solution)/shard_map/psum | solution.py:48
  93.5 15.1 %collective-permute-start.13 = (bf16[256,1536]{1,0:T(8,128)(2,1)S(1)}, bf16[256,1536]{1,0:T(8,128)(2,1)S(1)}, u32[]{:S(2)}, u32[]{:S(2)}) collective-permute-start(bf16[256,1536]{1,0:T(8,128)(2,1)S(1)} %copy-done.1), channel_id=1, source_target_pairs={{0,16},{4,12},{8,24},{12,4},{16,0},{20,28},{24,8},{28,20},{1,17},{... | collective-permute-start | bytes 2359304 | tf_op jit(solution)/shard_map/ppermute | solution.py:74
  108.8 33.3 %collective-permute-start.14 = (bf16[512,1536]{1,0:T(8,128)(2,1)S(1)}, bf16[512,1536]{1,0:T(8,128)(2,1)S(1)}, u32[]{:S(2)}, u32[]{:S(2)}) collective-permute-start(bf16[512,1536]{1,0:T(8,128)(2,1)S(1)} %pad_maximum_fusion.2), channel_id=1, source_target_pairs={{0,8},{4,20},{8,0},{12,28},{16,24},{20,4},{24,16},{28,12},{1,9},{5... | collective-permute-start | bytes 4718600 | tf_op jit(solution)/shard_map/ppermute | solution.py:74
  144.0 13.9 %collective-permute-start.15 = (bf16[1024,1536]{1,0:T(8,128)(2,1)}, bf16[1024,1536]{1,0:T(8,128)(2,1)}, u32[]{:S(2)}, u32[]{:S(2)}) collective-permute-start(bf16[1024,1536]{1,0:T(8,128)(2,1)} %pad_maximum_fusion), channel_id=1, source_target_pairs={{0,4},{4,0},{8,12},{12,8},{16,20},{20,16},{24,28},{28,24},{1,5},{5... | collective-permute-start | bytes 9437192 | tf_op jit(solution)/shard_map/ppermute | solution.py:74
  204.6 113.0 %reduce-scatter.4.cloned.1.call-start = ((), (), s32[]{:S(2)}) async-start(), calls=%async_computation.6 | async-start | bytes 7077888 | tf_op jit(solution)/shard_map/reduce_scatter | solution.py:44
  212.9 165.1 %all-reduce.9.cloned.1.call-start = ((), (), s32[]{:S(2)}) async-start(), calls=%async_computation.8 | async-start | bytes 4194304 | tf_op jit(solution)/shard_map/psum | solution.py:48
  290.2 88.3 %reduce-scatter.6.cloned.1.call-start = ((), (), s32[]{:S(2)}) async-start(), calls=%async_computation.7 | async-start | bytes 7077888 | tf_op jit(solution)/shard_map/reduce_scatter | solution.py:44
  317.6 148.8 %all-reduce.11.cloned.1.call-start = ((), (), s32[]{:S(2)}) async-start(), calls=%async_computation.9 | async-start | bytes 4194304 | tf_op jit(solution)/shard_map/psum | solution.py:48
  322.7 14.0 %collective-permute-start.17 = (bf16[512,512]{1,0:T(8,128)(2,1)S(1)}, bf16[512,512]{1,0:T(8,128)(2,1)S(1)}, u32[]{:S(2)}, u32[]{:S(2)}) collective-permute-start(bf16[512,512]{1,0:T(8,128)(2,1)S(1)} %get-tuple-element.125), channel_id=1, source_target_pairs={{0,8},{4,12},{8,0},{12,4},{1,9},{5,13},{9,1},{13,5},{2,10},{6,14},... | collective-permute-start | bytes 1572872 | tf_op jit(solution)/shard_map/ppermute | solution.py:131
  378.0 95.2 %reduce-scatter.8.cloned.1.call-start = ((), (), s32[]{:S(2)}) async-start(), calls=%async_computation.10 | async-start | bytes 7077888 | tf_op jit(solution)/shard_map/reduce_scatter | solution.py:44
  387.6 20.0 %collective-permute-start.24 = (bf16[512,1024]{1,0:T(8,128)(2,1)}, bf16[512,1024]{1,0:T(8,128)(2,1)}, u32[]{:S(2)}, u32[]{:S(2)}) collective-permute-start(bf16[512,1024]{1,0:T(8,128)(2,1)} %slice.108), channel_id=1, source_target_pairs={{0,8},{4,20},{8,0},{12,28},{16,24},{20,4},{24,16},{28,12},{1,9},{5... | collective-permute-start | bytes 3145736 | tf_op jit(solution)/shard_map/ppermute | solution.py:74
  390.2 15.2 %collective-permute-start.27 = (bf16[512,512]{1,0:T(8,128)(2,1)}, bf16[512,512]{1,0:T(8,128)(2,1)}, u32[]{:S(2)}, u32[]{:S(2)}) collective-permute-start(bf16[512,512]{1,0:T(8,128)(2,1)} %slice.119), channel_id=1, source_target_pairs={{0,16},{4,20},{8,24},{12,28},{16,0},{20,4},{24,8},{28,12},{1,17},{... | collective-permute-start | bytes 1572872 | tf_op jit(solution)/shard_map/ppermute | solution.py:74
  406.8 12.1 %collective-permute-start.28 = (bf16[256,512]{1,0:T(8,128)(2,1)S(1)}, bf16[256,512]{1,0:T(8,128)(2,1)}, u32[]{:S(2)}, u32[]{:S(2)}) collective-permute-start(bf16[256,512]{1,0:T(8,128)(2,1)S(1)} %slice.121), channel_id=1, source_target_pairs={{0,8},{4,12},{8,0},{12,4},{16,24},{20,28},{24,16},{28,20},{1,9},{5... | collective-permute-start | bytes 786440 | tf_op jit(solution)/shard_map/ppermute | solution.py:74
  409.2 24.0 %collective-permute-start.25 = (bf16[256,1024]{1,0:T(8,128)(2,1)S(1)}, bf16[256,1024]{1,0:T(8,128)(2,1)S(1)}, u32[]{:S(2)}, u32[]{:S(2)}) collective-permute-start(bf16[256,1024]{1,0:T(8,128)(2,1)S(1)} %slice.110), channel_id=1, source_target_pairs={{0,16},{4,12},{8,24},{12,4},{16,0},{20,28},{24,8},{28,20},{1,17},{... | collective-permute-start | bytes 1572872 | tf_op jit(solution)/shard_map/ppermute | solution.py:74
  420.8 12.5 %collective-permute-start.19 = (f32[4352]{0:T(1024)S(1)}, f32[4352]{0:T(1024)S(1)}, u32[]{:S(2)}, u32[]{:S(2)}) collective-permute-start(f32[4352]{0:T(1024)S(1)} %fusion.10), channel_id=1, source_target_pairs={{0,2},{1,3},{2,0},{3,1},{4,6},{5,7},{6,4},{7,5},{8,10},{9,11},{10,... | collective-permute-start | bytes 52232 | tf_op jit(solution)/shard_map/ppermute | solution.py:124
  433.4 11.3 %collective-permute-start.20 = (f32[4352]{0:T(1024)S(1)}, f32[4352]{0:T(1024)S(1)}, u32[]{:S(2)}, u32[]{:S(2)}) collective-permute-start(f32[4352]{0:T(1024)S(1)} %add.211), channel_id=1, source_target_pairs={{0,4},{4,0},{8,12},{12,8},{1,5},{5,1},{9,13},{13,9},{2,6},{6,2},{1... | collective-permute-start | bytes 52232 | tf_op jit(solution)/shard_map/ppermute | solution.py:124
  (50 other events, 324.4 us)
Sparse Core Ops, SparseCore 0:
  90.6 85.9 all-reduce.4
  204.7 85.4 all-reduce.6
  292.5 85.3 all-reduce.8
  380.3 86.0 all-reduce.10
Sparse Core Ops, SparseCore 1:
  93.6 81.0 all-gather.1
  213.0 60.4 reduce-scatter.3
  317.7 60.7 reduce-scatter.5
  382.2 72.2 reduce-scatter.7

commit v4 on v3

--- a/solution.py
+++ b/solution.py
@@ -13,7 +13,7 @@
 LOW = jnp.bfloat16
 F32 = jnp.float32
 LOG2E = 1.4426950408889634
-VMEM_BYTES = 56 * 1024 * 1024
+VMEM_MIB = 56
 
 
 def dot_plain(matrix_a, matrix_b):
@@ -131,8 +131,8 @@
     return lax.ppermute(values, "context", [(index, index ^ bit) for index in range(size)])
 
 
-def params():
-    return pltpu.CompilerParams(vmem_limit_bytes=VMEM_BYTES)
+def params(mib=VMEM_MIB):
+    return pltpu.CompilerParams(vmem_limit_bytes=mib * 1024 * 1024)
 
 
 def cost(flops, moved):
@@ -251,7 +251,7 @@
     by_rows(hidden.shape[0], body)
 
 
-def row_call(kernel, ids, arrays, out_types, gain=None, sums=False, after=()):
+def row_call(kernel, ids, arrays, out_types, gain=None, after=(), sums=False, mib=VMEM_MIB):
     rows, width = arrays[0].shape
     tile = min(256, rows)
     spec = pl.BlockSpec((tile, width), lambda step, *_: (step, 0))
@@ -275,7 +275,7 @@
         ),
         out_shape=[jax.ShapeDtypeStruct((rows, width), kind) for kind in out_types]
         + [jax.ShapeDtypeStruct((8, width), F32)] * sums,
-        compiler_params=params(),
+        compiler_params=params(mib),
         cost_estimate=cost(10 * rows * width, moved),
     )(ids, *after, *arrays, *gains)
 
@@ -360,59 +360,50 @@
 def attend_kernel(half, count, parts_in, info, qproj, *refs):
     weights, refs = refs[:parts_in], refs[parts_in:]
     pieces, (gain, cosine, sine, seg_row, seg_col), refs = refs[:count], refs[count : count + 5], refs[count + 5 :]
-    out, out_wide, log_out, part_out, qs, acc, total, segq, kv, part_sum = refs
+    out, out_wide, log_out, part_out, qs, acc, total, segq, kv = refs
     load_pieces(pieces, kv)
     dim = gain.shape[1]
-    group = qproj.shape[1] // dim
+    heads = kv.shape[1] // (2 * dim)
+    group = qproj.shape[1] // (dim * heads)
     pairs = info.shape[0] - 1
     factor = LOG2E * dim ** (-0.5)
-    for head in range(group):
-        cols = slice(head * dim, (head + 1) * dim)
-        query = head_forward(qproj[:, cols], gain[...], cosine[...], sine[...])[0]
-        for piece in range(2):
-            spot = slice(head * half, (head + 1) * half)
-            rows = slice(piece * half, (piece + 1) * half)
-            qs[piece, spot, :] = query[rows]
-            segq[piece, spot, :] = seg_col[rows, :]
+    for piece in range(2):
+        for member in range(group):
+            segq[piece, member * half : (member + 1) * half, :] = seg_col[piece * half : (piece + 1) * half, :1]
+    for head in range(heads):
+        for member in range(group):
+            at = (head * group + member) * dim
+            query = head_forward(qproj[:, at : at + dim], gain[...], cosine[...], sine[...])[0]
+            for piece in range(2):
+                qs[head, piece, member * half : (member + 1) * half, :] = query[piece * half : (piece + 1) * half]
     acc[...] = jnp.zeros_like(acc)
     total[...] = jnp.zeros_like(total)
     for step in range(pairs):
         piece, key_block, query_block, spot = pair_of(info, step)
         rows = pl.ds(pl.multiple_of(spot * half, half), half)
-        scores = dot_right_t(qs[piece], kv[rows, :dim])
         key_seg = seg_row[:, pl.ds(pl.multiple_of(key_block * half, half), half)]
-        allowed = allowed_pair(scores.shape, half, query_block, key_block, segq[piece], key_seg)
-        weight = jnp.where(allowed, jnp.exp2(scores * factor), 0.0)
-        total[piece] += sum(weight[:, at : at + 128] for at in range(0, half, 128))
-        acc[piece] += dot_plain(weight.astype(LOW), kv[rows, dim:])
-    for piece in range(2):
-        sums = jnp.sum(total[piece], axis=-1, keepdims=True)
-        result = acc[piece] / sums
-        logs = jnp.broadcast_to(jnp.log2(sums), result.shape)
-        for head in range(group):
-            cols = slice(head * dim, (head + 1) * dim)
+        allowed = allowed_pair((group * half, half), half, query_block, key_block, segq[piece], key_seg)
+        for head in range(heads):
+            at = 2 * head * dim
+            scores = dot_right_t(qs[head, piece], kv[rows, at : at + dim])
+            weight = jnp.where(allowed, jnp.exp2(scores * factor), 0.0)
+            total[head, piece] += sum(weight[:, col : col + 128] for col in range(0, half, 128))
+            acc[head, piece] += dot_plain(weight.astype(LOW), kv[rows, at + dim : at + 2 * dim])
+    for head in range(heads):
+        for piece in range(2):
+            sums = jnp.sum(total[head, piece], axis=-1, keepdims=True)
+            result = acc[head, piece] / sums
+            logs = jnp.broadcast_to(jnp.log2(sums), result.shape)
             rows = slice(piece * half, (piece + 1) * half)
-            part = result[head * half : (head + 1) * half]
-            out[rows, cols] = part.astype(LOW)
-            out_wide[rows, cols] = part
-            log_out[rows, cols] = logs[head * half : (head + 1) * half]
-    here = pl.program_id(0)
-
+            for member in range(group):
+                at = (head * group + member) * dim
+                part = result[member * half : (member + 1) * half]
+                out[rows, at : at + dim] = part.astype(LOW)
+                out_wide[rows, at : at + dim] = part
+                log_out[rows, at : at + dim] = logs[member * half : (member + 1) * half]
     for step, source in enumerate(weights):
         cols = slice(step * source.shape[0], (step + 1) * source.shape[0])
-        term = dot_right_t(out[...], source[...])
-
-        @pl.when(here == 0)
-        def _():
-            part_sum[:, cols] = term
-
-        @pl.when(here > 0)
-        def _():
-            part_sum[:, cols] += term
-
-    @pl.when(here == pl.num_programs(0) - 1)
-    def _():
-        part_out[...] = part_sum[...].astype(LOW)
+        part_out[:, cols] = dot_right_t(out[...], source[...]).astype(LOW)
 
 
 def attend_back_kernel(half, count, info, qproj, wide, logs, grad, *refs):
@@ -433,7 +424,7 @@
             rows = slice(piece * half, (piece + 1) * half)
             qs[piece, spot, :] = query[rows]
             gs[piece, spot, :] = grad[rows, cols]
-            segq[piece, spot, :] = seg_col[rows, :]
+            segq[piece, spot, :] = seg_col[rows, :1]
             ls[piece, spot, :] = logs[rows, head * dim : head * dim + 1]
             ds[piece, spot, :] = delta[rows]
     dq[...] = jnp.zeros_like(dq)
@@ -478,36 +469,32 @@
     count, kvcols = len(pieces), pieces[0].shape[1]
     dim = gain.shape[1]
     heads = kvcols // (2 * dim)
-    wide = qcols // heads
-    half = rows // 2
-    stacked = half * (wide // dim)
-    qspec, kspec = heads_spec(rows, wide), heads_spec(rows, 2 * dim)
-    tables = (gain, cosine, sine, seg_row, seg_col)
+    stacked = rows // 2 * (qcols // (heads * dim))
+    early = [pltpu.with_memory_space_constraint(item, pltpu.VMEM) for item in (qproj, cosine, sine, seg_col)]
+    qproj, cosine, sine, seg_col = early
+    operands = [qproj, *weights, *pieces, gain, cosine, sine, seg_row, seg_col]
+    in_vmem = pl.BlockSpec(memory_space=pltpu.VMEM)
     width = sum(item.shape[0] for item in weights)
+    shapes = [((rows, qcols), LOW), ((rows, qcols), F32), ((rows, qcols), F32), ((rows, width), LOW)]
     return pl.pallas_call(
-        functools.partial(attend_kernel, half, count, len(weights)),
+        functools.partial(attend_kernel, rows // 2, count, len(weights)),
         grid_spec=pltpu.PrefetchScalarGridSpec(
             num_scalar_prefetch=1,
-            grid=(heads,),
-            in_specs=[qspec]
-            + [heads_spec(item.shape[0], wide) for item in weights]
-            + [kspec] * count
-            + [whole(item.shape) for item in tables],
-            out_specs=[qspec] * 3 + [whole((rows, width))],
+            grid=(1,),
+            in_specs=[in_vmem if any(item is one for one in early) else whole(item.shape) for item in operands],
+            out_specs=[whole(shape) for shape, _ in shapes],
             scratch_shapes=[
-                pltpu.VMEM((2, stacked, dim), LOW),
-                pltpu.VMEM((2, stacked, dim), F32),
-                pltpu.VMEM((2, stacked, 128), F32),
+                pltpu.VMEM((heads, 2, stacked, dim), LOW),
+                pltpu.VMEM((heads, 2, stacked, dim), F32),
+                pltpu.VMEM((heads, 2, stacked, 128), F32),
                 pltpu.VMEM((2, stacked, 1), jnp.int32),
-                pltpu.VMEM((count * rows, 2 * dim), LOW),
-                pltpu.VMEM((rows, width), F32),
+                pltpu.VMEM((count * rows, kvcols), LOW),
             ],
         ),
-        out_shape=[jax.ShapeDtypeStruct((rows, qcols), kind) for kind in (LOW, F32, F32)]
-        + [jax.ShapeDtypeStruct((rows, width), LOW)],
-        compiler_params=params(),
+        out_shape=[jax.ShapeDtypeStruct(shape, kind) for shape, kind in shapes],
+        compiler_params=params(44),
         cost_estimate=cost(2 * rows * count * rows * qcols * 2, 8 * rows * qcols * 2),
-    )(info, qproj, *weights, *pieces, *tables)
+    )(info, *operands)
 
 
 def attend_back(info, qproj, wide_out, logs, grad, pieces, gain, cosine, sine, seg_row, seg_col):
@@ -585,7 +572,7 @@
         + [whole(kgain.shape), tiled(cosine.shape[1]), tiled(sine.shape[1])],
         out_specs=[tiled(cols) for cols, _ in shapes],
         out_shape=[jax.ShapeDtypeStruct((rows, cols), kind) for cols, kind in shapes],
-        compiler_params=params(),
+        compiler_params=params(28),
         cost_estimate=cost(2 * rows * width * (kvcols + qcols), 4 * rows * width + 2 * width * kvcols),
     )(inputs, *halves, kgain, cosine, sine)
 
@@ -602,10 +589,26 @@
     )(mine, other, proj, gain, cosine, sine)
 
 
-def feed_kernel(inputs, gate, up, dproduct, product, dgate, dup, dinputs, total):
+def feed_kernel(
+    ids, hidden, attn, gain, weights, dproduct, product, dgate, dup, dinputs, middle_out, inputs_out,
+    total, both, middle, inputs, sems,
+):
+    tile = dproduct.shape[1]
     step = pl.program_id(0)
-    gate_in = dot_plain(inputs[...], gate[...])
-    up_in = dot_plain(inputs[...], up[...])
+    copies = [
+        pltpu.make_async_copy(middle, middle_out, sems.at[0]),
+        pltpu.make_async_copy(inputs, inputs_out, sems.at[1]),
+    ]
+
+    @pl.when(step == 0)
+    def _():
+        second_norm_kernel(gain.shape[0], ids, hidden, attn, gain, middle, inputs)
+        for copy in copies:
+            copy.start()
+        total[...] = jnp.zeros_like(total)
+
+    ins = dot_plain(inputs[...], weights[...])
+    gate_in, up_in = ins[:, :tile], ins[:, tile:]
     sigmoid = 1.0 / (1.0 + jnp.exp(-gate_in))
     active = gate_in * sigmoid
     product[...] = (active * up_in).astype(LOW)
@@ -614,39 +617,65 @@
     dup_low = (grad * active).astype(LOW)
     dgate[...] = dgate_low
     dup[...] = dup_low
-    part = dot_right_t(dgate_low, gate[...]) + dot_right_t(dup_low, up[...])
-
-    @pl.when(step == 0)
-    def _():
-        total[...] = part
-
-    @pl.when(step > 0)
-    def _():
-        total[...] += part
+    both[:, :tile] = dgate_low
+    both[:, tile:] = dup_low
+    total[...] += dot_right_t(both[...], weights[...])
 
     @pl.when(step == pl.num_programs(0) - 1)
     def _():
         dinputs[...] = total[...].astype(LOW)
-
-
-def feed(inputs, gate_up, dproduct):
-    rows, width = inputs.shape
+        for copy in copies:
+            copy.wait()
+
+
+def feed_tile(units):
+    return 256 if units % 256 == 0 else units
+
+
+def by_tiles(gate, up):
+    rows, units = gate.shape
+    tile = feed_tile(units)
+
+    def kernel(gate_ref, up_ref, out):
+        for at in range(0, units, tile):
+            out[:, 2 * at : 2 * at + tile] = gate_ref[:, at : at + tile]
+            out[:, 2 * at + tile : 2 * at + 2 * tile] = up_ref[:, at : at + tile]
+
+    return pl.pallas_call(
+        kernel,
+        out_shape=jax.ShapeDtypeStruct((rows, 2 * units), gate.dtype),
+        compiler_params=params(),
+        cost_estimate=cost(0, 8 * rows * units),
+    )(gate, up)
+
+
+def feed(ids, hidden, attn, gain, gate_up, dproduct):
+    rows, width = hidden.shape
     units = dproduct.shape[1]
-    tile = min(256, units)
-    count = units // tile
-    gspec = pl.BlockSpec((width, tile), lambda step: (0, step))
-    uspec = pl.BlockSpec((width, tile), lambda step: (0, step + count))
-    tspec = pl.BlockSpec((rows, tile), lambda step: (0, step))
+    tile = feed_tile(units)
+    tspec = pl.BlockSpec((rows, tile), lambda step, *_: (0, step))
+    anywhere = pl.BlockSpec(memory_space=pl.ANY)
     return pl.pallas_call(
         feed_kernel,
-        grid=(count,),
-        in_specs=[whole((rows, width)), gspec, uspec, tspec],
-        out_specs=[tspec, tspec, tspec, whole((rows, width))],
-        out_shape=[jax.ShapeDtypeStruct((rows, units), LOW)] * 3 + [jax.ShapeDtypeStruct((rows, width), LOW)],
-        scratch_shapes=[pltpu.VMEM((rows, width), F32)],
+        grid_spec=pltpu.PrefetchScalarGridSpec(
+            num_scalar_prefetch=1,
+            grid=(units // tile,),
+            in_specs=[whole((rows, width)), whole((rows, width)), whole(gain.shape)]
+            + [pl.BlockSpec((width, 2 * tile), lambda step, *_: (0, step)), tspec],
+            out_specs=[tspec, tspec, tspec, whole((rows, width)), anywhere, anywhere],
+            scratch_shapes=[
+                pltpu.VMEM((rows, width), F32),
+                pltpu.VMEM((rows, 2 * tile), LOW),
+                pltpu.VMEM((rows, width), F32),
+                pltpu.VMEM((rows, width), LOW),
+                pltpu.SemaphoreType.DMA((2,)),
+            ],
+        ),
+        out_shape=[jax.ShapeDtypeStruct((rows, units), LOW)] * 3
+        + [jax.ShapeDtypeStruct((rows, width), kind) for kind in (LOW, F32, LOW)],
         compiler_params=params(),
         cost_estimate=cost(8 * rows * width * units, 4 * width * units + 10 * rows * units),
-    )(inputs, gate_up, gate_up, dproduct)
+    )(ids, hidden, attn, gain, gate_up, dproduct)
 
 
 def shards(
@@ -685,7 +714,8 @@
     blocks = staged_blocks() if is_staged else jnp.zeros((1,), jnp.int32)
     count = blocks.shape[0]
     near_shard = assemble(key_weight, value_weight, query_weight, head_dim)
-    gains = gather_fast(jnp.stack([attn_gain, ffn_gain])).reshape(-1, 2, shard_rows).astype(F32)
+    gain_shard, near_shard = tie(jnp.stack([attn_gain, ffn_gain]), near_shard)
+    gains = gather_fast(gain_shard).reshape(-1, 2, shard_rows).astype(F32)
     gain_one = gains[:, 0].reshape(count, -1)
     gain_two = gains[:, 1].reshape(count, -1)
 
@@ -704,6 +734,7 @@
             for block in (me, last - me)
         ]
     )[:, None]
+    seg_col = jnp.broadcast_to(seg_col, (local_rows, head_dim))
     half_dim = head_dim // 2
     inverse = THETA ** (-(jnp.arange(half_dim).astype(F32) * 2.0 / head_dim))
     angles = positions.astype(F32)[:, None] * inverse[None, :]
@@ -722,15 +753,13 @@
     if is_staged:
         near_pair = staged_pair(near_shard)
         near_far = staged(near_pair, "yx")
-        near_far, gain_one, gain_two, blocks, info, seg_col, cosine, sine = tie(
-            near_far, gain_one, gain_two, blocks, info, seg_col, cosine, sine
-        )
+        near_far, gain_one = tie(near_far, gain_one)
         near_last, out_shard = tie(staged(near_far, "core"), output_weight)
         near_halves = [near_pair, near_far, staged(near_pair, "core"), near_last]
         out_pair = staged_pair(out_shard, "y")
     else:
         near_halves = [gather_rows(near_shard)]
-    (inputs_one,) = row_call(first_norm_kernel, blocks, [hidden_in], [LOW], gain_one)
+    (inputs_one,) = row_call(first_norm_kernel, blocks, [hidden_in], [LOW], gain_one, [info, seg_col, cosine, sine, qgain, kgain, gain_two], mib=20)
     kv_proj, query_proj, kv_own = opening(inputs_one, near_halves, 2 * kcols, qcols, kgain, cosine, sine)
     if is_staged:
         out_pair, kv_own = tie(out_pair, kv_own)
@@ -739,7 +768,7 @@
         out_halves = [gather_rows(output_weight)]
     kv_across = swap_context(kv_own, 2)
     kv_pieces = [kv_own, swap_context(kv_own, 1), kv_across, swap_context(kv_across, 1)]
-    gate_up_shard, kv_proj = tie(jnp.concatenate([gate_weight, up_weight], axis=1), kv_proj)
+    gate_up_shard, kv_proj = tie(by_tiles(gate_weight, up_weight), kv_proj)
     gate_up = gather_rows(gate_up_shard)
     attended, attended_wide, logs, attn_part = attend(
         info, query_proj, out_halves, kv_pieces, qgain, cosine, sine, segments, seg_col
@@ -751,8 +780,9 @@
     near_full = jnp.concatenate(near_halves)
     out_full = jnp.concatenate(out_halves)
     attn_out, dproduct, near_full, out_full = tie(attn_out, dproduct, near_full, out_full)
-    middle, inputs_two = row_call(second_norm_kernel, out_blocks, [hidden_in, attn_out], [F32, LOW], gain_two)
-    product, dgate, dup_low, dnormed_two_part = feed(inputs_two, gate_up, dproduct)
+    product, dgate, dup_low, dnormed_two_part, middle, inputs_two = feed(
+        out_blocks, hidden_in, attn_out, gain_two, gate_up, dproduct
+    )
     dnormed_two = sum_tensor(dnormed_two_part)
 
     ffn_part = dot_right_t(product, down_full).astype(LOW)
@@ -762,7 +792,7 @@
     dnormed_two, ffn_part, grad_gate, grad_up = tie(dnormed_two, ffn_part, grad_gate, grad_up)
     ffn_out = sum_tensor(ffn_part)
     dmiddle, dattn, gain_two_sums = row_call(
-        second_back_kernel, out_blocks, [dnormed_two, middle, cotangent], [F32, LOW], gain_two, True
+        second_back_kernel, out_blocks, [dnormed_two, middle, cotangent], [F32, LOW], gain_two, sums=True
     )
     gain_two_part = jnp.sum(gain_two_sums, axis=0) / lax.axis_size("tensor")
     dattended = dot_plain(dattn, out_full).astype(LOW)

time: 491 us -> 480 us (0.978)
  Pallas kernels: 94.7 us -> 85.3 us
  other arithmetic: 26.7 us -> 18.6 us
    pallas_call x6 -> x5, Pallas kernels: 33.1 us -> 24.8 us  [row_call(): pl.pallas_call(ordered, grid_spec=pltpu.PrefetchScalarGridSpec(num_scalar...]
    ppermute x19, waiting for transfers between devices: 114 us -> 109 us  [staged(): return lax.ppermute(values, ROWS, staged_pairs(step))]
    unnamed x84 -> x116, local copies, waits for them, and re-layouts: 17.4 us -> 22.6 us
    pallas_call x2 -> x3, Pallas kernels: 34.9 us -> 34.4 us  [the longest x1 22.8 us: feed(): pl.pallas_call(feed_kernel, grid_spec=pltpu.PrefetchScalarGridSpec(num_sc...]
  transfers between devices with their start and end apart: 37 -> 37, of which waited for: 23 -> 22; matrix products, arithmetic and copies ran while one was open for 18% -> 17% of each run, Pallas kernels for 12% -> 11%
where the time goes in v4:
time: 480 us; the launch traced here: 471 us
  waiting for transfers between devices  229 us (48%)
  Pallas kernels  85.3 us (18%)
  matrix products  47.4 us (10%)
  starting transfers between devices  39.8 us (8%)
  local copies, waits for them, and re-layouts  34.1 us (7%)
  other arithmetic  18.6 us (4%)
  between operations  16.8 us (4%)
    ppermute x19, waiting for transfers between devices, staged(): return lax.ppermute(values, ROWS, staged_pairs(step))  109 us
    psum x4, waiting for transfers between devices, sum_tensor(): return lax.psum(partial.astype(LOW), 'tensor')  98.4 us
    pallas_call x5, Pallas kernels, row_call(): pl.pallas_call(ordered, grid_spec=pltpu.PrefetchScalarGridSpec(num_scalar...  24.8 us
    dot_general x5, matrix products, dot_left_t(): lax.dot_general(matrix_a, matrix_b, (((0,), (0,)), ((), ())), preferred_e...  24.3 us
    pallas_call x1, Pallas kernels, feed(): pl.pallas_call(feed_kernel, grid_spec=pltpu.PrefetchScalarGridSpec(num_sc...  22.8 us
    unnamed x116, local copies, waits for them, and re-layouts  22.6 us
    ppermute x19, starting transfers between devices, staged(): return lax.ppermute(values, ROWS, staged_pairs(step))  20.2 us
    ppermute x5, waiting for transfers between devices, swap_context(): lax.ppermute(values, 'context', [(index, index ^ bit) for index in range(...  18.7 us
  transfers between devices with their start and end apart: 37, of which 22 were waited for; matrix products, arithmetic and copies ran while one was open for 17% of the time, Pallas kernels for 11%

profile of v4, /device:TPU:0, one launch (start us, length us, event | category | flops | bytes accessed | tf_op | source)
XLA Modules:
  0.0 471.3 jit_solution(3365107470204624915)
XLA Ops:
  28.6 9.3 %collective-permute-done.1 = bf16[4,256]{1,0:T(4,128)(2,1)S(1)} collective-permute-done((bf16[4,256]{1,0:T(4,128)(2,1)S(1)}, bf16[4,256]{1,0:T(4,128)(2,1)S(1)}, u32[]{:S(2)}, u32[]{:S(2)}) %collective-permute-start.1) | collective-permute-done | bytes 2080 | tf_op jit(solution)/shard_map/ppermute | solution.py:74
  46.8 5.4 %shard_map.239 = (f32[512,512]{1,0:T(8,128)S(1)}, f32[512,512]{1,0:T(8,128)S(1)}, bf16[512,512]{1,0:T(8,128)(2,1)S(1)}) custom-call(bf16[512,2048]{1,0:T(8,128)(2,1)S(1)} %shard_map.238.inputs, bf16[512,1024]{1,0:T(8,128)(2,1)} %get-tuple-element.120.refs_0_, bf16[512,1024]{1,0:T(8,128)(2,1)} %collective-permute-done.4.refs_1_, ...), custom_call_target="tpu_custom_call" | custom-call | flops 2147483648 | bytes 6291456 | tf_op jit(solution)/shard_map/pallas_call | solution.py:567
  55.4 11.7 %collective-permute-done.8 = bf16[512,512]{1,0:T(8,128)(2,1)S(1)} collective-permute-done((bf16[512,512]{1,0:T(8,128)(2,1)S(1)}, bf16[512,512]{1,0:T(8,128)(2,1)S(1)}, u32[]{:S(2)}, u32[]{:S(2)}) %collective-permute-start.8) | collective-permute-done | bytes 524320 | tf_op jit(solution)/shard_map/ppermute | solution.py:74
  72.2 8.5 %shard_map.240 = (bf16[512,512]{1,0:T(8,128)(2,1)S(1)}, f32[512,512]{1,0:T(8,128)S(1)}, f32[512,512]{1,0:T(8,128)S(1)}, bf16[512,2048]{1,0:T(8,128)(2,1)}) custom-call(s32[10]{0:T(128)S(1)} %stack.112.refs_0_.info, f32[512,512]{1,0:T(8,128)S(1)} %get-tuple-element.68.qproj, bf16[1024,512]{1,0:T(8,128)(2,1)S(1)} %constant_dynamic-update-slice_fusion.2.refs_0_, ...), custom_call_target="tpu_custom_call" | custom-call | flops 2147483648 | bytes 4194304 | tf_op jit(solution)/shard_map/pallas_call | solution.py:479
  87.6 14.0 %collective-permute-done.13 = bf16[256,1536]{1,0:T(8,128)(2,1)S(1)} collective-permute-done((bf16[256,1536]{1,0:T(8,128)(2,1)S(1)}, bf16[256,1536]{1,0:T(8,128)(2,1)S(1)}, u32[]{:S(2)}, u32[]{:S(2)}) %collective-permute-start.13) | collective-permute-done | bytes 786464 | tf_op jit(solution)/shard_map/ppermute | solution.py:74
  101.8 31.9 %collective-permute-done.14 = bf16[512,1536]{1,0:T(8,128)(2,1)S(1)} collective-permute-done((bf16[512,1536]{1,0:T(8,128)(2,1)S(1)}, bf16[512,1536]{1,0:T(8,128)(2,1)S(1)}, u32[]{:S(2)}, u32[]{:S(2)}) %collective-permute-start.14) | collective-permute-done | bytes 1572896 | tf_op jit(solution)/shard_map/ppermute | solution.py:74
  160.1 9.5 %all-reduce.5.cloned.1.call-done.attn = bf16[512,2048]{1,0:T(8,128)(2,1)} async-done(((bf16[512,2048]{1,0:T(8,128)(2,1)}), bf16[512,2048]{1,0:T(8,128)(2,1)}) %all-reduce.5.cloned.1.call-update) | async-done | bytes 2097168 | tf_op jit(solution)/shard_map/psum | solution.py:48
  169.6 22.8 %shard_map.243 = (bf16[512,1536]{1,0:T(8,128)(2,1)}, bf16[512,1536]{1,0:T(8,128)(2,1)}, bf16[512,1536]{1,0:T(8,128)(2,1)}, bf16[512,2048]{1,0:T(8,128)(2,1)}, f3...) custom-call(s32[8]{0:T(128)} %copy-done.46, bf16[512,2048]{1,0:T(8,128)(2,1)} %refs_9_.3, ...), custom_call_target="tpu_custom_call" | custom-call | flops 12884901888 | bytes 20447232 | tf_op jit(solution)/shard_map/pallas_call | solution.py:658
  194.0 6.7 %fusion = bf16[2048,1536]{1,0:T(8,128)(2,1)} fusion(bf16[512,1536]{1,0:T(8,128)(2,1)} %get-tuple-element.82, bf16[512,2048]{1,0:T(8,128)(2,1)S(1)} %copy-done.26), kind=kOutput, calls=%fused_computation.3 | convolution fusion | flops 3224371200 | bytes 9961472 | tf_op jit(solution)/shard_map/dot_general | solution.py:28
  202.3 6.9 %convolution_convert_fusion.2 = bf16[2048,1536]{1,0:T(8,128)(2,1)} fusion(bf16[512,2048]{1,0:T(8,128)(2,1)S(1)} %copy-done.52, bf16[512,1536]{1,0:T(8,128)(2,1)} %get-tuple-element.84), kind=kOutput, calls=%fused_computation.2 | convolution fusion | flops 3224371200 | bytes 9961472 | tf_op jit(solution)/shard_map/dot_general | solution.py:28
  209.2 7.0 %convolution_convert_fusion.1 = bf16[2048,1536]{1,0:T(8,128)(2,1)} fusion(bf16[512,2048]{1,0:T(8,128)(2,1)S(1)} %copy-done.52, bf16[512,1536]{1,0:T(8,128)(2,1)} %get-tuple-element.85), kind=kOutput, calls=%fused_computation.1 | convolution fusion | flops 3224371200 | bytes 9961472 | tf_op jit(solution)/shard_map/dot_general | solution.py:28
  216.2 8.2 %convolution_convert_fusion.6 = bf16[512,2048]{1,0:T(8,128)(2,1)} fusion(bf16[512,1536]{1,0:T(8,128)(2,1)} %get-tuple-element.82, bf16[2048,1536]{1,0:T(8,128)(2,1)} %copy-done.42), kind=kOutput, calls=%fused_computation.10 | convolution fusion | flops 3222274048 | bytes 9961472 | tf_op jit(solution)/shard_map/dot_general | solution.py:24
  224.4 53.7 %all-reduce.7.cloned.1.call-done.refs_0_ = bf16[512,2048]{1,0:T(8,128)(2,1)} async-done(((bf16[512,2048]{1,0:T(8,128)(2,1)}), bf16[512,2048]{1,0:T(8,128)(2,1)}) %all-reduce.7.cloned.1.call-update) | async-done | bytes 2097168 | tf_op jit(solution)/shard_map/psum | solution.py:48
  278.3 8.0 %shard_map.244 = (f32[512,2048]{1,0:T(8,128)}, bf16[512,2048]{1,0:T(8,128)(2,1)}, f32[8,2048]{1,0:T(8,128)}) custom-call(s32[8]{0:T(128)} %copy-done.46, bf16[512,2048]{1,0:T(8,128)(2,1)} %all-reduce.7.cloned.1.call-done.refs_0_, f32[512,2048]{1,0:T(8,128)} %get-tuple-element.80.refs_1_.refs_0_, bf16[512,2048]{1,0:T(8,128)(2,1)} %refs_2_.1, f32[8,256]{1,0:T(8,128)} %copy-done.17), custom_call_target="tpu_custom_call" | custom-call | flops 10485760 | bytes 14680064 | tf_op jit(solution)/shard_map/pallas_call | solution.py:266
  289.9 15.4 %shard_map.245 = (bf16[512,512]{1,0:T(8,128)(2,1)}, bf16[1024,512]{1,0:T(8,128)(2,1)}, bf16[1024,512]{1,0:T(8,128)(2,1)}, f32[2,8,128]{2,1,0:T(8,128)}) custom-call(s32[10]{0:T(128)} %copy-done.22, f32[512,512]{1,0:T(8,128)} %copy-done.7, f32[512,512]{1,0:T(8,128)} %copy-done.8, f32[512,512]{1,0:T(8,128)} %copy-done.9, ...), custom_call_target="tpu_custom_call" | custom-call | bytes 262144 | tf_op jit(solution)/shard_map/pallas_call | solution.py:511
  311.9 12.5 %collective-permute-done.17.other = bf16[512,512]{1,0:T(8,128)(2,1)S(1)} collective-permute-done((bf16[512,512]{1,0:T(8,128)(2,1)S(1)}, bf16[512,512]{1,0:T(8,128)(2,1)S(1)}, u32[]{:S(2)}, u32[]{:S(2)}) %collective-permute-start.17) | collective-permute-done | bytes 524320 | tf_op jit(solution)/shard_map/ppermute | solution.py:131
  329.9 6.0 %multiply_reduce_fusion = (f32[2048]{0:T(1024)S(1)}, bf16[512,2048]{1,0:T(8,128)(2,1)}) fusion(bf16[512,2048]{1,0:T(8,128)(2,1)S(1)} %copy-done.5, bf16[512,1024]{1,0:T(8,128)(2,1)S(1)} %constant_dynamic-update-slice_fusion.13, bf16[2048,1024]{1,0:T(8,128)(2,1)} %constant_dynamic-update-slice_fusion.8), kind=kOutput, calls=%fused_computation.5 | convolution fusion | flops 2152724480 | bytes 9445376 | tf_op jit(solution)/shard_map/dot_general | solution.py:24
  335.9 30.0 %all-reduce.9.cloned.1.call-done.refs_1_ = bf16[512,2048]{1,0:T(8,128)(2,1)} async-done(((bf16[512,2048]{1,0:T(8,128)(2,1)}), bf16[512,2048]{1,0:T(8,128)(2,1)}) %all-reduce.9.cloned.1.call-update) | async-done | bytes 2097168 | tf_op jit(solution)/shard_map/psum | solution.py:48
  379.8 13.5 %collective-permute-done.27 = bf16[512,512]{1,0:T(8,128)(2,1)} collective-permute-done((bf16[512,512]{1,0:T(8,128)(2,1)}, bf16[512,512]{1,0:T(8,128)(2,1)}, u32[]{:S(2)}, u32[]{:S(2)}) %collective-permute-start.27) | collective-permute-done | bytes 524320 | tf_op jit(solution)/shard_map/ppermute | solution.py:74
  399.5 7.3 %collective-permute-done.28 = bf16[256,512]{1,0:T(8,128)(2,1)} collective-permute-done((bf16[256,512]{1,0:T(8,128)(2,1)S(1)}, bf16[256,512]{1,0:T(8,128)(2,1)}, u32[]{:S(2)}, u32[]{:S(2)}) %collective-permute-start.28) | collective-permute-done | bytes 262176 | tf_op jit(solution)/shard_map/ppermute | solution.py:74
  410.6 10.5 %collective-permute-done.25 = bf16[256,1024]{1,0:T(8,128)(2,1)S(1)} collective-permute-done((bf16[256,1024]{1,0:T(8,128)(2,1)S(1)}, bf16[256,1024]{1,0:T(8,128)(2,1)S(1)}, u32[]{:S(2)}, u32[]{:S(2)}) %collective-permute-start.25) | collective-permute-done | bytes 524320 | tf_op jit(solution)/shard_map/ppermute | solution.py:74
  421.3 10.3 %collective-permute-start.20 = (f32[4352]{0:T(1024)S(1)}, f32[4352]{0:T(1024)S(1)}, u32[]{:S(2)}, u32[]{:S(2)}) collective-permute-start(f32[4352]{0:T(1024)S(1)} %add.211), channel_id=1, source_target_pairs={{0,4},{4,0},{8,12},{12,8},{1,5},{5,1},{9,13},{13,9},{2,6},{6,2},{1... | collective-permute-start | bytes 52232 | tf_op jit(solution)/shard_map/ppermute | solution.py:124
  449.0 5.2 %all-reduce.11.cloned.1.call-done.refs_8_ = bf16[512,2048]{1,0:T(8,128)(2,1)} async-done(((bf16[512,2048]{1,0:T(8,128)(2,1)}), bf16[512,2048]{1,0:T(8,128)(2,1)}) %all-reduce.11.cloned.1.call-update) | async-done | bytes 2097168 | tf_op jit(solution)/shard_map/psum | solution.py:48
  454.3 6.7 %shard_map.248 = f32[512,2048]{1,0:T(8,128)} custom-call(s32[8]{0:T(128)} %copy-done.18, bf16[512,2048]{1,0:T(8,128)(2,1)} %shard_map.247.refs_0_, f32[4352]{0:T(1024)} %copy-done.41, f32[256,512]{1,0:T(8,128)} %slice.111.refs_2_, f32[256,256]{1,0:T(8,128)} %pad_maximum_fusion.6.refs_3_, f32[256,256]{1,0:T(8,128)} %pad_maximum_fusion.7.refs_4_, ...), custom_call_target="tpu_custom_call" | custom-call | flops 10485760 | bytes 12582912 | tf_op jit(solution)/shard_map/pallas_call | solution.py:266
  (263 shorter events, 133.5 us)
Async XLA Ops:
  8.0 161.6 %all-reduce.5.cloned.1.call-start = ((), (), s32[]{:S(2)}) async-start(), calls=%async_computation.3 | async-start | bytes 4194304 | tf_op jit(solution)/shard_map/psum | solution.py:48
  11.4 10.3 %collective-permute-start.3 = (bf16[256,1024]{1,0:T(8,128)(2,1)}, bf16[256,1024]{1,0:T(8,128)(2,1)S(1)}, u32[]{:S(2)}, u32[]{:S(2)}) collective-permute-start(bf16[256,1024]{1,0:T(8,128)(2,1)} %shard_map.237), channel_id=1, source_target_pairs={{0,16},{4,12},{8,24},{12,4},{16,0},{20,28},{24,8},{28,20},{1,17},{... | collective-permute-start | bytes 1572872 | tf_op jit(solution)/shard_map/ppermute | solution.py:74
  22.8 16.5 %collective-permute-start.4 = (bf16[512,1024]{1,0:T(8,128)(2,1)}, bf16[512,1024]{1,0:T(8,128)(2,1)}, u32[]{:S(2)}, u32[]{:S(2)}) collective-permute-start(bf16[512,1024]{1,0:T(8,128)(2,1)} %get-tuple-element.120.refs_0_), channel_id=1, source_target_pairs={{0,8},{4,20},{8,0},{12,28},{16,24},{20,4},{24,16},{28,12},{1,9},{5... | collective-permute-start | bytes 3145736 | tf_op jit(solution)/shard_map/ppermute | solution.py:74
  42.3 11.0 %collective-permute-start.7 = (bf16[256,512]{1,0:T(8,128)(2,1)S(1)}, bf16[256,512]{1,0:T(8,128)(2,1)S(1)}, u32[]{:S(2)}, u32[]{:S(2)}) collective-permute-start(bf16[256,512]{1,0:T(8,128)(2,1)S(1)} %copy-done.40), channel_id=1, source_target_pairs={{0,8},{4,12},{8,0},{12,4},{16,24},{20,28},{24,16},{28,20},{1,9},{5... | collective-permute-start | bytes 786440 | tf_op jit(solution)/shard_map/ppermute | solution.py:74
  53.3 13.8 %collective-permute-start.8 = (bf16[512,512]{1,0:T(8,128)(2,1)S(1)}, bf16[512,512]{1,0:T(8,128)(2,1)S(1)}, u32[]{:S(2)}, u32[]{:S(2)}) collective-permute-start(bf16[512,512]{1,0:T(8,128)(2,1)S(1)} %pad_maximum_fusion.3), channel_id=1, source_target_pairs={{0,16},{4,20},{8,24},{12,28},{16,0},{20,4},{24,8},{28,12},{1,17},{... | collective-permute-start | bytes 1572872 | tf_op jit(solution)/shard_map/ppermute | solution.py:74
  54.9 13.6 %collective-permute-start.11 = (bf16[512,512]{1,0:T(8,128)(2,1)S(1)}, bf16[512,512]{1,0:T(8,128)(2,1)S(1)}, u32[]{:S(2)}, u32[]{:S(2)}) collective-permute-start(bf16[512,512]{1,0:T(8,128)(2,1)S(1)} %get-tuple-element.72.refs_2_.refs_0_), channel_id=1, source_target_pairs={{0,8},{4,12},{8,0},{12,4},{1,9},{5,13},{9,1},{13,5},{2,10},{6,14},... | collective-permute-start | bytes 1572872 | tf_op jit(solution)/shard_map/ppermute | solution.py:131
  82.6 87.0 %all-gather.2.cloned.1.call-start = ((), (), s32[]{:S(2)}) async-start(), calls=%async_computation.4 | async-start | bytes 14155776 | tf_op jit(solution)/shard_map/all_gather | solution.py:40
  85.8 192.2 %all-reduce.7.cloned.1.call-start = ((), (), s32[]{:S(2)}) async-start(), calls=%async_computation.5 | async-start | bytes 4194304 | tf_op jit(solution)/shard_map/psum | solution.py:48
  86.1 15.5 %collective-permute-start.13 = (bf16[256,1536]{1,0:T(8,128)(2,1)S(1)}, bf16[256,1536]{1,0:T(8,128)(2,1)S(1)}, u32[]{:S(2)}, u32[]{:S(2)}) collective-permute-start(bf16[256,1536]{1,0:T(8,128)(2,1)S(1)} %copy-done.27), channel_id=1, source_target_pairs={{0,16},{4,12},{8,24},{12,4},{16,0},{20,28},{24,8},{28,20},{1,17},{... | collective-permute-start | bytes 2359304 | tf_op jit(solution)/shard_map/ppermute | solution.py:74
  101.7 32.0 %collective-permute-start.14 = (bf16[512,1536]{1,0:T(8,128)(2,1)S(1)}, bf16[512,1536]{1,0:T(8,128)(2,1)S(1)}, u32[]{:S(2)}, u32[]{:S(2)}) collective-permute-start(bf16[512,1536]{1,0:T(8,128)(2,1)S(1)} %pad_maximum_fusion.2), channel_id=1, source_target_pairs={{0,8},{4,20},{8,0},{12,28},{16,24},{20,4},{24,16},{28,12},{1,9},{5... | collective-permute-start | bytes 4718600 | tf_op jit(solution)/shard_map/ppermute | solution.py:74
  135.5 14.6 %collective-permute-start.15 = (bf16[1024,1536]{1,0:T(8,128)(2,1)}, bf16[1024,1536]{1,0:T(8,128)(2,1)}, u32[]{:S(2)}, u32[]{:S(2)}) collective-permute-start(bf16[1024,1536]{1,0:T(8,128)(2,1)} %pad_maximum_fusion), channel_id=1, source_target_pairs={{0,4},{4,0},{8,12},{12,8},{16,20},{20,16},{24,28},{28,24},{1,5},{5... | collective-permute-start | bytes 9437192 | tf_op jit(solution)/shard_map/ppermute | solution.py:74
  192.4 112.9 %reduce-scatter.4.cloned.1.call-start = ((), (), s32[]{:S(2)}) async-start(), calls=%async_computation.6 | async-start | bytes 7077888 | tf_op jit(solution)/shard_map/reduce_scatter | solution.py:44
  200.7 165.2 %all-reduce.9.cloned.1.call-start = ((), (), s32[]{:S(2)}) async-start(), calls=%async_computation.8 | async-start | bytes 4194304 | tf_op jit(solution)/shard_map/psum | solution.py:48
  278.0 88.2 %reduce-scatter.6.cloned.1.call-start = ((), (), s32[]{:S(2)}) async-start(), calls=%async_computation.7 | async-start | bytes 7077888 | tf_op jit(solution)/shard_map/reduce_scatter | solution.py:44
  305.4 148.9 %all-reduce.11.cloned.1.call-start = ((), (), s32[]{:S(2)}) async-start(), calls=%async_computation.9 | async-start | bytes 4194304 | tf_op jit(solution)/shard_map/psum | solution.py:48
  310.4 14.0 %collective-permute-start.17 = (bf16[512,512]{1,0:T(8,128)(2,1)S(1)}, bf16[512,512]{1,0:T(8,128)(2,1)S(1)}, u32[]{:S(2)}, u32[]{:S(2)}) collective-permute-start(bf16[512,512]{1,0:T(8,128)(2,1)S(1)} %get-tuple-element.117), channel_id=1, source_target_pairs={{0,8},{4,12},{8,0},{12,4},{1,9},{5,13},{9,1},{13,5},{2,10},{6,14},... | collective-permute-start | bytes 1572872 | tf_op jit(solution)/shard_map/ppermute | solution.py:131
  365.9 95.1 %reduce-scatter.8.cloned.1.call-start = ((), (), s32[]{:S(2)}) async-start(), calls=%async_computation.10 | async-start | bytes 7077888 | tf_op jit(solution)/shard_map/reduce_scatter | solution.py:44
  375.5 19.9 %collective-permute-start.24 = (bf16[512,1024]{1,0:T(8,128)(2,1)}, bf16[512,1024]{1,0:T(8,128)(2,1)}, u32[]{:S(2)}, u32[]{:S(2)}) collective-permute-start(bf16[512,1024]{1,0:T(8,128)(2,1)} %slice.108), channel_id=1, source_target_pairs={{0,8},{4,20},{8,0},{12,28},{16,24},{20,4},{24,16},{28,12},{1,9},{5... | collective-permute-start | bytes 3145736 | tf_op jit(solution)/shard_map/ppermute | solution.py:74
  378.1 15.2 %collective-permute-start.27 = (bf16[512,512]{1,0:T(8,128)(2,1)}, bf16[512,512]{1,0:T(8,128)(2,1)}, u32[]{:S(2)}, u32[]{:S(2)}) collective-permute-start(bf16[512,512]{1,0:T(8,128)(2,1)} %slice.119), channel_id=1, source_target_pairs={{0,16},{4,20},{8,24},{12,28},{16,0},{20,4},{24,8},{28,12},{1,17},{... | collective-permute-start | bytes 1572872 | tf_op jit(solution)/shard_map/ppermute | solution.py:74
  394.6 12.1 %collective-permute-start.28 = (bf16[256,512]{1,0:T(8,128)(2,1)S(1)}, bf16[256,512]{1,0:T(8,128)(2,1)}, u32[]{:S(2)}, u32[]{:S(2)}) collective-permute-start(bf16[256,512]{1,0:T(8,128)(2,1)S(1)} %slice.121), channel_id=1, source_target_pairs={{0,8},{4,12},{8,0},{12,4},{16,24},{20,28},{24,16},{28,20},{1,9},{5... | collective-permute-start | bytes 786440 | tf_op jit(solution)/shard_map/ppermute | solution.py:74
  397.1 24.1 %collective-permute-start.25 = (bf16[256,1024]{1,0:T(8,128)(2,1)S(1)}, bf16[256,1024]{1,0:T(8,128)(2,1)S(1)}, u32[]{:S(2)}, u32[]{:S(2)}) collective-permute-start(bf16[256,1024]{1,0:T(8,128)(2,1)S(1)} %slice.110), channel_id=1, source_target_pairs={{0,16},{4,12},{8,24},{12,4},{16,0},{20,28},{24,8},{28,20},{1,17},{... | collective-permute-start | bytes 1572872 | tf_op jit(solution)/shard_map/ppermute | solution.py:74
  398.6 10.0 %collective-permute-start.18 = (f32[4352]{0:T(1024)S(1)}, f32[4352]{0:T(1024)S(1)}, u32[]{:S(2)}, u32[]{:S(2)}) collective-permute-start(f32[4352]{0:T(1024)S(1)} %pad_maximum_fusion.8), channel_id=1, source_target_pairs={{0,1},{1,0},{2,3},{3,2},{4,5},{5,4},{6,7},{7,6},{8,9},{9,8},{10,11... | collective-permute-start | bytes 52232 | tf_op jit(solution)/shard_map/ppermute | solution.py:124
  408.7 12.6 %collective-permute-start.19 = (f32[4352]{0:T(1024)S(1)}, f32[4352]{0:T(1024)S(1)}, u32[]{:S(2)}, u32[]{:S(2)}) collective-permute-start(f32[4352]{0:T(1024)S(1)} %fusion.10), channel_id=1, source_target_pairs={{0,2},{1,3},{2,0},{3,1},{4,6},{5,7},{6,4},{7,5},{8,10},{9,11},{10,... | collective-permute-start | bytes 52232 | tf_op jit(solution)/shard_map/ppermute | solution.py:124
  421.3 11.1 %collective-permute-start.20 = (f32[4352]{0:T(1024)S(1)}, f32[4352]{0:T(1024)S(1)}, u32[]{:S(2)}, u32[]{:S(2)}) collective-permute-start(f32[4352]{0:T(1024)S(1)} %add.211), channel_id=1, source_target_pairs={{0,4},{4,0},{8,12},{12,8},{1,5},{5,1},{9,13},{13,9},{2,6},{6,2},{1... | collective-permute-start | bytes 52232 | tf_op jit(solution)/shard_map/ppermute | solution.py:124
  (66 other events, 620.4 us)
Sparse Core Ops, SparseCore 0:
  82.7 86.8 all-reduce.4
  192.5 85.4 all-reduce.6
  280.4 85.4 all-reduce.8
  368.2 85.9 all-reduce.10
Sparse Core Ops, SparseCore 1:
  85.9 81.4 all-gather.1
  200.8 60.4 reduce-scatter.3
  305.5 60.7 reduce-scatter.5
  370.1 72.0 reduce-scatter.7

commit v5 on v4

--- a/solution.py
+++ b/solution.py
@@ -74,17 +74,26 @@
     return lax.ppermute(values, ROWS, staged_pairs(step))
 
 
+def staged_block(index, step, first="xy"):
+    x, y, core = place(index)
+    d_core, d_second, d_first = step // 4, (step // 2) % 2, step % 2
+    its_core = core ^ d_core
+    x_first = 1 - its_core if first == "xy" else int(first == "x")
+    its_x = x ^ (x_first * d_first + (1 - x_first) * d_second)
+    its_y = y ^ (x_first * d_second + (1 - x_first) * d_first)
+    return its_x * 4 + its_y * 2 + its_core
+
+
 def staged_blocks(first="xy"):
-    x, y, core = place(lax.axis_index(ROWS))
-    blocks = []
-    for step in range(8):
-        d_core, d_second, d_first = step // 4, (step // 2) % 2, step % 2
-        its_core = core ^ d_core
-        x_first = its_core == 0 if first == "xy" else first == "x"
-        its_x = x ^ jnp.where(x_first, d_first, d_second)
-        its_y = y ^ jnp.where(x_first, d_second, d_first)
-        blocks.append(its_x * 4 + its_y * 2 + its_core)
-    return jnp.stack(blocks).astype(jnp.int32)
+    index = lax.axis_index(ROWS)
+    return jnp.stack([staged_block(index, step, first) for step in range(8)]).astype(jnp.int32)
+
+
+def staged_direct(shard):
+    parts = [shard]
+    for step in range(1, 8):
+        parts.append(lax.ppermute(shard, ROWS, [(staged_block(index, step), index) for index in range(8)]))
+    return jnp.concatenate(parts)
 
 
 OTHER = {"xy": "yx", "yx": "xy", "x": "y", "y": "x"}
@@ -227,7 +236,7 @@
             term = raw[step] * parts[step] * scale
             gain_out[:, spots[step]] += term[:8] + term[8:]
             part = cotangent[rows, spots[step]].astype(F32) + scale * (grads[step] - parts[step] * mean)
-            dmiddle[rows, spots[step]] = part
+            dmiddle[rows, spots[step]] = part.astype(LOW)
             staged_out[rows, step * width : (step + 1) * width] = part.astype(LOW)
 
     by_rows(middle.shape[0], body)
@@ -246,7 +255,8 @@
         scale = scale_of(parts)
         mean = row_sum([one * two for one, two in zip(parts, grads)]) * scale * scale / hidden.shape[1]
         for step in range(count):
-            out[rows, spots[step]] = dmiddle[rows, spots[step]] + scale * (grads[step] - parts[step] * mean)
+            term = dmiddle[rows, spots[step]].astype(F32)
+            out[rows, spots[step]] = term + scale * (grads[step] - parts[step] * mean)
 
     by_rows(hidden.shape[0], body)
 
@@ -715,7 +725,8 @@
     count = blocks.shape[0]
     near_shard = assemble(key_weight, value_weight, query_weight, head_dim)
     gain_shard, near_shard = tie(jnp.stack([attn_gain, ffn_gain]), near_shard)
-    gains = gather_fast(gain_shard).reshape(-1, 2, shard_rows).astype(F32)
+    gains = staged_direct(gain_shard) if is_staged else gather_rows(gain_shard)
+    gains = gains.reshape(-1, 2, shard_rows).astype(F32)
     gain_one = gains[:, 0].reshape(count, -1)
     gain_two = gains[:, 1].reshape(count, -1)
 
@@ -751,11 +762,12 @@
         match = (out_blocks[:, None] == blocks[None, :]).astype(F32)
         gain_two = jnp.dot(match, gain_two, precision=lax.Precision.HIGHEST)
     if is_staged:
-        near_pair = staged_pair(near_shard)
-        near_far = staged(near_pair, "yx")
-        near_far, gain_one = tie(near_far, gain_one)
-        near_last, out_shard = tie(staged(near_far, "core"), output_weight)
-        near_halves = [near_pair, near_far, staged(near_pair, "core"), near_last]
+        near_first = staged(near_shard, "xy")
+        near_second = staged(near_shard, "yx")
+        near_both, gain_one = tie(staged(near_first, "yx"), gain_one)
+        near_parts = [near_shard, near_first, near_second, near_both]
+        near_last, out_shard = tie(staged(near_both, "core"), output_weight)
+        near_halves = near_parts + [staged(part, "core") for part in near_parts[:3]] + [near_last]
         out_pair = staged_pair(out_shard, "y")
     else:
         near_halves = [gather_rows(near_shard)]
@@ -792,7 +804,7 @@
     dnormed_two, ffn_part, grad_gate, grad_up = tie(dnormed_two, ffn_part, grad_gate, grad_up)
     ffn_out = sum_tensor(ffn_part)
     dmiddle, dattn, gain_two_sums = row_call(
-        second_back_kernel, out_blocks, [dnormed_two, middle, cotangent], [F32, LOW], gain_two, sums=True
+        second_back_kernel, out_blocks, [dnormed_two, middle, cotangent], [LOW, LOW], gain_two, sums=True
     )
     gain_two_part = jnp.sum(gain_two_sums, axis=0) / lax.axis_size("tensor")
     dattended = dot_plain(dattn, out_full).astype(LOW)

time: 480 us -> 477 us (level)
  local copies, waits for them, and re-layouts: 34.1 us -> 27.3 us
  starting transfers between devices: 39.8 us -> 44.6 us
    ppermute x0 -> x7, starting transfers between devices: none -> 9.31 us  [staged_direct(): lax.ppermute(shard, ROWS, [(staged_block(index, step), index) for index i...]
    ppermute x19, starting transfers between devices: 20.2 us -> 14.5 us  [staged(): return lax.ppermute(values, ROWS, staged_pairs(step))]
    unnamed x116 -> x141, local copies, waits for them, and re-layouts: 22.6 us -> 19.9 us
  transfers between devices with their start and end apart: 37 -> 44, of which waited for: 22 -> 21; matrix products, arithmetic and copies ran while one was open for 17% -> 16% of each run, Pallas kernels for 11% -> 11%
where the time goes in v5:
time: 477 us; the launch traced here: 469 us
  waiting for transfers between devices  228 us (48%)
  Pallas kernels  84.3 us (18%)
  matrix products  47.5 us (10%)
  starting transfers between devices  44.6 us (9%)
  local copies, waits for them, and re-layouts  27.3 us (6%)
  other arithmetic  20.4 us (4%)
  between operations  17.1 us (4%)
    ppermute x19, waiting for transfers between devices, staged(): return lax.ppermute(values, ROWS, staged_pairs(step))  105 us
    psum x4, waiting for transfers between devices, sum_tensor(): return lax.psum(partial.astype(LOW), 'tensor')  96.6 us
    pallas_call x5, Pallas kernels, row_call(): pl.pallas_call(ordered, grid_spec=pltpu.PrefetchScalarGridSpec(num_scalar...  24.3 us
    dot_general x5, matrix products, dot_left_t(): lax.dot_general(matrix_a, matrix_b, (((0,), (0,)), ((), ())), preferred_e...  24.3 us
    pallas_call x1, Pallas kernels, feed(): pl.pallas_call(feed_kernel, grid_spec=pltpu.PrefetchScalarGridSpec(num_sc...  22.8 us
    unnamed x141, local copies, waits for them, and re-layouts  19.9 us
    ppermute x5, waiting for transfers between devices, swap_context(): lax.ppermute(values, 'context', [(index, index ^ bit) for index in range(...  18.7 us
    ppermute x5, starting transfers between devices, sum_all(): lax.ppermute(values, axis, [(index, index ^ bit) for index in range(size)])  17.4 us
  transfers between devices with their start and end apart: 44, of which 21 were waited for; matrix products, arithmetic and copies ran while one was open for 16% of the time, Pallas kernels for 11%

profile of v5, /device:TPU:0, one launch (start us, length us, event | category | flops | bytes accessed | tf_op | source)
XLA Modules:
  0.0 468.7 jit_solution(13297188894888004696)
XLA Ops:
  19.6 7.2 %collective-permute-done.7.refs_1_ = bf16[256,1024]{1,0:T(8,128)(2,1)} collective-permute-done((bf16[256,1024]{1,0:T(8,128)(2,1)}, bf16[256,1024]{1,0:T(8,128)(2,1)}, u32[]{:S(2)}, u32[]{:S(2)}) %collective-permute-start.7) | collective-permute-done | bytes 524320 | tf_op jit(solution)/shard_map/ppermute | solution.py:74
  46.7 5.0 %shard_map.239 = (f32[512,512]{1,0:T(8,128)S(1)}, f32[512,512]{1,0:T(8,128)S(1)}, bf16[512,512]{1,0:T(8,128)(2,1)S(1)}) custom-call(bf16[512,2048]{1,0:T(8,128)(2,1)S(1)} %shard_map.238.inputs, bf16[256,1024]{1,0:T(8,128)(2,1)S(1)} %copy-done.6, bf16[256,1024]{1,0:T(8,128)(2,1)} %collective-permute-done.7.refs_1_, ...), custom_call_target="tpu_custom_call" | custom-call | flops 2147483648 | bytes 6291456 | tf_op jit(solution)/shard_map/pallas_call | solution.py:577
  53.9 12.6 %collective-permute-done.15 = bf16[512,512]{1,0:T(8,128)(2,1)S(1)} collective-permute-done((bf16[512,512]{1,0:T(8,128)(2,1)S(1)}, bf16[512,512]{1,0:T(8,128)(2,1)S(1)}, u32[]{:S(2)}, u32[]{:S(2)}) %collective-permute-start.15) | collective-permute-done | bytes 524320 | tf_op jit(solution)/shard_map/ppermute | solution.py:74
  70.9 8.5 %shard_map.240 = (bf16[512,512]{1,0:T(8,128)(2,1)S(1)}, f32[512,512]{1,0:T(8,128)S(1)}, f32[512,512]{1,0:T(8,128)S(1)}, bf16[512,2048]{1,0:T(8,128)(2,1)}) custom-call(s32[10]{0:T(128)S(1)} %stack.112.refs_0_.info, f32[512,512]{1,0:T(8,128)S(1)} %get-tuple-element.68.qproj, bf16[1024,512]{1,0:T(8,128)(2,1)S(1)} %constant_dynamic-update-slice_fusion.refs_0_, ...), custom_call_target="tpu_custom_call" | custom-call | flops 2147483648 | bytes 4194304 | tf_op jit(solution)/shard_map/pallas_call | solution.py:489
  85.2 15.0 %collective-permute-done.20 = bf16[256,1536]{1,0:T(8,128)(2,1)S(1)} collective-permute-done((bf16[256,1536]{1,0:T(8,128)(2,1)S(1)}, bf16[256,1536]{1,0:T(8,128)(2,1)S(1)}, u32[]{:S(2)}, u32[]{:S(2)}) %collective-permute-start.20) | collective-permute-done | bytes 786464 | tf_op jit(solution)/shard_map/ppermute | solution.py:74
  100.4 33.3 %collective-permute-done.21 = bf16[512,1536]{1,0:T(8,128)(2,1)S(1)} collective-permute-done((bf16[512,1536]{1,0:T(8,128)(2,1)S(1)}, bf16[512,1536]{1,0:T(8,128)(2,1)S(1)}, u32[]{:S(2)}, u32[]{:S(2)}) %collective-permute-start.21) | collective-permute-done | bytes 1572896 | tf_op jit(solution)/shard_map/ppermute | solution.py:74
  152.6 5.0 %fusion.16.dproduct = f32[512,1536]{1,0:T(8,128)} fusion(bf16[512,2048]{1,0:T(8,128)(2,1)S(1)} %copy-done.42, bf16[2048,1536]{1,0:T(8,128)(2,1)S(1)} %constant_dynamic-update-slice_fusion.2), kind=kOutput, calls=%fused_computation.74 | convolution fusion | flops 3221225472 | bytes 11534336 | tf_op jit(solution)/shard_map/dot_general | solution.py:20
  157.6 9.5 %all-reduce.5.cloned.1.call-done.attn = bf16[512,2048]{1,0:T(8,128)(2,1)} async-done(((bf16[512,2048]{1,0:T(8,128)(2,1)}), bf16[512,2048]{1,0:T(8,128)(2,1)}) %all-reduce.5.cloned.1.call-update) | async-done | bytes 2097168 | tf_op jit(solution)/shard_map/psum | solution.py:48
  167.2 22.8 %shard_map.243 = (bf16[512,1536]{1,0:T(8,128)(2,1)}, bf16[512,1536]{1,0:T(8,128)(2,1)}, bf16[512,1536]{1,0:T(8,128)(2,1)}, bf16[512,2048]{1,0:T(8,128)(2,1)}, f3...) custom-call(s32[8]{0:T(128)} %copy-done.57, bf16[512,2048]{1,0:T(8,128)(2,1)} %refs_9_.3, ...), custom_call_target="tpu_custom_call" | custom-call | flops 12884901888 | bytes 20447232 | tf_op jit(solution)/shard_map/pallas_call | solution.py:668
  191.5 6.8 %fusion = bf16[2048,1536]{1,0:T(8,128)(2,1)} fusion(bf16[512,1536]{1,0:T(8,128)(2,1)} %get-tuple-element.82, bf16[512,2048]{1,0:T(8,128)(2,1)S(1)} %copy-done.36), kind=kOutput, calls=%fused_computation.3 | convolution fusion | flops 3224371200 | bytes 9961472 | tf_op jit(solution)/shard_map/dot_general | solution.py:28
  199.9 6.8 %convolution_convert_fusion.2 = bf16[2048,1536]{1,0:T(8,128)(2,1)} fusion(bf16[512,2048]{1,0:T(8,128)(2,1)S(1)} %copy-done.63, bf16[512,1536]{1,0:T(8,128)(2,1)} %get-tuple-element.84), kind=kOutput, calls=%fused_computation.2 | convolution fusion | flops 3224371200 | bytes 9961472 | tf_op jit(solution)/shard_map/dot_general | solution.py:28
  206.7 7.0 %convolution_convert_fusion.1 = bf16[2048,1536]{1,0:T(8,128)(2,1)} fusion(bf16[512,2048]{1,0:T(8,128)(2,1)S(1)} %copy-done.63, bf16[512,1536]{1,0:T(8,128)(2,1)} %get-tuple-element.85), kind=kOutput, calls=%fused_computation.1 | convolution fusion | flops 3224371200 | bytes 9961472 | tf_op jit(solution)/shard_map/dot_general | solution.py:28
  213.7 8.2 %convolution_convert_fusion.6 = bf16[512,2048]{1,0:T(8,128)(2,1)} fusion(bf16[512,1536]{1,0:T(8,128)(2,1)} %get-tuple-element.82, bf16[2048,1536]{1,0:T(8,128)(2,1)} %copy-done.52), kind=kOutput, calls=%fused_computation.10 | convolution fusion | flops 3222274048 | bytes 9961472 | tf_op jit(solution)/shard_map/dot_general | solution.py:24
  221.9 53.7 %all-reduce.7.cloned.1.call-done.refs_0_ = bf16[512,2048]{1,0:T(8,128)(2,1)} async-done(((bf16[512,2048]{1,0:T(8,128)(2,1)}), bf16[512,2048]{1,0:T(8,128)(2,1)}) %all-reduce.7.cloned.1.call-update) | async-done | bytes 2097168 | tf_op jit(solution)/shard_map/psum | solution.py:48
  275.9 7.6 %shard_map.244 = (bf16[512,2048]{1,0:T(8,128)(2,1)}, bf16[512,2048]{1,0:T(8,128)(2,1)}, f32[8,2048]{1,0:T(8,128)}) custom-call(s32[8]{0:T(128)} %copy-done.57, bf16[512,2048]{1,0:T(8,128)(2,1)} %all-reduce.7.cloned.1.call-done.refs_0_, f32[512,2048]{1,0:T(8,128)} %get-tuple-element.80.refs_1_.refs_0_, bf16[512,2048]{1,0:T(8,128)(2,1)} %refs_2_.1, ...), custom_call_target="tpu_custom_call" | custom-call | flops 10485760 | bytes 12582912 | tf_op jit(solution)/shard_map/pallas_call | solution.py:276
  287.1 15.3 %shard_map.245 = (bf16[512,512]{1,0:T(8,128)(2,1)}, bf16[1024,512]{1,0:T(8,128)(2,1)}, bf16[1024,512]{1,0:T(8,128)(2,1)}, f32[2,8,128]{2,1,0:T(8,128)}) custom-call(s32[10]{0:T(128)} %copy-done.32, f32[512,512]{1,0:T(8,128)} %copy-done.8, f32[512,512]{1,0:T(8,128)} %copy-done.9, f32[512,512]{1,0:T(8,128)} %copy-done.10, ...), custom_call_target="tpu_custom_call" | custom-call | bytes 262144 | tf_op jit(solution)/shard_map/pallas_call | solution.py:521
  309.0 12.5 %collective-permute-done.24.other = bf16[512,512]{1,0:T(8,128)(2,1)S(1)} collective-permute-done((bf16[512,512]{1,0:T(8,128)(2,1)S(1)}, bf16[512,512]{1,0:T(8,128)(2,1)S(1)}, u32[]{:S(2)}, u32[]{:S(2)}) %collective-permute-start.24) | collective-permute-done | bytes 524320 | tf_op jit(solution)/shard_map/ppermute | solution.py:140
  327.0 6.1 %multiply_reduce_fusion = (f32[2048]{0:T(1024)S(1)}, bf16[512,2048]{1,0:T(8,128)(2,1)}) fusion(bf16[512,2048]{1,0:T(8,128)(2,1)S(1)} %copy-done.5, bf16[512,1024]{1,0:T(8,128)(2,1)S(1)} %constant_dynamic-update-slice_fusion.14, bf16[2048,1024]{1,0:T(8,128)(2,1)} %copy-done.54), kind=kOutput, calls=%fused_computation.5 | convolution fusion | flops 2152724480 | bytes 9445376 | tf_op jit(solution)/shard_map/dot_general | solution.py:24
  333.1 30.4 %all-reduce.9.cloned.1.call-done.refs_1_ = bf16[512,2048]{1,0:T(8,128)(2,1)} async-done(((bf16[512,2048]{1,0:T(8,128)(2,1)}), bf16[512,2048]{1,0:T(8,128)(2,1)}) %all-reduce.9.cloned.1.call-update) | async-done | bytes 2097168 | tf_op jit(solution)/shard_map/psum | solution.py:48
  377.3 13.5 %collective-permute-done.34 = bf16[512,512]{1,0:T(8,128)(2,1)} collective-permute-done((bf16[512,512]{1,0:T(8,128)(2,1)}, bf16[512,512]{1,0:T(8,128)(2,1)}, u32[]{:S(2)}, u32[]{:S(2)}) %collective-permute-start.34) | collective-permute-done | bytes 524320 | tf_op jit(solution)/shard_map/ppermute | solution.py:74
  396.7 7.7 %collective-permute-done.35 = bf16[256,512]{1,0:T(8,128)(2,1)} collective-permute-done((bf16[256,512]{1,0:T(8,128)(2,1)S(1)}, bf16[256,512]{1,0:T(8,128)(2,1)}, u32[]{:S(2)}, u32[]{:S(2)}) %collective-permute-start.35) | collective-permute-done | bytes 262176 | tf_op jit(solution)/shard_map/ppermute | solution.py:74
  407.8 11.2 %collective-permute-done.32 = bf16[256,1024]{1,0:T(8,128)(2,1)S(1)} collective-permute-done((bf16[256,1024]{1,0:T(8,128)(2,1)S(1)}, bf16[256,1024]{1,0:T(8,128)(2,1)S(1)}, u32[]{:S(2)}, u32[]{:S(2)}) %collective-permute-start.32) | collective-permute-done | bytes 524320 | tf_op jit(solution)/shard_map/ppermute | solution.py:74
  419.2 10.2 %collective-permute-start.27 = (f32[4352]{0:T(1024)S(1)}, f32[4352]{0:T(1024)S(1)}, u32[]{:S(2)}, u32[]{:S(2)}) collective-permute-start(f32[4352]{0:T(1024)S(1)} %add.243), channel_id=1, source_target_pairs={{0,4},{4,0},{8,12},{12,8},{1,5},{5,1},{9,13},{13,9},{2,6},{6,2},{1... | collective-permute-start | bytes 52232 | tf_op jit(solution)/shard_map/ppermute | solution.py:133
  451.9 6.6 %shard_map.248 = f32[512,2048]{1,0:T(8,128)} custom-call(s32[8]{0:T(128)} %copy-done.28, bf16[512,2048]{1,0:T(8,128)(2,1)} %shard_map.247.refs_0_, f32[4352]{0:T(1024)} %copy-done.51, f32[256,512]{1,0:T(8,128)} %slice.111.refs_2_, f32[256,256]{1,0:T(8,128)} %pad_maximum_fusion.6.refs_3_, f32[256,256]{1,0:T(8,128)} %pad_maximum_fusion.7.refs_4_, ...), custom_call_target="tpu_custom_call" | custom-call | flops 10485760 | bytes 10485760 | tf_op jit(solution)/shard_map/pallas_call | solution.py:276
  (300 shorter events, 129.3 us)
Async XLA Ops:
  8.1 159.1 %all-reduce.5.cloned.1.call-start = ((), (), s32[]{:S(2)}) async-start(), calls=%async_computation.3 | async-start | bytes 4194304 | tf_op jit(solution)/shard_map/psum | solution.py:48
  11.5 16.0 %collective-permute-start.6 = (bf16[2,256]{1,0:T(2,128)(2,1)S(1)}, bf16[2,256]{1,0:T(2,128)(2,1)S(1)}, u32[]{:S(2)}, u32[]{:S(2)}) collective-permute-start(bf16[2,256]{1,0:T(2,128)(2,1)S(1)} %pad_maximum_fusion.9), channel_id=1, source_target_pairs={{28,0},{24,4},{20,8},{16,12},{12,16},{8,20},{4,24},{0,28},{29,1},{... | collective-permute-start | bytes 3080 | tf_op jit(solution)/shard_map/ppermute | solution.py:95
  14.9 14.3 %collective-permute-start.5 = (bf16[2,256]{1,0:T(2,128)(2,1)S(1)}, bf16[2,256]{1,0:T(2,128)(2,1)S(1)}, u32[]{:S(2)}, u32[]{:S(2)}) collective-permute-start(bf16[2,256]{1,0:T(2,128)(2,1)S(1)} %pad_maximum_fusion.9), channel_id=1, source_target_pairs={{20,0},{8,4},{28,8},{0,12},{4,16},{24,20},{12,24},{16,28},{21,1},{... | collective-permute-start | bytes 3080 | tf_op jit(solution)/shard_map/ppermute | solution.py:95
  15.7 13.6 %collective-permute-start.4 = (bf16[2,256]{1,0:T(2,128)(2,1)S(1)}, bf16[2,256]{1,0:T(2,128)(2,1)S(1)}, u32[]{:S(2)}, u32[]{:S(2)}) collective-permute-start(bf16[2,256]{1,0:T(2,128)(2,1)S(1)} %pad_maximum_fusion.9), channel_id=1, source_target_pairs={{12,0},{16,4},{4,8},{24,12},{28,16},{0,20},{20,24},{8,28},{13,1},{... | collective-permute-start | bytes 3080 | tf_op jit(solution)/shard_map/ppermute | solution.py:95
  16.6 14.7 %collective-permute-start.3 = (bf16[2,256]{1,0:T(2,128)(2,1)S(1)}, bf16[2,256]{1,0:T(2,128)(2,1)S(1)}, u32[]{:S(2)}, u32[]{:S(2)}) collective-permute-start(bf16[2,256]{1,0:T(2,128)(2,1)S(1)} %pad_maximum_fusion.9), channel_id=1, source_target_pairs={{4,0},{0,4},{12,8},{8,12},{20,16},{16,20},{28,24},{24,28},{5,1},{1... | collective-permute-start | bytes 3080 | tf_op jit(solution)/shard_map/ppermute | solution.py:95
  31.3 15.3 %collective-permute-start.10 = (bf16[256,1024]{1,0:T(8,128)(2,1)}, bf16[256,1024]{1,0:T(8,128)(2,1)}, u32[]{:S(2)}, u32[]{:S(2)}) collective-permute-start(bf16[256,1024]{1,0:T(8,128)(2,1)} %shard_map.237.refs_0_), channel_id=1, source_target_pairs={{0,4},{4,0},{8,12},{12,8},{16,20},{20,16},{24,28},{28,24},{1,5},{5... | collective-permute-start | bytes 1572872 | tf_op jit(solution)/shard_map/ppermute | solution.py:74
  52.9 13.6 %collective-permute-start.15 = (bf16[512,512]{1,0:T(8,128)(2,1)S(1)}, bf16[512,512]{1,0:T(8,128)(2,1)S(1)}, u32[]{:S(2)}, u32[]{:S(2)}) collective-permute-start(bf16[512,512]{1,0:T(8,128)(2,1)S(1)} %pad_maximum_fusion.3), channel_id=1, source_target_pairs={{0,16},{4,20},{8,24},{12,28},{16,0},{20,4},{24,8},{28,12},{1,17},{... | collective-permute-start | bytes 1572872 | tf_op jit(solution)/shard_map/ppermute | solution.py:74
  53.5 13.6 %collective-permute-start.18 = (bf16[512,512]{1,0:T(8,128)(2,1)S(1)}, bf16[512,512]{1,0:T(8,128)(2,1)S(1)}, u32[]{:S(2)}, u32[]{:S(2)}) collective-permute-start(bf16[512,512]{1,0:T(8,128)(2,1)S(1)} %get-tuple-element.72.refs_2_.refs_0_), channel_id=1, source_target_pairs={{0,8},{4,12},{8,0},{12,4},{1,9},{5,13},{9,1},{13,5},{2,10},{6,14},... | collective-permute-start | bytes 1572872 | tf_op jit(solution)/shard_map/ppermute | solution.py:140
  81.2 86.0 %all-gather.2.cloned.1.call-start = ((), (), s32[]{:S(2)}) async-start(), calls=%async_computation.4 | async-start | bytes 14155776 | tf_op jit(solution)/shard_map/all_gather | solution.py:40
  84.4 191.2 %all-reduce.7.cloned.1.call-start = ((), (), s32[]{:S(2)}) async-start(), calls=%async_computation.5 | async-start | bytes 4194304 | tf_op jit(solution)/shard_map/psum | solution.py:48
  84.6 15.6 %collective-permute-start.20 = (bf16[256,1536]{1,0:T(8,128)(2,1)S(1)}, bf16[256,1536]{1,0:T(8,128)(2,1)S(1)}, u32[]{:S(2)}, u32[]{:S(2)}) collective-permute-start(bf16[256,1536]{1,0:T(8,128)(2,1)S(1)} %copy-done.37), channel_id=1, source_target_pairs={{0,16},{4,12},{8,24},{12,4},{16,0},{20,28},{24,8},{28,20},{1,17},{... | collective-permute-start | bytes 2359304 | tf_op jit(solution)/shard_map/ppermute | solution.py:74
  100.4 33.3 %collective-permute-start.21 = (bf16[512,1536]{1,0:T(8,128)(2,1)S(1)}, bf16[512,1536]{1,0:T(8,128)(2,1)S(1)}, u32[]{:S(2)}, u32[]{:S(2)}) collective-permute-start(bf16[512,1536]{1,0:T(8,128)(2,1)S(1)} %pad_maximum_fusion.2), channel_id=1, source_target_pairs={{0,8},{4,20},{8,0},{12,28},{16,24},{20,4},{24,16},{28,12},{1,9},{5... | collective-permute-start | bytes 4718600 | tf_op jit(solution)/shard_map/ppermute | solution.py:74
  135.6 14.2 %collective-permute-start.22 = (bf16[1024,1536]{1,0:T(8,128)(2,1)}, bf16[1024,1536]{1,0:T(8,128)(2,1)S(1)}, u32[]{:S(2)}, u32[]{:S(2)}) collective-permute-start(bf16[1024,1536]{1,0:T(8,128)(2,1)} %pad_maximum_fusion), channel_id=1, source_target_pairs={{0,4},{4,0},{8,12},{12,8},{16,20},{20,16},{24,28},{28,24},{1,5},{5... | collective-permute-start | bytes 9437192 | tf_op jit(solution)/shard_map/ppermute | solution.py:74
  190.0 112.5 %reduce-scatter.4.cloned.1.call-start = ((), (), s32[]{:S(2)}) async-start(), calls=%async_computation.6 | async-start | bytes 7077888 | tf_op jit(solution)/shard_map/reduce_scatter | solution.py:44
  198.3 165.2 %all-reduce.9.cloned.1.call-start = ((), (), s32[]{:S(2)}) async-start(), calls=%async_computation.8 | async-start | bytes 4194304 | tf_op jit(solution)/shard_map/psum | solution.py:48
  275.6 88.2 %reduce-scatter.6.cloned.1.call-start = ((), (), s32[]{:S(2)}) async-start(), calls=%async_computation.7 | async-start | bytes 7077888 | tf_op jit(solution)/shard_map/reduce_scatter | solution.py:44
  302.6 149.3 %all-reduce.11.cloned.1.call-start = ((), (), s32[]{:S(2)}) async-start(), calls=%async_computation.9 | async-start | bytes 4194304 | tf_op jit(solution)/shard_map/psum | solution.py:48
  307.6 14.0 %collective-permute-start.24 = (bf16[512,512]{1,0:T(8,128)(2,1)S(1)}, bf16[512,512]{1,0:T(8,128)(2,1)S(1)}, u32[]{:S(2)}, u32[]{:S(2)}) collective-permute-start(bf16[512,512]{1,0:T(8,128)(2,1)S(1)} %get-tuple-element.117), channel_id=1, source_target_pairs={{0,8},{4,12},{8,0},{12,4},{1,9},{5,13},{9,1},{13,5},{2,10},{6,14},... | collective-permute-start | bytes 1572872 | tf_op jit(solution)/shard_map/ppermute | solution.py:140
  363.5 94.9 %reduce-scatter.8.cloned.1.call-start = ((), (), s32[]{:S(2)}) async-start(), calls=%async_computation.10 | async-start | bytes 7077888 | tf_op jit(solution)/shard_map/reduce_scatter | solution.py:44
  373.1 19.9 %collective-permute-start.31 = (bf16[512,1024]{1,0:T(8,128)(2,1)}, bf16[512,1024]{1,0:T(8,128)(2,1)}, u32[]{:S(2)}, u32[]{:S(2)}) collective-permute-start(bf16[512,1024]{1,0:T(8,128)(2,1)} %slice.108), channel_id=1, source_target_pairs={{0,8},{4,20},{8,0},{12,28},{16,24},{20,4},{24,16},{28,12},{1,9},{5... | collective-permute-start | bytes 3145736 | tf_op jit(solution)/shard_map/ppermute | solution.py:74
  375.7 15.2 %collective-permute-start.34 = (bf16[512,512]{1,0:T(8,128)(2,1)}, bf16[512,512]{1,0:T(8,128)(2,1)}, u32[]{:S(2)}, u32[]{:S(2)}) collective-permute-start(bf16[512,512]{1,0:T(8,128)(2,1)} %slice.119), channel_id=1, source_target_pairs={{0,16},{4,20},{8,24},{12,28},{16,0},{20,4},{24,8},{28,12},{1,17},{... | collective-permute-start | bytes 1572872 | tf_op jit(solution)/shard_map/ppermute | solution.py:74
  392.2 12.1 %collective-permute-start.35 = (bf16[256,512]{1,0:T(8,128)(2,1)S(1)}, bf16[256,512]{1,0:T(8,128)(2,1)}, u32[]{:S(2)}, u32[]{:S(2)}) collective-permute-start(bf16[256,512]{1,0:T(8,128)(2,1)S(1)} %slice.121), channel_id=1, source_target_pairs={{0,8},{4,12},{8,0},{12,4},{16,24},{20,28},{24,16},{28,20},{1,9},{5... | collective-permute-start | bytes 786440 | tf_op jit(solution)/shard_map/ppermute | solution.py:74
  394.6 24.4 %collective-permute-start.32 = (bf16[256,1024]{1,0:T(8,128)(2,1)S(1)}, bf16[256,1024]{1,0:T(8,128)(2,1)S(1)}, u32[]{:S(2)}, u32[]{:S(2)}) collective-permute-start(bf16[256,1024]{1,0:T(8,128)(2,1)S(1)} %slice.110), channel_id=1, source_target_pairs={{0,16},{4,12},{8,24},{12,4},{16,0},{20,28},{24,8},{28,20},{1,17},{... | collective-permute-start | bytes 1572872 | tf_op jit(solution)/shard_map/ppermute | solution.py:74
  406.2 12.9 %collective-permute-start.26 = (f32[4352]{0:T(1024)S(1)}, f32[4352]{0:T(1024)S(1)}, u32[]{:S(2)}, u32[]{:S(2)}) collective-permute-start(f32[4352]{0:T(1024)S(1)} %fusion.10), channel_id=1, source_target_pairs={{0,2},{1,3},{2,0},{3,1},{4,6},{5,7},{6,4},{7,5},{8,10},{9,11},{10,... | collective-permute-start | bytes 52232 | tf_op jit(solution)/shard_map/ppermute | solution.py:133
  (84 other events, 782.8 us)
Sparse Core Ops, SparseCore 0:
  81.3 85.8 all-reduce.4
  190.1 85.4 all-reduce.6
  278.0 85.4 all-reduce.8
  365.8 85.9 all-reduce.10
Sparse Core Ops, SparseCore 1:
  84.5 81.3 all-gather.1
  198.4 60.5 reduce-scatter.3
  302.6 60.7 reduce-scatter.5
  367.7 71.5 reduce-scatter.7
